TPU v7x, 32 devices: a whole 2x2x4 slice. The times are simulated.
32 devices in a mesh: ctx: 8 (over y, x, core), tp: 4 (over z).
Axes of the slice: x: 2, y: 2, z: 4, core: 2. Of those that a mesh axis runs over, the one named last changes fastest.
Arguments:
- queries: bfloat16 [512, 8192], P('ctx', 'tp'), may hold values from -45 to 45
- key_rows: bfloat16 [512, 1024], P('ctx', 'tp'), may hold values from -6 to 6
- value_rows: bfloat16 [512, 1024], P('ctx', 'tp'), may hold values from -6 to 6
- out_weight: bfloat16 [8192, 5120], P('tp', 'ctx'), may hold values from -0.5 to 0.5
- stream: bfloat16 [512, 5120], P('tp', 'ctx'), may hold values from -18 to 18
- final_gain: bfloat16 [5120], replicated, may hold values from 0.5 to 1.5
- head_weight: bfloat16 [5120, 12288], P(None, ('ctx', 'tp')), may hold values from -1 to 1
- token_ids: int32 [512], replicated, may hold values from 0 to 12287
- policy_logprob: float32 [512], P('ctx'), may hold values from -20 to -10
- doc_lengths: int32 [64], replicated, may hold values from 1 to 8192, 131072 in all
- slab_start: int32 [1], replicated, may hold values from 0 to 130560
Outputs:
- ref_logprob: float32 [512], P('ctx')
- kl_penalty: float32 [512], P('ctx')
All inputs are finite; a program needn't handle non-finite values.
Results may differ from a plain program's by a relative error of at most 0.017.
Values may be sent and summed in bfloat16 or wider, within the bound.
No kernel may reach another device: no remote copies, remote signals or barrier semaphores. Data moves between devices by JAX's collectives and lax.ppermute only.
A program may use at most 128 MiB of HBM per device.

v0:
```python
import jax
import jax.numpy as jnp
from jax import lax
from jax.sharding import PartitionSpec as P

D = 5120
HEADS = 64
KV_HEADS = 8
HD = 128


EPSILON = 1e-06
CEILING = 10.0
NEGATIVE = -1e30


def document_ids(doc_lengths, slab_start, length):
    doc_ends = jnp.cumsum(doc_lengths)
    places = slab_start[0] + jnp.arange(length, dtype=jnp.int32)
    return jnp.sum((doc_ends[None, :] <= places[:, None]).astype(jnp.int32), axis=1)


def attention(query_set, query_places, all_docs, key_rows, value_rows):
    query_count = query_set.shape[0]
    local_kv = key_rows.shape[1] // HD
    group_size = HEADS // KV_HEADS
    grouped = query_set.reshape(query_count, local_kv, group_size, HD)
    query_docs = jnp.take(all_docs, query_places)
    score_scale = HD ** (-0.5)
    starting = (
        jnp.full((local_kv, group_size, query_count), NEGATIVE, jnp.float32),
        jnp.zeros((local_kv, group_size, query_count), jnp.float32),
        jnp.zeros((local_kv, group_size, query_count, HD), jnp.float32),
    )
    key_block = lax.all_gather(key_rows, "ctx", axis=0, tiled=True)
    value_block = lax.all_gather(value_rows, "ctx", axis=0, tiled=True)
    key_count = key_block.shape[0]
    key_places = jnp.arange(key_count, dtype=jnp.int32)
    allowed = (key_places[None, :] <= query_places[:, None]) & (
        all_docs[None, :] == query_docs[:, None]
    )

    def update(current):
        highest, denominator, weighted = current
        key_split = key_block.reshape(key_count, local_kv, HD)
        value_split = value_block.reshape(key_count, local_kv, HD)
        scores = (
            jnp.einsum("nkgd,mkd->kgnm", grouped, key_split, preferred_element_type=jnp.float32)
            * score_scale
        )
        scores = jnp.where(allowed, scores, NEGATIVE)
        new_peak = jnp.maximum(highest, jnp.max(scores, axis=3))
        weights = jnp.where(allowed, jnp.exp(scores - new_peak[..., None]), 0.0)
        denominator = jnp.sum(weights, axis=3)
        contribution = jnp.einsum(
            "kgnm,mkd->kgnd",
            weights.astype(jnp.bfloat16),
            value_split,
            preferred_element_type=jnp.float32,
        )
        return (new_peak, denominator, contribution)

    def keep_state(current):
        return current

    highest, denominator, weighted = lax.cond(jnp.any(allowed), update, keep_state, starting)
    attended = weighted / denominator[..., None]
    return (
        attended.transpose(2, 0, 1, 3)
        .reshape(query_count, local_kv * group_size * HD)
        .astype(jnp.bfloat16)
    )


def local(
    queries,
    key_rows,
    value_rows,
    out_weight,
    stream,
    final_gain,
    head_weight,
    token_ids,
    policy_logprob,
    doc_lengths,
    slab_start,
):
    ctx_count = lax.axis_size("ctx")
    tp_count = lax.axis_size("tp")
    ctx_rank = lax.axis_index("ctx")
    tp_rank = lax.axis_index("tp")
    own_rows = queries.shape[0]
    slab_length = own_rows * ctx_count
    all_docs = document_ids(doc_lengths, slab_start, slab_length)
    own_places = ctx_rank * own_rows + jnp.arange(own_rows, dtype=jnp.int32)
    heads_out = attention(queries, own_places, all_docs, key_rows, value_rows)
    partial_out = jnp.dot(
        lax.all_gather(heads_out, "ctx", axis=0, tiled=True),
        out_weight,
        preferred_element_type=jnp.float32,
    )
    summed = lax.psum_scatter(partial_out, "tp", scatter_dimension=0, tiled=True)
    updated = (stream.astype(jnp.float32) + summed).astype(jnp.bfloat16)
    feature_count = updated.shape[1]
    wide = updated.astype(jnp.float32)
    squares = lax.psum(jnp.sum(wide * wide, axis=1), "ctx")
    inverse = lax.rsqrt(squares / D + EPSILON)
    gain_slice = lax.dynamic_slice_in_dim(
        final_gain, ctx_rank * feature_count, feature_count
    ).astype(jnp.float32)
    normed = (wide * inverse[:, None] * gain_slice).astype(jnp.bfloat16)
    stacked = lax.all_gather(normed, "tp", axis=0, tiled=True)
    logits = jnp.dot(
        lax.all_gather(stacked, "ctx", axis=1, tiled=True),
        head_weight,
        preferred_element_type=jnp.float32,
    )
    vocab_local = head_weight.shape[1]
    vocab_offset = (ctx_rank * tp_count + tp_rank) * vocab_local
    local_ids = token_ids - vocab_offset
    columns = jnp.arange(vocab_local, dtype=jnp.int32)
    target = jnp.sum(jnp.where(columns[None, :] == local_ids[:, None], logits, 0.0), axis=1)
    highest = lax.pmax(jnp.max(logits, axis=1), ("ctx", "tp"))
    exp_sums = jnp.sum(jnp.exp(logits - highest[:, None]), axis=1)
    exp_total, target_logit = lax.psum((exp_sums, target), ("ctx", "tp"))
    normalizer = highest + jnp.log(exp_total)
    own_target = lax.dynamic_slice_in_dim(target_logit, ctx_rank * own_rows, own_rows)
    own_normalizer = lax.dynamic_slice_in_dim(normalizer, ctx_rank * own_rows, own_rows)
    ref_logprob = own_target - own_normalizer
    ratio_log = ref_logprob - policy_logprob
    kl_penalty = jnp.minimum(jnp.exp(ratio_log) - ratio_log - 1.0, CEILING)
    return (ref_logprob, kl_penalty)


def solution(mesh):
    placed = (
        P("ctx", "tp"),
        P("ctx", "tp"),
        P("ctx", "tp"),
        P("tp", "ctx"),
        P("tp", "ctx"),
        P(),
        P(None, ("ctx", "tp")),
        P(),
        P("ctx"),
        P(),
        P(),
    )
    return jax.shard_map(
        local, mesh=mesh, in_specs=placed, out_specs=(P("ctx"), P("ctx")), check_vma=False
    )
```

profile of v0, /device:TPU:0, one launch (start us, length us, event | category | flops | bytes accessed | tf_op | source)
XLA Modules:
  0.0 267.7 jit_solution(5989594314381619514)
XLA Ops:
  7.2 0.0 copy-start
  7.2 0.0 all-gather.3.cloned.1.call-start
  7.3 0.9 copy.26
  8.2 0.1 reduce-window.8
  8.2 0.1 reduce
  9.0 0.1 convert_reduce_fusion
  9.1 0.8 gather_fusion
  9.9 11.0 %all_gather.15 = bf16[512,256]{1,0:T(8,128)(2,1)S(1)} all-gather(bf16[64,256]{1,0:T(8,128)(2,1)} %param.14), channel_id=1, replica_groups=mesh['ctx'=8,'tp'=4] {'ctx'}, dimensions={0}, use_global_device_ids=true | all-gather | bytes 294912 | tf_op jit(solution)/shard_map/all_gather | solution.py:35
  20.9 9.1 %all_gather.16 = bf16[512,256]{1,0:T(8,128)(2,1)S(1)} all-gather(bf16[64,256]{1,0:T(8,128)(2,1)} %param.15), channel_id=1, replica_groups=mesh['ctx'=8,'tp'=4] {'ctx'}, dimensions={0}, use_global_device_ids=true | all-gather | bytes 294912 | tf_op jit(solution)/shard_map/all_gather | solution.py:36
  30.0 0.7 fusion.17
  31.4 6.1 %conditional.1 = (f32[2,8,64]{2,1,0:T(8,128)S(1)}, f32[2,8,64,128]{3,2,1,0:T(8,128)S(1)}) conditional(s32[]{:T(128)} %convert_element_type.35, () %tuple.16, (pred[64,512]{1,0:T(8,128)(4,1)S(1)}, bf16[512,256]{1,0:T(8,128)(2,1)S(1)}, bf16[64,2048]{1,0:T(8,128)(2,1)}, bf16[512,256]{1,0:T(8,128)(2,1)S(1)}) %tuple.17), branch_computations={%region_3.4_spmd, %region_4.7_spmd} | conditional | flops 275250176 | bytes 17686572 | solution.py:66
  31.4 0.1 reshape.79
  31.4 1.0 copy.34
  32.4 1.8 fusion
  34.3 0.1 reshape.81
  34.3 0.0 copy-start.1
  34.3 2.4 fusion.3
  36.7 0.0 copy-done.1
  36.8 0.7 fusion.2
  37.5 0.2 fusion.16
  37.7 0.2 copy.27
  37.9 0.8 copy.47
  38.6 0.0 all-gather.3.cloned.1.call-update
  38.7 0.0 copy-start.2
  38.7 0.0 reduce-scatter.2.cloned.1.call-start
  38.7 28.3 %all-gather.3.cloned.1.call-done = bf16[512,2048]{1,0:T(8,128)(2,1)} async-done(((bf16[64,2048]{1,0:T(8,128)(2,1)}), bf16[512,2048]{1,0:T(8,128)(2,1)}) %all-gather.3.cloned.1.call-update) | async-done | bytes 2097168 | tf_op jit(solution)/shard_map/all_gather | solution.py:98
  67.0 0.0 copy-done
  67.0 4.4 %fusion.23 = f32[512,640]{1,0:T(8,128)} fusion(bf16[512,2048]{1,0:T(8,128)(2,1)} %all-gather.3.cloned.1.call-done, bf16[2048,640]{1,0:T(8,128)(2,1)S(1)} %copy-done), kind=kOutput, calls=%fused_computation.48 | convolution fusion | flops 1342177280 | bytes 6029312 | tf_op jit(solution)/shard_map/dot_general | solution.py:97
  71.5 0.0 copy-start.3
  71.5 0.0 reduce-scatter.2.cloned.1.call-update
  71.5 0.0 all-gather.5.cloned.1.call-start
  71.5 0.8 dynamic-slice_convert_fusion
  72.3 30.6 %reduce-scatter.2.cloned.1.call-done = f32[128,640]{1,0:T(8,128)} async-done(((f32[512,640]{1,0:T(8,128)}), f32[128,640]{1,0:T(8,128)}) %reduce-scatter.2.cloned.1.call-update) | async-done | bytes 327696 | tf_op jit(solution)/shard_map/reduce_scatter | solution.py:102
  102.9 0.0 copy-done.2
  102.9 1.1 fusion.13
  104.0 13.4 %psum.21 = f32[128]{0:T(128)S(1)} all-reduce(f32[128]{0:T(128)S(1)} %fusion.13), channel_id=1, replica_groups=mesh['ctx'=8,'tp'=4] {'ctx'}, use_global_device_ids=true, to_apply=%region_9.10 | all-reduce | flops 128 | bytes 1024 | tf_op jit(solution)/shard_map/psum | solution.py:106
  117.4 1.1 fusion.15
  118.5 17.5 %all_gather.18 = bf16[512,640]{1,0:T(8,128)(2,1)} all-gather(bf16[128,640]{1,0:T(8,128)(2,1)S(1)} %fusion.15), channel_id=1, replica_groups=mesh['ctx'=8,'tp'=4] {'tp'}, dimensions={0}, use_global_device_ids=true | all-gather | bytes 819200 | tf_op jit(solution)/shard_map/all_gather | solution.py:112
  136.0 0.0 all-gather.5.cloned.1.call-update
  136.1 0.0 copy-done.3
  136.1 0.0 copy-start.4
  136.1 37.9 %all-gather.5.cloned.1.call-done = bf16[512,5120]{1,0:T(8,128)(2,1)} async-done(((bf16[512,640]{1,0:T(8,128)(2,1)}), bf16[512,5120]{1,0:T(8,128)(2,1)}) %all-gather.5.cloned.1.call-update) | async-done | bytes 5242896 | tf_op jit(solution)/shard_map/all_gather | solution.py:114
  174.0 5.9 %fusion.22 = (f32[512]{0:T(512)S(1)}, f32[512,384]{0,1:T(8,128)S(1)}) fusion(bf16[512,5120]{1,0:T(8,128)(2,1)} %all-gather.5.cloned.1.call-done, bf16[5120,384]{1,0:T(8,128)(2,1)} %param.19), kind=kOutput, calls=%fused_computation.47 | convolution fusion | flops 2013462016 | bytes 9963520 | tf_op jit(solution)/shard_map/dot_general | solution.py:113
  180.0 39.4 %pmax.7 = f32[512]{0:T(512)S(1)} all-reduce(f32[512]{0:T(512)S(1)} %get-tuple-element.31), channel_id=1, replica_groups=mesh['ctx'=8,'tp'=4] {'ctx','tp'}, use_global_device_ids=true, to_apply=%region_13.14 | all-reduce | flops 512 | bytes 4096 | tf_op jit(solution)/shard_map/pmax | solution.py:123
  219.3 0.2 select_reduce_fusion
  219.5 41.0 %all-reduce = (f32[512]{0:T(512)S(1)}, f32[512]{0:T(512)S(1)}) all-reduce(f32[512]{0:T(512)S(1)} %get-tuple-element.22, f32[512]{0:T(512)S(1)} %get-tuple-element.21), channel_id=1, replica_groups=mesh['ctx'=8,'tp'=4] {'ctx','tp'}, use_global_device_ids=true, to_apply=%region_15.16 | all-reduce | flops 1024 | bytes 8192 | tf_op jit(solution)/shard_map/psum | solution.py:125
  260.5 0.0 copy-done.4
  260.6 0.6 fusion.19
  (8 shorter events, 0.0 us)
Async XLA Ops:
  7.2 59.9 %copy-start = (bf16[2048,640]{1,0:T(8,128)(2,1)S(1)}, bf16[2048,640]{1,0:T(8,128)(2,1)}, u32[]{:S(2)}) copy-start(bf16[2048,640]{1,0:T(8,128)(2,1)} %param.16) | copy-start | bytes 7864324
  7.2 59.8 %all-gather.3.cloned.1.call-start = ((), (), s32[]{:S(2)}) async-start(), calls=%async_computation.1 | async-start | bytes 2359296 | tf_op jit(solution)/shard_map/all_gather | solution.py:98
  34.3 2.4 copy-start.1
  38.7 64.2 %copy-start.2 = (bf16[128,640]{1,0:T(8,128)(2,1)S(1)}, bf16[128,640]{1,0:T(8,128)(2,1)}, u32[]{:S(2)}) copy-start(bf16[128,640]{1,0:T(8,128)(2,1)} %param.17) | copy-start | bytes 491524
  38.7 64.2 %reduce-scatter.2.cloned.1.call-start = ((), (), s32[]{:S(2)}) async-start(), calls=%async_computation.2 | async-start | bytes 1638400 | tf_op jit(solution)/shard_map/reduce_scatter | solution.py:102
  71.5 64.6 %copy-start.3 = (s32[512]{0:T(512)S(1)}, s32[512]{0:T(512)}, u32[]{:S(2)}) copy-start(s32[512]{0:T(512)} %param.20) | copy-start | bytes 6148
  71.5 102.5 %all-gather.5.cloned.1.call-start = ((), (), s32[]{:S(2)}) async-start(), calls=%async_computation.3 | async-start | bytes 5898240 | tf_op jit(solution)/shard_map/all_gather | solution.py:114
  136.1 124.5 %copy-start.4 = (f32[64]{0:T(128)S(1)}, f32[64]{0:T(128)}, u32[]{:S(2)}) copy-start(f32[64]{0:T(128)} %param.21) | copy-start | bytes 772
Sparse Core Ops, SparseCore 0:
  38.8 28.1 all-gather.2
  71.6 31.2 reduce-scatter.1
  136.2 37.8 all-gather.4
where the time goes:
time: 268 us
  blocking collectives  131 us (49%)
  waiting for transfers between devices  96.9 us (36%)
  between operations  15.2 us (6%)
  matrix products  14.6 us (5%)
  other arithmetic  5.74 us (2%)
  local copies, waits for them, and re-layouts  3.82 us (1%)
    psum x1, blocking collectives, local(): exp_total, target_logit = lax.psum((exp_sums, target), ('ctx', 'tp'))  41 us
    pmax x1, blocking collectives, local(): highest = lax.pmax(jnp.max(logits, axis=1), ('ctx', 'tp'))  39.4 us
    all_gather x1, waiting for transfers between devices, local(): lax.all_gather(stacked, 'ctx', axis=1, tiled=True)  37.9 us
    reduce_scatter x1, waiting for transfers between devices, local(): lax.psum_scatter(partial_out, 'tp', scatter_dimension=0, tiled=True)  30.6 us
    all_gather x1, waiting for transfers between devices, local(): lax.all_gather(heads_out, 'ctx', axis=0, tiled=True)  28.3 us
    all_gather x1, blocking collectives, local(): stacked = lax.all_gather(normed, 'tp', axis=0, tiled=True)  17.5 us
    psum x1, blocking collectives, local(): squares = lax.psum(jnp.sum(wide * wide, axis=1), 'ctx')  13.4 us
    all_gather x1, blocking collectives, attention(): key_block = lax.all_gather(key_rows, 'ctx', axis=0, tiled=True)  11 us
  transfers between devices with their start and end apart: 3, of which 3 were waited for; matrix products, arithmetic and copies ran while one was open for 0% of the time, Pallas kernels for 0%

commit v1 on v0

v1 whole, which is shorter than its diff:
```python
import jax
import jax.numpy as jnp
from jax import lax
from jax.experimental import pallas as pl
from jax.experimental.pallas import tpu as pltpu
from jax.sharding import PartitionSpec as P

HD = 128
EPSILON = 1e-06
CEILING = 10.0
NEGATIVE = -1e30
F32 = jnp.float32
BF16 = jnp.bfloat16
VMEM = pl.BlockSpec(memory_space=pltpu.VMEM)
SMEM = pl.BlockSpec(memory_space=pltpu.SMEM)
ANY = pl.BlockSpec(memory_space=pl.ANY)


def swap(x, axis, k):
    size = lax.axis_size(axis)
    return lax.ppermute(x, axis, [(i, i ^ k) for i in range(size)])


def gather_plane(pair, chips):
    first, second = pair
    if chips != 4:
        return [pair] + [(swap(first, "ctx", 2 * j), swap(second, "ctx", 2 * j)) for j in range(1, chips)]
    x0, y0 = swap(first, "ctx", 2), swap(first, "ctx", 4)
    x1, y1 = swap(second, "ctx", 2), swap(second, "ctx", 4)
    return [pair, (x0, x1), (y0, y1), (swap(y0, "ctx", 2), swap(x1, "ctx", 4))]


def attend_kernel(chips, tp_count, own_rows, blocks, place_ref, lens_ref, *refs):
    queries = refs[: 2 * chips]
    pairs = refs[2 * chips : 3 * chips]
    sibling_ref, w_own_ref, w_sib_ref = refs[3 * chips : 3 * chips + 3]
    outs = refs[3 * chips + 3 : 3 * chips + 3 + tp_count]
    keys, values, mixed, w_own, w_sib, product, sems = refs[3 * chips + 3 + tp_count :]
    copies = [
        pltpu.make_async_copy(w_own_ref, w_own, sems.at[0]),
        pltpu.make_async_copy(w_sib_ref, w_sib, sems.at[1]),
    ]
    for copy in copies:
        copy.start()
    ctx, tp, slab_start = place_ref[0], place_ref[1], place_ref[2]
    kv_width = keys.shape[1]
    kv_heads = kv_width // HD
    group = queries[0].shape[1] * 2 // kv_width
    length = keys.shape[0]
    for j in range(chips):
        own_at = pl.ds(pl.multiple_of((ctx ^ (2 * j)) * own_rows, own_rows), own_rows)
        sib_at = pl.ds(pl.multiple_of((ctx ^ (2 * j + 1)) * own_rows, own_rows), own_rows)
        keys[own_at, :] = pairs[j][:, :kv_width]
        values[own_at, :] = pairs[j][:, kv_width:]
        rows = slice(j * own_rows, (j + 1) * own_rows)
        keys[sib_at, :] = sibling_ref[rows, :kv_width]
        values[sib_at, :] = sibling_ref[rows, kv_width:]

    count = lens_ref.shape[0]
    before = lax.broadcasted_iota(jnp.int32, (count, count), 0) <= lax.broadcasted_iota(jnp.int32, (count, count), 1)
    ends = jnp.sum(jnp.where(before, lens_ref[...], 0), axis=0, keepdims=True)
    columns = lax.broadcasted_iota(jnp.int32, (own_rows, length), 1)
    for j in range(chips):
        spot = (ctx ^ (2 * j)) * own_rows + lax.broadcasted_iota(jnp.int32, (own_rows, 1), 0)
        opened = jnp.max(jnp.where(ends <= spot + slab_start, ends, 0), axis=1, keepdims=True) - slab_start
        allowed = ((columns <= spot) & (columns >= opened))[None]
        for h in range(kv_heads):
            heads = []
            for g in range(group):
                half, inner = divmod((h * group + g) * HD, queries[0].shape[1])
                heads.append(queries[2 * j + half][:, inner : inner + HD])
            stack = jnp.concatenate(heads, axis=0)
            scores = lax.dot_general(
                stack, keys[:, h * HD : (h + 1) * HD], (((1,), (1,)), ((), ())), preferred_element_type=F32
            ).reshape(group, own_rows, length)
            scores = jnp.where(allowed, scores, NEGATIVE)
            highest = jnp.max(scores, axis=2, keepdims=True)
            weights = jnp.exp((scores - highest) * HD ** (-0.5))
            denominator = jnp.sum(weights, axis=2, keepdims=True).reshape(group * own_rows, 1)
            mix = jnp.dot(
                weights.reshape(group * own_rows, length).astype(BF16),
                values[:, h * HD : (h + 1) * HD],
                preferred_element_type=F32,
            )
            mix = (mix / denominator).astype(BF16)
            for g in range(group):
                at = (h * group + g) * HD
                mixed[j * own_rows : (j + 1) * own_rows, at : at + HD] = mix[g * own_rows : (g + 1) * own_rows]
    for copy in copies:
        copy.wait()
    width = w_own.shape[1]
    product[:, :width] = jnp.dot(mixed[...], w_own[...], preferred_element_type=F32)
    product[:, width:] = jnp.dot(mixed[...], w_sib[...], preferred_element_type=F32)
    for k in range(tp_count):
        for b in range(blocks // 2):
            wanted = (tp ^ k) * blocks + 2 * b + lax.rem(ctx, 2)
            at = pl.multiple_of(lax.shift_right_logical(wanted ^ ctx, 1) * own_rows, own_rows)
            outs[k][b * own_rows : (b + 1) * own_rows, :] = product[pl.ds(at, own_rows), :].astype(outs[k].dtype)


def attend(place, lens, queries, pairs, sibling, w_own, w_sib, tp_count, blocks):
    chips, own_rows = len(pairs), pairs[0].shape[0]
    kv_width = pairs[0].shape[1] // 2
    length, plane_rows = 2 * chips * own_rows, chips * own_rows
    depth, width = w_own.shape
    out_rows = blocks // 2 * own_rows
    need = 4 * depth * width + 4 * plane_rows * (2 * depth + 2 * 2 * width) + 24 * 8 * own_rows * length
    return pl.pallas_call(
        lambda *refs: attend_kernel(chips, tp_count, own_rows, blocks, *refs),
        out_shape=[jax.ShapeDtypeStruct((out_rows, 2 * width), F32 if k == 0 else BF16) for k in range(tp_count)],
        in_specs=[SMEM] + [VMEM] * (2 + 3 * chips) + [ANY, ANY],
        out_specs=[VMEM] * tp_count,
        scratch_shapes=[
            pltpu.VMEM((length, kv_width), BF16),
            pltpu.VMEM((length, kv_width), BF16),
            pltpu.VMEM((plane_rows, depth), BF16),
            pltpu.VMEM((depth, width), BF16),
            pltpu.VMEM((depth, width), BF16),
            pltpu.VMEM((plane_rows, 2 * width), F32),
            pltpu.SemaphoreType.DMA((2,)),
        ],
        compiler_params=pltpu.CompilerParams(vmem_limit_bytes=need + (12 << 20)),
        name="attend",
    )(place, lens, *[q for two in queries for q in two], *pairs, sibling, w_own, w_sib)


def score_kernel(chips, tp_count, own_rows, blocks, place_ref, tokens_ref, gain_ref, *refs):
    halves = refs[: 2 * chips]
    h_own_ref, h_sib_ref, out_ref, head, normed, sems = refs[2 * chips :]
    ctx, tp = place_ref[0], place_ref[1]
    ranks = 2 * chips
    part, vocab = h_own_ref.shape[0] // ranks, h_own_ref.shape[1]
    copies = []
    for k in range(ranks):
        source = pl.ds(pl.multiple_of((ctx ^ k) * part, part), part)
        target = slice(k * part, (k + 1) * part)
        copies.append(pltpu.make_async_copy(h_own_ref.at[source], head.at[target, :vocab], sems.at[0, k]))
        copies.append(pltpu.make_async_copy(h_sib_ref.at[source], head.at[target, vocab:], sems.at[1, k]))
    for copy in copies:
        copy.start()
    half_rows = halves[0].shape[0]
    squares = [jnp.zeros((half_rows, 1), F32), jnp.zeros((half_rows, 1), F32)]
    for j in range(chips):
        gain = jnp.concatenate([gain_ref[pl.ds(ctx ^ (2 * j), 1), :], gain_ref[pl.ds(ctx ^ (2 * j + 1), 1), :]], axis=1)
        for s in range(2):
            wide = halves[2 * j + s][...].astype(F32)
            squares[s] += jnp.sum(wide * wide, axis=1, keepdims=True)
            normed[s * half_rows : (s + 1) * half_rows, 2 * j * part : 2 * (j + 1) * part] = (wide * gain).astype(BF16)
    square = jnp.concatenate(squares, axis=0)
    inverse = lax.rsqrt(square * (1.0 / (ranks * part)) + EPSILON)
    for copy in copies:
        copy.wait()
    logits = jnp.dot(normed[...], head[...], preferred_element_type=F32) * inverse
    rows = logits.shape[0]
    column = lax.broadcasted_iota(jnp.int32, (1, 2 * vocab), 1)
    offset = jnp.where(column < vocab, (ctx * tp_count + tp) * vocab, ((ctx ^ 1) * tp_count + tp) * vocab - vocab)
    owners = [
        (tp ^ k) * blocks + 2 * b + lax.rem(ctx, 2) for k in range(tp_count) for b in range(blocks // 2)
    ]
    tokens = jnp.concatenate(
        [tokens_ref[pl.ds(pl.multiple_of(owner * own_rows, own_rows), own_rows), :] for owner in owners], axis=0
    )
    highest = jnp.max(logits, axis=1, keepdims=True)
    total = jnp.sum(jnp.exp(logits - highest), axis=1, keepdims=True)
    target = jnp.sum(jnp.where(column + offset == tokens, logits, 0.0), axis=1, keepdims=True)
    lane = lax.broadcasted_iota(jnp.int32, (rows, 128), 1)
    packed = jnp.where(lane == 0, highest, jnp.where(lane == 1, total, jnp.where(lane == 2, target, 0.0)))
    turned = packed.T[:8]
    out_ref[...] = jnp.zeros(out_ref.shape, F32)
    for i, owner in enumerate(owners):
        tile = turned[:, i * own_rows : (i + 1) * own_rows]
        for k in range(tp_count):
            out_ref[pl.ds(owner * tp_count + k, 1), :, :own_rows] = tile[None]


def score(place, tokens, gain, halves, h_own, h_sib, tp_count, own_rows, blocks):
    chips = len(halves)
    half_rows, both = halves[0][0].shape
    depth, vocab = h_own.shape
    need = 4 * depth * vocab + 2 * half_rows * depth * 6 + 2 * half_rows * vocab * 2 * 4 * 8
    return pl.pallas_call(
        lambda *refs: score_kernel(chips, tp_count, own_rows, blocks, *refs),
        out_shape=jax.ShapeDtypeStruct((2 * chips * tp_count, 8, 128), F32),
        in_specs=[SMEM] + [VMEM] * (2 + 2 * chips) + [ANY, ANY],
        out_specs=VMEM,
        scratch_shapes=[
            pltpu.VMEM((depth, 2 * vocab), BF16),
            pltpu.VMEM((2 * half_rows, depth), BF16),
            pltpu.SemaphoreType.DMA((2, 2 * chips)),
        ],
        compiler_params=pltpu.CompilerParams(vmem_limit_bytes=need + (12 << 20)),
        name="score",
    )(place, tokens, gain, *[h for two in halves for h in two], h_own, h_sib)


def merge_kernel(chips, tp_count, place_ref, policy_ref, stats_ref, logprob_ref, penalty_ref):
    parity = lax.rem(place_ref[0], 2)
    own_rows = policy_ref.shape[1]
    tiles = [
        stats_ref[(2 * j + parity) * tp_count + k] for j in range(chips) for k in range(tp_count)
    ]
    highest = tiles[0][0:1]
    for tile in tiles[1:]:
        highest = jnp.maximum(highest, tile[0:1])
    total = jnp.zeros_like(highest)
    target = jnp.zeros_like(highest)
    for tile in tiles:
        total += tile[1:2] * jnp.exp(tile[0:1] - highest)
        target += tile[2:3]
    logprob = (target - (highest + jnp.log(total)))[:, :own_rows]
    ratio = logprob - policy_ref[...]
    logprob_ref[...] = logprob
    penalty_ref[...] = jnp.minimum(jnp.exp(ratio) - ratio - 1.0, CEILING)


def merge(place, policy, stats, chips, tp_count):
    shape = jax.ShapeDtypeStruct(policy.shape, F32)
    return pl.pallas_call(
        lambda *refs: merge_kernel(chips, tp_count, *refs),
        out_shape=[shape, shape],
        in_specs=[SMEM, VMEM, VMEM],
        out_specs=[VMEM, VMEM],
        name="merge",
    )(place, policy, stats)


def local(
    queries,
    key_rows,
    value_rows,
    out_weight,
    stream,
    final_gain,
    head_weight,
    token_ids,
    policy_logprob,
    doc_lengths,
    slab_start,
):
    ctx_count, tp_count = lax.axis_size("ctx"), lax.axis_size("tp")
    ctx, tp = lax.axis_index("ctx"), lax.axis_index("tp")
    core = lax.rem(ctx, 2)
    chips = ctx_count // 2
    own_rows = queries.shape[0]
    blocks = ctx_count // tp_count
    place = jnp.stack([ctx, tp, slab_start[0]]).astype(jnp.int32)

    pair = jnp.concatenate([key_rows, value_rows], axis=1)
    pairs = [pair] + [swap(pair, "ctx", 2 * j) for j in range(1, chips)]
    half = queries.shape[1] // 2
    query_sets = gather_plane((queries[:, :half], queries[:, half:]), chips)
    sibling = swap(jnp.concatenate(pairs, axis=0), "ctx", 1)
    out_sibling = swap(out_weight, "ctx", 1)
    head_sibling = swap(head_weight, "ctx", 1)
    cut = stream.reshape(blocks // 2, 2, own_rows, stream.shape[1])
    kept = lax.dynamic_index_in_dim(cut, core, 1, keepdims=False)
    given = lax.dynamic_index_in_dim(cut, 1 - core, 1, keepdims=False)
    stream_rows = jnp.concatenate([kept, swap(given, "ctx", 1)], axis=2).reshape(blocks // 2 * own_rows, -1)

    sums = attend(
        place, doc_lengths[:, None], query_sets, pairs, sibling, out_weight, out_sibling, tp_count, blocks
    )
    total = stream_rows.astype(F32) + sums[0]
    for k in range(1, tp_count):
        total = total + swap(sums[k], "tp", k).astype(F32)
    updated = total.astype(BF16)
    near = [updated] + [swap(updated, "tp", k) for k in range(1, tp_count)]
    mid = tp_count // 2
    halves = gather_plane((jnp.concatenate(near[:mid], axis=0), jnp.concatenate(near[mid:], axis=0)), chips)
    gain = final_gain.astype(F32).reshape(ctx_count, -1)
    stats = score(
        place, token_ids[:, None], gain, halves, head_weight, head_sibling, tp_count, own_rows, blocks
    )
    stats = lax.all_to_all(stats, ("ctx", "tp"), 0, 0, tiled=True)
    logprob, penalty = merge(place, policy_logprob[None], stats, chips, tp_count)
    return (logprob[0], penalty[0])


def solution(mesh):
    placed = (
        P("ctx", "tp"),
        P("ctx", "tp"),
        P("ctx", "tp"),
        P("tp", "ctx"),
        P("tp", "ctx"),
        P(),
        P(None, ("ctx", "tp")),
        P(),
        P("ctx"),
        P(),
        P(),
    )
    return jax.shard_map(
        local, mesh=mesh, in_specs=placed, out_specs=(P("ctx"), P("ctx")), check_vma=False
    )
```

time: 268 us -> 116 us (0.43)
  blocking collectives: 131 us -> 10.8 us
  waiting for transfers between devices: 96.9 us -> 50 us
  starting transfers between devices: 0.12 us -> 27.7 us
  matrix products: 14.6 us -> 0 us
  Pallas kernels: 0 us -> 14.4 us
  between operations: 15.2 us -> 1.41 us
  local copies, waits for them, and re-layouts: 3.82 us -> 10.5 us
  other arithmetic: 5.74 us -> 0.93 us
    all_gather x2 -> x0, waiting for transfers between devices: 66.2 us -> none  [the longest x1 37.9 us: local(): lax.all_gather(stacked, 'ctx', axis=1, tiled=True)]
    psum x2 -> x0, blocking collectives: 54.4 us -> none  [the longest x1 41 us: local(): exp_total, target_logit = lax.psum((exp_sums, target), ('ctx', 'tp'))]
    ppermute x0 -> x25, waiting for transfers between devices: none -> 50 us  [swap(): return lax.ppermute(x, axis, [(i, i ^ k) for i in range(size)])]
    pmax x1 -> x0, blocking collectives: 39.4 us -> none  [local(): highest = lax.pmax(jnp.max(logits, axis=1), ('ctx', 'tp'))]
    all_gather x3 -> x0, blocking collectives: 37.6 us -> none  [the longest x1 17.5 us: local(): stacked = lax.all_gather(normed, 'tp', axis=0, tiled=True)]
    reduce_scatter x1 -> x0, waiting for transfers between devices: 30.6 us -> none  [local(): lax.psum_scatter(partial_out, 'tp', scatter_dimension=0, tiled=True)]
    ppermute x0 -> x25, starting transfers between devices: none -> 27.7 us  [swap(): return lax.ppermute(x, axis, [(i, i ^ k) for i in range(size)])]
    dot_general x4 -> x0, matrix products: 14.6 us -> none  [the longest x1 5.93 us: local(): jnp.dot(lax.all_gather(stacked, 'ctx', axis=1, tiled=True), head_weight,...]
  transfers between devices with their start and end apart: 3 -> 25, of which waited for: 3 -> 14; matrix products, arithmetic and copies ran while one was open for 0% -> 4% of each run, Pallas kernels for 0% -> 6%
where the time goes in v1:
time: 116 us
  waiting for transfers between devices  50 us (43%)
  starting transfers between devices  27.7 us (24%)
  Pallas kernels  14.4 us (12%)
  blocking collectives  10.8 us (9%)
  local copies, waits for them, and re-layouts  10.5 us (9%)
  between operations  1.41 us (1%)
    ppermute x25, waiting for transfers between devices, swap(): return lax.ppermute(x, axis, [(i, i ^ k) for i in range(size)])  50 us
    ppermute x25, starting transfers between devices, swap(): return lax.ppermute(x, axis, [(i, i ^ k) for i in range(size)])  27.7 us
    all_to_all x1, blocking collectives, local(): stats = lax.all_to_all(stats, ('ctx', 'tp'), 0, 0, tiled=True)  10.8 us
    unnamed x22, local copies, waits for them, and re-layouts  7.77 us
    pallas_call x1, Pallas kernels, attend(): pl.pallas_call(lambda *refs: attend_kernel(chips, tp_count, own_rows, blo...  7.33 us
    pallas_call x1, Pallas kernels, score(): pl.pallas_call(lambda *refs: score_kernel(chips, tp_count, own_rows, bloc...  5.55 us
  transfers between devices with their start and end apart: 25, of which 14 were waited for; matrix products, arithmetic and copies ran while one was open for 4% of the time, Pallas kernels for 6%

profile of v1, /device:TPU:0, one launch (start us, length us, event | category | flops | bytes accessed | tf_op | source)
XLA Modules:
  0.0 115.7 jit_solution(14915930100779033549)
XLA Ops:
  0.6 0.5 collective-permute-start.11
  1.1 0.1 collective-permute-start.24
  1.2 0.8 constant_dynamic-update-slice_fusion.1
  2.0 0.8 constant_dynamic-update-slice_fusion.refs_10_
  2.7 3.9 %collective-permute-start.9 = (bf16[64,512]{1,0:T(8,128)(2,1)S(1)}, bf16[64,512]{1,0:T(8,128)(2,1)S(1)}, u32[]{:S(2)}, u32[]{:S(2)}) collective-permute-start(bf16[64,512]{1,0:T(8,128)(2,1)S(1)} %constant_dynamic-update-slice_fusion.refs_10_), channel_id=1, source_target_pairs={{0,24},{4,28},{8,16},{12,20},{16,8},{20,12},{24,0},{28,4},{1,25},{... | collective-permute-start | bytes 196616 | tf_op jit(solution)/shard_map/ppermute | solution.py:21
  6.6 1.0 fusion.4
  7.6 0.6 collective-permute-start.4
  8.2 1.5 %collective-permute-start.8 = (bf16[64,512]{1,0:T(8,128)(2,1)S(1)}, bf16[64,512]{1,0:T(8,128)(2,1)S(1)}, u32[]{:S(2)}, u32[]{:S(2)}) collective-permute-start(bf16[64,512]{1,0:T(8,128)(2,1)S(1)} %constant_dynamic-update-slice_fusion.refs_10_), channel_id=1, source_target_pairs={{0,16},{4,20},{8,24},{12,28},{16,0},{20,4},{24,8},{28,12},{1,17},{... | collective-permute-start | bytes 196616 | tf_op jit(solution)/shard_map/ppermute | solution.py:21
  9.7 0.0 collective-permute-done.9.refs_13_
  9.7 1.1 collective-permute-start.7
  10.9 3.4 %collective-permute-done.8.refs_12_ = bf16[64,512]{1,0:T(8,128)(2,1)S(1)} collective-permute-done((bf16[64,512]{1,0:T(8,128)(2,1)S(1)}, bf16[64,512]{1,0:T(8,128)(2,1)S(1)}, u32[]{:S(2)}, u32[]{:S(2)}) %collective-permute-start.8) | collective-permute-done | bytes 65568 | tf_op jit(solution)/shard_map/ppermute | solution.py:21
  14.3 0.8 collective-permute-start.2
  15.0 0.0 collective-permute-done.7.refs_11_
  15.0 1.3 %collective-permute-start.3 = (bf16[64,1024]{1,0:T(8,128)(2,1)S(1)}, bf16[64,1024]{1,0:T(8,128)(2,1)}, u32[]{:S(2)}, u32[]{:S(2)}) collective-permute-start(bf16[64,1024]{1,0:T(8,128)(2,1)S(1)} %get-tuple-element.15.refs_2_), channel_id=1, source_target_pairs={{0,16},{4,20},{8,24},{12,28},{16,0},{20,4},{24,8},{28,12},{1,17},{... | collective-permute-start | bytes 393224 | tf_op jit(solution)/shard_map/ppermute | solution.py:21
  16.4 0.0 collective-permute-done.4.refs_7_
  16.4 0.7 copy-done.2
  17.0 0.7 collective-permute-start.1
  17.8 0.7 pad_maximum_fusion.1
  18.5 1.1 collective-permute-done.2.refs_5_
  19.6 0.5 collective-permute-done.3.refs_6_
  20.1 1.4 %collective-permute-start.6 = (bf16[64,1024]{1,0:T(8,128)(2,1)}, bf16[64,1024]{1,0:T(8,128)(2,1)}, u32[]{:S(2)}, u32[]{:S(2)}) collective-permute-start(bf16[64,1024]{1,0:T(8,128)(2,1)} %collective-permute-done.2.refs_5_), channel_id=1, source_target_pairs={{0,16},{4,20},{8,24},{12,28},{16,0},{20,4},{24,8},{28,12},{1,17},{... | collective-permute-start | bytes 393224 | tf_op jit(solution)/shard_map/ppermute | solution.py:21
  21.5 0.5 collective-permute-done.1.refs_4_
  22.1 0.7 copy-done.4
  22.7 0.8 collective-permute-start.5
  24.2 0.7 copy.14.refs_1_
  24.9 0.1 pad_add_fusion.refs_0_
  25.0 0.8 collective-permute-done.6.refs_9_
  25.8 2.2 %collective-permute-done.5.refs_8_ = bf16[64,1024]{1,0:T(8,128)(2,1)} collective-permute-done((bf16[64,1024]{1,0:T(8,128)(2,1)}, bf16[64,1024]{1,0:T(8,128)(2,1)}, u32[]{:S(2)}, u32[]{:S(2)}) %collective-permute-start.5) | collective-permute-done | bytes 131104 | tf_op jit(solution)/shard_map/ppermute | solution.py:21
  28.0 0.0 collective-permute-done.10.refs_14_
  28.0 0.0 collective-permute-done.11.refs_16_
  28.0 1.7 %copy-done.1 = bf16[2048,640]{1,0:T(8,128)(2,1)S(1)} copy-done((bf16[2048,640]{1,0:T(8,128)(2,1)S(1)}, bf16[2048,640]{1,0:T(8,128)(2,1)}, u32[]{:S(2)}) %copy-start.1) | copy-done | bytes 2621464
  29.8 0.9 copy-done.3
  30.7 0.9 copy-done.5
  31.6 7.3 %attend.1 = (f32[64,1280]{1,0:T(8,128)S(1)}, bf16[64,1280]{1,0:T(8,128)(2,1)S(1)}, bf16[64,1280]{1,0:T(8,128)(2,1)S(1)}, bf16[64,1280]{1,0:T(8,128)(2,1)S(1)}) custom-call(s32[3]{0:T(128)S(1)} %pad_add_fusion.refs_0_, s32[64,1]{1,0:T(8,128)S(1)} %copy.14.refs_1_, bf16[64,1024]{1,0:T(8,128)(2,1)S(1)} %get-tuple-element.15.refs_2_, ...), custom_call_target="tpu_custom_call" | custom-call | tf_op jit(solution)/shard_map/attend/pallas_call | solution.py:108
  38.9 1.6 %collective-permute-start.12 = (bf16[64,1280]{1,0:T(8,128)(2,1)S(1)}, bf16[64,1280]{1,0:T(8,128)(2,1)S(1)}, u32[]{:S(2)}, u32[]{:S(2)}) collective-permute-start(bf16[64,1280]{1,0:T(8,128)(2,1)S(1)} %get-tuple-element.9), channel_id=1, source_target_pairs={{0,1},{1,0},{2,3},{3,2},{4,5},{5,4},{6,7},{7,6},{8,9},{9,8},{10,11... | collective-permute-start | bytes 491528 | tf_op jit(solution)/shard_map/ppermute | solution.py:21
  40.6 2.6 %collective-permute-start.13 = (bf16[64,1280]{1,0:T(8,128)(2,1)S(1)}, bf16[64,1280]{1,0:T(8,128)(2,1)S(1)}, u32[]{:S(2)}, u32[]{:S(2)}) collective-permute-start(bf16[64,1280]{1,0:T(8,128)(2,1)S(1)} %get-tuple-element.10), channel_id=1, source_target_pairs={{0,2},{1,3},{2,0},{3,1},{4,6},{5,7},{6,4},{7,5},{8,10},{9,11},{10,... | collective-permute-start | bytes 491528 | tf_op jit(solution)/shard_map/ppermute | solution.py:21
  43.1 0.2 collective-permute-start.14
  43.4 0.1 collective-permute-start
  43.5 1.3 %collective-permute-done = bf16[1,64,640]{2,1,0:T(8,128)(2,1)S(1)} collective-permute-done((bf16[1,64,640]{2,1,0:T(8,128)(2,1)S(1)}, bf16[1,64,640]{2,1,0:T(8,128)(2,1)S(1)}, u32[]{:S(2)}, u32[]{:S(2)}) %collective-permute-start) | collective-permute-done | bytes 81952 | tf_op jit(solution)/shard_map/ppermute | solution.py:21
  44.7 1.1 collective-permute-done.12
  45.9 8.6 %collective-permute-done.13 = bf16[64,1280]{1,0:T(8,128)(2,1)S(1)} collective-permute-done((bf16[64,1280]{1,0:T(8,128)(2,1)S(1)}, bf16[64,1280]{1,0:T(8,128)(2,1)S(1)}, u32[]{:S(2)}, u32[]{:S(2)}) %collective-permute-start.13) | collective-permute-done | bytes 163872 | tf_op jit(solution)/shard_map/ppermute | solution.py:21
  54.5 0.0 collective-permute-done.14
  54.5 0.1 fusion.3
  54.6 2.4 %collective-permute-start.15 = (bf16[64,1280]{1,0:T(8,128)(2,1)S(1)}, bf16[64,1280]{1,0:T(8,128)(2,1)S(1)}, u32[]{:S(2)}, u32[]{:S(2)}) collective-permute-start(bf16[64,1280]{1,0:T(8,128)(2,1)S(1)} %fusion.3), channel_id=1, source_target_pairs={{0,1},{1,0},{2,3},{3,2},{4,5},{5,4},{6,7},{7,6},{8,9},{9,8},{10,11... | collective-permute-start | bytes 491528 | tf_op jit(solution)/shard_map/ppermute | solution.py:21
  56.9 2.5 %collective-permute-start.17 = (bf16[64,1280]{1,0:T(8,128)(2,1)S(1)}, bf16[64,1280]{1,0:T(8,128)(2,1)S(1)}, u32[]{:S(2)}, u32[]{:S(2)}) collective-permute-start(bf16[64,1280]{1,0:T(8,128)(2,1)S(1)} %fusion.3), channel_id=1, source_target_pairs={{0,3},{1,2},{2,1},{3,0},{4,7},{5,6},{6,5},{7,4},{8,11},{9,10},{10,... | collective-permute-start | bytes 491528 | tf_op jit(solution)/shard_map/ppermute | solution.py:21
  59.5 0.0 collective-permute-start.16
  59.5 2.8 %collective-permute-done.15 = bf16[64,1280]{1,0:T(8,128)(2,1)S(1)} collective-permute-done((bf16[64,1280]{1,0:T(8,128)(2,1)S(1)}, bf16[64,1280]{1,0:T(8,128)(2,1)S(1)}, u32[]{:S(2)}, u32[]{:S(2)}) %collective-permute-start.15) | collective-permute-done | bytes 163872 | tf_op jit(solution)/shard_map/ppermute | solution.py:21
  62.3 0.7 collective-permute-start.20
  63.0 9.1 %collective-permute-done.16 = bf16[64,1280]{1,0:T(8,128)(2,1)S(1)} collective-permute-done((bf16[64,1280]{1,0:T(8,128)(2,1)S(1)}, bf16[64,1280]{1,0:T(8,128)(2,1)S(1)}, u32[]{:S(2)}, u32[]{:S(2)}) %collective-permute-start.16) | collective-permute-done | bytes 163872 | tf_op jit(solution)/shard_map/ppermute | solution.py:21
  72.1 2.8 %collective-permute-start.19 = (bf16[128,1280]{1,0:T(8,128)(2,1)S(1)}, bf16[128,1280]{1,0:T(8,128)(2,1)S(1)}, u32[]{:S(2)}, u32[]{:S(2)}) collective-permute-start(bf16[128,1280]{1,0:T(8,128)(2,1)S(1)} %constant_dynamic-update-slice_fusion.2.refs_4_), channel_id=1, source_target_pairs={{0,8},{4,12},{8,0},{12,4},{16,24},{20,28},{24,16},{28,20},{1,9},{5... | collective-permute-start | bytes 983048 | tf_op jit(solution)/shard_map/ppermute | solution.py:21
  74.9 0.1 collective-permute-start.18
  75.0 0.0 collective-permute-start.21
  75.0 1.9 %collective-permute-start.22 = (bf16[128,1280]{1,0:T(8,128)(2,1)S(1)}, bf16[128,1280]{1,0:T(8,128)(2,1)S(1)}, u32[]{:S(2)}, u32[]{:S(2)}) collective-permute-start(bf16[128,1280]{1,0:T(8,128)(2,1)S(1)} %collective-permute-done.20.refs_7_), channel_id=1, source_target_pairs={{0,8},{4,12},{8,0},{12,4},{16,24},{20,28},{24,16},{28,20},{1,9},{5... | collective-permute-start | bytes 983048 | tf_op jit(solution)/shard_map/ppermute | solution.py:21
  77.0 6.6 %collective-permute-done.19.refs_6_ = bf16[128,1280]{1,0:T(8,128)(2,1)S(1)} collective-permute-done((bf16[128,1280]{1,0:T(8,128)(2,1)S(1)}, bf16[128,1280]{1,0:T(8,128)(2,1)S(1)}, u32[]{:S(2)}, u32[]{:S(2)}) %collective-permute-start.19) | collective-permute-done | bytes 327712 | tf_op jit(solution)/shard_map/ppermute | solution.py:21
  83.6 0.0 collective-permute-start.23
  83.6 0.1 copy.15.refs_1_
  83.8 6.8 %collective-permute-done.18.refs_5_ = bf16[128,1280]{1,0:T(8,128)(2,1)S(1)} collective-permute-done((bf16[128,1280]{1,0:T(8,128)(2,1)S(1)}, bf16[128,1280]{1,0:T(8,128)(2,1)S(1)}, u32[]{:S(2)}, u32[]{:S(2)}) %collective-permute-start.18) | collective-permute-done | bytes 327712 | tf_op jit(solution)/shard_map/ppermute | solution.py:21
  90.6 0.0 collective-permute-done.21.refs_8_
  90.6 5.1 %collective-permute-done.22.refs_9_ = bf16[128,1280]{1,0:T(8,128)(2,1)S(1)} collective-permute-done((bf16[128,1280]{1,0:T(8,128)(2,1)S(1)}, bf16[128,1280]{1,0:T(8,128)(2,1)S(1)}, u32[]{:S(2)}, u32[]{:S(2)}) %collective-permute-start.22) | collective-permute-done | bytes 327712 | tf_op jit(solution)/shard_map/ppermute | solution.py:21
  95.7 0.0 copy-start
  95.7 2.1 %copy-done = bf16[5120,384]{1,0:T(8,128)(2,1)S(1)} copy-done((bf16[5120,384]{1,0:T(8,128)(2,1)S(1)}, bf16[5120,384]{1,0:T(8,128)(2,1)}, u32[]{:S(2)}) %copy-start) | copy-done | bytes 3932184
  97.8 5.6 %score.1 = f32[32,8,128]{2,1,0:T(8,128)S(1)} custom-call(s32[3]{0:T(128)S(1)} %pad_add_fusion.refs_0_, s32[512,1]{1,0:T(8,128)S(1)} %copy.15.refs_1_, f32[8,640]{1,0:T(8,128)S(1)} %reshape.19.refs_2_, bf16[128,1280]{1,0:T(8,128)(2,1)S(1)} %pad_maximum_fusion.refs_3_, bf16[128,1280]{1,0:T(8,128)(2,1)S(1)} %constant_dynamic-update-slice_fusion.2.refs_4_, ...), custom_call_target="tpu_custom_call" | custom-call | tf_op jit(solution)/shard_map/score/pallas_call | solution.py:181
  103.4 10.8 %all_to_all.5.refs_2_ = f32[32,8,128]{2,1,0:T(8,128)} all-to-all(f32[32,8,128]{2,1,0:T(8,128)S(1)} %score.1), channel_id=1, replica_groups=mesh['ctx'=8,'tp'=4] {'ctx','tp'}, dimensions={0} | all-to-all | bytes 262144 | tf_op jit(solution)/shard_map/all_to_all | solution.py:274
  114.2 1.5 %merge.1 = (f32[1,64]{1,0:T(1,128)}, f32[1,64]{1,0:T(1,128)}) custom-call(s32[3]{0:T(128)} %copy-done.6, f32[1,64]{1,0:T(1,128)} %bitcast.20, f32[32,8,128]{2,1,0:T(8,128)} %all_to_all.5.refs_2_), custom_call_target="tpu_custom_call" | custom-call | tf_op jit(solution)/shard_map/merge/pallas_call | solution.py:218
  (23 shorter events, 0.1 us)
Async XLA Ops:
  0.6 27.4 %collective-permute-start.11 = (bf16[2048,640]{1,0:T(8,128)(2,1)}, bf16[2048,640]{1,0:T(8,128)(2,1)S(1)}, u32[]{:S(2)}, u32[]{:S(2)}) collective-permute-start(bf16[2048,640]{1,0:T(8,128)(2,1)} %refs_15_.1), channel_id=1, source_target_pairs={{0,4},{4,0},{8,12},{12,8},{16,20},{20,16},{24,28},{28,24},{1,5},{5... | collective-permute-start | bytes 7864328 | tf_op jit(solution)/shard_map/ppermute | solution.py:21
  1.1 94.6 %collective-permute-start.24 = (bf16[5120,384]{1,0:T(8,128)(2,1)}, bf16[5120,384]{1,0:T(8,128)(2,1)}, u32[]{:S(2)}, u32[]{:S(2)}) collective-permute-start(bf16[5120,384]{1,0:T(8,128)(2,1)} %refs_11_.1), channel_id=1, source_target_pairs={{0,4},{4,0},{8,12},{12,8},{16,20},{20,16},{24,28},{28,24},{1,5},{5... | collective-permute-start | bytes 11796488 | tf_op jit(solution)/shard_map/ppermute | solution.py:21
  2.7 7.0 %collective-permute-start.9 = (bf16[64,512]{1,0:T(8,128)(2,1)S(1)}, bf16[64,512]{1,0:T(8,128)(2,1)S(1)}, u32[]{:S(2)}, u32[]{:S(2)}) collective-permute-start(bf16[64,512]{1,0:T(8,128)(2,1)S(1)} %constant_dynamic-update-slice_fusion.refs_10_), channel_id=1, source_target_pairs={{0,24},{4,28},{8,16},{12,20},{16,8},{20,12},{24,0},{28,4},{1,25},{... | collective-permute-start | bytes 196616 | tf_op jit(solution)/shard_map/ppermute | solution.py:21
  7.6 8.8 %collective-permute-start.4 = (bf16[64,1024]{1,0:T(8,128)(2,1)S(1)}, bf16[64,1024]{1,0:T(8,128)(2,1)S(1)}, u32[]{:S(2)}, u32[]{:S(2)}) collective-permute-start(bf16[64,1024]{1,0:T(8,128)(2,1)S(1)} %get-tuple-element.14.refs_3_), channel_id=1, source_target_pairs={{0,16},{4,20},{8,24},{12,28},{16,0},{20,4},{24,8},{28,12},{1,17},{... | collective-permute-start | bytes 393224 | tf_op jit(solution)/shard_map/ppermute | solution.py:21
  8.2 6.1 %collective-permute-start.8 = (bf16[64,512]{1,0:T(8,128)(2,1)S(1)}, bf16[64,512]{1,0:T(8,128)(2,1)S(1)}, u32[]{:S(2)}, u32[]{:S(2)}) collective-permute-start(bf16[64,512]{1,0:T(8,128)(2,1)S(1)} %constant_dynamic-update-slice_fusion.refs_10_), channel_id=1, source_target_pairs={{0,16},{4,20},{8,24},{12,28},{16,0},{20,4},{24,8},{28,12},{1,17},{... | collective-permute-start | bytes 196616 | tf_op jit(solution)/shard_map/ppermute | solution.py:21
  9.7 5.3 %collective-permute-start.7 = (bf16[64,512]{1,0:T(8,128)(2,1)S(1)}, bf16[64,512]{1,0:T(8,128)(2,1)S(1)}, u32[]{:S(2)}, u32[]{:S(2)}) collective-permute-start(bf16[64,512]{1,0:T(8,128)(2,1)S(1)} %constant_dynamic-update-slice_fusion.refs_10_), channel_id=1, source_target_pairs={{0,8},{4,12},{8,0},{12,4},{16,24},{20,28},{24,16},{28,20},{1,9},{5... | collective-permute-start | bytes 196616 | tf_op jit(solution)/shard_map/ppermute | solution.py:21
  14.3 5.3 %collective-permute-start.2 = (bf16[64,1024]{1,0:T(8,128)(2,1)S(1)}, bf16[64,1024]{1,0:T(8,128)(2,1)}, u32[]{:S(2)}, u32[]{:S(2)}) collective-permute-start(bf16[64,1024]{1,0:T(8,128)(2,1)S(1)} %get-tuple-element.14.refs_3_), channel_id=1, source_target_pairs={{0,8},{4,12},{8,0},{12,4},{16,24},{20,28},{24,16},{28,20},{1,9},{5... | collective-permute-start | bytes 393224 | tf_op jit(solution)/shard_map/ppermute | solution.py:21
  15.0 5.1 %collective-permute-start.3 = (bf16[64,1024]{1,0:T(8,128)(2,1)S(1)}, bf16[64,1024]{1,0:T(8,128)(2,1)}, u32[]{:S(2)}, u32[]{:S(2)}) collective-permute-start(bf16[64,1024]{1,0:T(8,128)(2,1)S(1)} %get-tuple-element.15.refs_2_), channel_id=1, source_target_pairs={{0,16},{4,20},{8,24},{12,28},{16,0},{20,4},{24,8},{28,12},{1,17},{... | collective-permute-start | bytes 393224 | tf_op jit(solution)/shard_map/ppermute | solution.py:21
  16.4 0.7 copy-start.2
  17.0 5.0 %collective-permute-start.1 = (bf16[64,1024]{1,0:T(8,128)(2,1)S(1)}, bf16[64,1024]{1,0:T(8,128)(2,1)S(1)}, u32[]{:S(2)}, u32[]{:S(2)}) collective-permute-start(bf16[64,1024]{1,0:T(8,128)(2,1)S(1)} %get-tuple-element.15.refs_2_), channel_id=1, source_target_pairs={{0,8},{4,12},{8,0},{12,4},{16,24},{20,28},{24,16},{28,20},{1,9},{5... | collective-permute-start | bytes 393224 | tf_op jit(solution)/shard_map/ppermute | solution.py:21
  19.6 8.4 %collective-permute-start.10 = (bf16[256,512]{1,0:T(8,128)(2,1)}, bf16[256,512]{1,0:T(8,128)(2,1)S(1)}, u32[]{:S(2)}, u32[]{:S(2)}) collective-permute-start(bf16[256,512]{1,0:T(8,128)(2,1)} %pad_maximum_fusion.1), channel_id=1, source_target_pairs={{0,4},{4,0},{8,12},{12,8},{16,20},{20,16},{24,28},{28,24},{1,5},{5... | collective-permute-start | bytes 786440 | tf_op jit(solution)/shard_map/ppermute | solution.py:21
  20.1 5.7 %collective-permute-start.6 = (bf16[64,1024]{1,0:T(8,128)(2,1)}, bf16[64,1024]{1,0:T(8,128)(2,1)}, u32[]{:S(2)}, u32[]{:S(2)}) collective-permute-start(bf16[64,1024]{1,0:T(8,128)(2,1)} %collective-permute-done.2.refs_5_), channel_id=1, source_target_pairs={{0,16},{4,20},{8,24},{12,28},{16,0},{20,4},{24,8},{28,12},{1,17},{... | collective-permute-start | bytes 393224 | tf_op jit(solution)/shard_map/ppermute | solution.py:21
  22.1 0.7 copy-start.4
  22.7 5.3 %collective-permute-start.5 = (bf16[64,1024]{1,0:T(8,128)(2,1)}, bf16[64,1024]{1,0:T(8,128)(2,1)}, u32[]{:S(2)}, u32[]{:S(2)}) collective-permute-start(bf16[64,1024]{1,0:T(8,128)(2,1)} %collective-permute-done.3.refs_6_), channel_id=1, source_target_pairs={{0,8},{4,12},{8,0},{12,4},{16,24},{20,28},{24,16},{28,20},{1,9},{5... | collective-permute-start | bytes 393224 | tf_op jit(solution)/shard_map/ppermute | solution.py:21
  24.9 58.7 %copy-start.9 = (s32[512]{0:T(512)S(1)}, s32[512]{0:T(512)}, u32[]{:S(2)}) copy-start(s32[512]{0:T(512)} %param.18) | copy-start | bytes 6148
  25.0 70.7 %copy-start.6 = (s32[3]{0:T(128)}, s32[3]{0:T(128)S(1)}, u32[]{:S(2)}) copy-start(s32[3]{0:T(128)S(1)} %pad_add_fusion.refs_0_) | copy-start | bytes 40
  28.0 1.7 %copy-start.1 = (bf16[2048,640]{1,0:T(8,128)(2,1)S(1)}, bf16[2048,640]{1,0:T(8,128)(2,1)}, u32[]{:S(2)}) copy-start(bf16[2048,640]{1,0:T(8,128)(2,1)} %refs_15_.1) | copy-start | bytes 7864324
  29.8 0.9 copy-start.3
  30.7 0.9 copy-start.5
  31.6 11.8 %copy-start.7 = (bf16[128,640]{1,0:T(8,128)(2,1)S(1)}, bf16[128,640]{1,0:T(8,128)(2,1)}, u32[]{:S(2)}) copy-start(bf16[128,640]{1,0:T(8,128)(2,1)} %param.15) | copy-start | bytes 491524
  31.6 52.0 %copy-start.8 = (bf16[5120]{0:T(1024)(128)(2,1)S(1)}, bf16[5120]{0:T(1024)(128)(2,1)}, u32[]{:S(2)}) copy-start(bf16[5120]{0:T(1024)(128)(2,1)} %param.16) | copy-start | bytes 30724
  38.9 6.9 %collective-permute-start.12 = (bf16[64,1280]{1,0:T(8,128)(2,1)S(1)}, bf16[64,1280]{1,0:T(8,128)(2,1)S(1)}, u32[]{:S(2)}, u32[]{:S(2)}) collective-permute-start(bf16[64,1280]{1,0:T(8,128)(2,1)S(1)} %get-tuple-element.9), channel_id=1, source_target_pairs={{0,1},{1,0},{2,3},{3,2},{4,5},{5,4},{6,7},{7,6},{8,9},{9,8},{10,11... | collective-permute-start | bytes 491528 | tf_op jit(solution)/shard_map/ppermute | solution.py:21
  40.6 13.9 %collective-permute-start.13 = (bf16[64,1280]{1,0:T(8,128)(2,1)S(1)}, bf16[64,1280]{1,0:T(8,128)(2,1)S(1)}, u32[]{:S(2)}, u32[]{:S(2)}) collective-permute-start(bf16[64,1280]{1,0:T(8,128)(2,1)S(1)} %get-tuple-element.10), channel_id=1, source_target_pairs={{0,2},{1,3},{2,0},{3,1},{4,6},{5,7},{6,4},{7,5},{8,10},{9,11},{10,... | collective-permute-start | bytes 491528 | tf_op jit(solution)/shard_map/ppermute | solution.py:21
  43.1 11.3 %collective-permute-start.14 = (bf16[64,1280]{1,0:T(8,128)(2,1)S(1)}, bf16[64,1280]{1,0:T(8,128)(2,1)S(1)}, u32[]{:S(2)}, u32[]{:S(2)}) collective-permute-start(bf16[64,1280]{1,0:T(8,128)(2,1)S(1)} %get-tuple-element.11), channel_id=1, source_target_pairs={{0,3},{1,2},{2,1},{3,0},{4,7},{5,6},{6,5},{7,4},{8,11},{9,10},{10,... | collective-permute-start | bytes 491528 | tf_op jit(solution)/shard_map/ppermute | solution.py:21
  43.4 1.3 %collective-permute-start = (bf16[1,64,640]{2,1,0:T(8,128)(2,1)S(1)}, bf16[1,64,640]{2,1,0:T(8,128)(2,1)S(1)}, u32[]{:S(2)}, u32[]{:S(2)}) collective-permute-start(bf16[1,64,640]{2,1,0:T(8,128)(2,1)S(1)} %get-tuple-element.17), channel_id=1, source_target_pairs={{0,4},{4,0},{8,12},{12,8},{16,20},{20,16},{24,28},{28,24},{1,5},{5... | collective-permute-start | bytes 245768 | tf_op jit(solution)/shard_map/ppermute | solution.py:21
  54.6 7.7 %collective-permute-start.15 = (bf16[64,1280]{1,0:T(8,128)(2,1)S(1)}, bf16[64,1280]{1,0:T(8,128)(2,1)S(1)}, u32[]{:S(2)}, u32[]{:S(2)}) collective-permute-start(bf16[64,1280]{1,0:T(8,128)(2,1)S(1)} %fusion.3), channel_id=1, source_target_pairs={{0,1},{1,0},{2,3},{3,2},{4,5},{5,4},{6,7},{7,6},{8,9},{9,8},{10,11... | collective-permute-start | bytes 491528 | tf_op jit(solution)/shard_map/ppermute | solution.py:21
  56.9 15.1 %collective-permute-start.17 = (bf16[64,1280]{1,0:T(8,128)(2,1)S(1)}, bf16[64,1280]{1,0:T(8,128)(2,1)S(1)}, u32[]{:S(2)}, u32[]{:S(2)}) collective-permute-start(bf16[64,1280]{1,0:T(8,128)(2,1)S(1)} %fusion.3), channel_id=1, source_target_pairs={{0,3},{1,2},{2,1},{3,0},{4,7},{5,6},{6,5},{7,4},{8,11},{9,10},{10,... | collective-permute-start | bytes 491528 | tf_op jit(solution)/shard_map/ppermute | solution.py:21
  59.5 12.6 %collective-permute-start.16 = (bf16[64,1280]{1,0:T(8,128)(2,1)S(1)}, bf16[64,1280]{1,0:T(8,128)(2,1)S(1)}, u32[]{:S(2)}, u32[]{:S(2)}) collective-permute-start(bf16[64,1280]{1,0:T(8,128)(2,1)S(1)} %fusion.3), channel_id=1, source_target_pairs={{0,2},{1,3},{2,0},{3,1},{4,6},{5,7},{6,4},{7,5},{8,10},{9,11},{10,... | collective-permute-start | bytes 491528 | tf_op jit(solution)/shard_map/ppermute | solution.py:21
  62.3 12.7 %collective-permute-start.20 = (bf16[128,1280]{1,0:T(8,128)(2,1)S(1)}, bf16[128,1280]{1,0:T(8,128)(2,1)S(1)}, u32[]{:S(2)}, u32[]{:S(2)}) collective-permute-start(bf16[128,1280]{1,0:T(8,128)(2,1)S(1)} %pad_maximum_fusion.refs_3_), channel_id=1, source_target_pairs={{0,16},{4,20},{8,24},{12,28},{16,0},{20,4},{24,8},{28,12},{1,17},{... | collective-permute-start | bytes 983048 | tf_op jit(solution)/shard_map/ppermute | solution.py:21
  72.1 11.5 %collective-permute-start.19 = (bf16[128,1280]{1,0:T(8,128)(2,1)S(1)}, bf16[128,1280]{1,0:T(8,128)(2,1)S(1)}, u32[]{:S(2)}, u32[]{:S(2)}) collective-permute-start(bf16[128,1280]{1,0:T(8,128)(2,1)S(1)} %constant_dynamic-update-slice_fusion.2.refs_4_), channel_id=1, source_target_pairs={{0,8},{4,12},{8,0},{12,4},{16,24},{20,28},{24,16},{28,20},{1,9},{5... | collective-permute-start | bytes 983048 | tf_op jit(solution)/shard_map/ppermute | solution.py:21
  74.9 15.6 %collective-permute-start.18 = (bf16[128,1280]{1,0:T(8,128)(2,1)S(1)}, bf16[128,1280]{1,0:T(8,128)(2,1)S(1)}, u32[]{:S(2)}, u32[]{:S(2)}) collective-permute-start(bf16[128,1280]{1,0:T(8,128)(2,1)S(1)} %pad_maximum_fusion.refs_3_), channel_id=1, source_target_pairs={{0,8},{4,12},{8,0},{12,4},{16,24},{20,28},{24,16},{28,20},{1,9},{5... | collective-permute-start | bytes 983048 | tf_op jit(solution)/shard_map/ppermute | solution.py:21
  75.0 15.6 %collective-permute-start.21 = (bf16[128,1280]{1,0:T(8,128)(2,1)S(1)}, bf16[128,1280]{1,0:T(8,128)(2,1)S(1)}, u32[]{:S(2)}, u32[]{:S(2)}) collective-permute-start(bf16[128,1280]{1,0:T(8,128)(2,1)S(1)} %constant_dynamic-update-slice_fusion.2.refs_4_), channel_id=1, source_target_pairs={{0,16},{4,20},{8,24},{12,28},{16,0},{20,4},{24,8},{28,12},{1,17},{... | collective-permute-start | bytes 983048 | tf_op jit(solution)/shard_map/ppermute | solution.py:21
  75.0 20.7 %collective-permute-start.22 = (bf16[128,1280]{1,0:T(8,128)(2,1)S(1)}, bf16[128,1280]{1,0:T(8,128)(2,1)S(1)}, u32[]{:S(2)}, u32[]{:S(2)}) collective-permute-start(bf16[128,1280]{1,0:T(8,128)(2,1)S(1)} %collective-permute-done.20.refs_7_), channel_id=1, source_target_pairs={{0,8},{4,12},{8,0},{12,4},{16,24},{20,28},{24,16},{28,20},{1,9},{5... | collective-permute-start | bytes 983048 | tf_op jit(solution)/shard_map/ppermute | solution.py:21
  83.6 12.1 %collective-permute-start.23 = (bf16[128,1280]{1,0:T(8,128)(2,1)S(1)}, bf16[128,1280]{1,0:T(8,128)(2,1)S(1)}, u32[]{:S(2)}, u32[]{:S(2)}) collective-permute-start(bf16[128,1280]{1,0:T(8,128)(2,1)S(1)} %collective-permute-done.19.refs_6_), channel_id=1, source_target_pairs={{0,16},{4,20},{8,24},{12,28},{16,0},{20,4},{24,8},{28,12},{1,17},{... | collective-permute-start | bytes 983048 | tf_op jit(solution)/shard_map/ppermute | solution.py:21
  95.7 2.1 %copy-start = (bf16[5120,384]{1,0:T(8,128)(2,1)S(1)}, bf16[5120,384]{1,0:T(8,128)(2,1)}, u32[]{:S(2)}) copy-start(bf16[5120,384]{1,0:T(8,128)(2,1)} %refs_11_.1) | copy-start | bytes 11796484

commit v2 on v1

v2 whole, which is shorter than its diff:
```python
import jax
import jax.numpy as jnp
from jax import lax
from jax.experimental import pallas as pl
from jax.experimental.pallas import tpu as pltpu
from jax.sharding import PartitionSpec as P

HD = 128
EPSILON = 1e-06
CEILING = 10.0
NEGATIVE = -1e30
F32 = jnp.float32
BF16 = jnp.bfloat16
VMEM = pl.BlockSpec(memory_space=pltpu.VMEM)
SMEM = pl.BlockSpec(memory_space=pltpu.SMEM)
HBM = pl.BlockSpec(memory_space=pltpu.HBM)
ANY = pl.BlockSpec(memory_space=pl.ANY)


def swap(x, axis, k):
    size = lax.axis_size(axis)
    return lax.ppermute(x, axis, [(i, i ^ k) for i in range(size)])


def sides(piece, chips):
    if chips != 4:
        return [piece] + [swap(piece, "ctx", 2 * j) for j in range(1, chips)]
    return [piece, swap(piece, "ctx", 2), swap(piece, "ctx", 4)]


def corners(found, turn):
    if len(found) != 3:
        return found
    return [*found, swap(found[2 - turn], "ctx", 2 + 2 * turn)]


def attend_kernel(counts, tp_count, own_rows, kv_width, ks, blocks, place_ref, after_ref, lens_ref, weight_ref, *refs):
    chips, total = len(counts), sum(counts)
    outs = refs[total : total + len(ks)]
    queries, keys, values, mixed = refs[total + len(ks) :]
    ctx, tp, slab_start = place_ref[0], place_ref[1], place_ref[2]
    kv_heads = kv_width // HD
    depth = queries.shape[1]
    group = depth // kv_width
    length = keys.shape[0]
    owners = [(tp ^ k) * blocks + 2 * b + lax.rem(ctx, 2) for k in ks for b in range(blocks // 2)]
    for j in range(chips):
        parts = refs[sum(counts[:j]) : sum(counts[: j + 1])]
        if parts[0].shape[1] == depth:
            spans = [(parts[0], 0, 0, depth)]
            own, sib, start = parts[1], parts[1], 2 * kv_width
            at = 0
        else:
            half = depth // 2
            spans = [(parts[0], 0, 0, half), (parts[1], 0, half, half)]
            own, sib, start = parts[0], parts[1], half
            at = half
        own_at = pl.ds(pl.multiple_of((ctx ^ (2 * j)) * own_rows, own_rows), own_rows)
        sib_at = pl.ds(pl.multiple_of((ctx ^ (2 * j + 1)) * own_rows, own_rows), own_rows)
        for rows, part, first in ((own_at, own, at), (sib_at, sib, start)):
            keys[rows, :] = part[:, first : first + kv_width]
            values[rows, :] = part[:, first + kv_width : first + 2 * kv_width]
        for i, owner in enumerate(owners):

            @pl.when(owner == (ctx ^ (2 * j)))
            def _(spans=spans, i=i):
                for part, first, target, width in spans:
                    queries[i * own_rows : (i + 1) * own_rows, target : target + width] = part[:, first : first + width]

    count = lens_ref.shape[1]
    first = lax.broadcasted_iota(jnp.int32, (count, count), 0)
    second = lax.broadcasted_iota(jnp.int32, (count, count), 1)
    column = jnp.sum(jnp.where(first == second, lens_ref[...], 0), axis=1, keepdims=True)
    ends = jnp.sum(jnp.where(first <= second, column, 0), axis=0, keepdims=True)
    columns = lax.broadcasted_iota(jnp.int32, (own_rows, length), 1)
    for i, owner in enumerate(owners):
        spot = owner * own_rows + lax.broadcasted_iota(jnp.int32, (own_rows, 1), 0)
        opened = jnp.max(jnp.where(ends <= spot + slab_start, ends, 0), axis=1, keepdims=True) - slab_start
        allowed = ((columns <= spot) & (columns >= opened))[None]
        at = slice(i * own_rows, (i + 1) * own_rows)
        for h in range(kv_heads):
            heads = [(h * group + g) * HD for g in range(group)]
            stack = jnp.concatenate([queries[at, head : head + HD] for head in heads], axis=0)
            scores = lax.dot_general(
                stack, keys[:, h * HD : (h + 1) * HD], (((1,), (1,)), ((), ())), preferred_element_type=F32
            ).reshape(group, own_rows, length)
            scores = jnp.where(allowed, scores, NEGATIVE)
            highest = jnp.max(scores, axis=2, keepdims=True)
            weights = jnp.exp((scores - highest) * HD ** (-0.5))
            denominator = jnp.sum(weights, axis=2, keepdims=True).reshape(group * own_rows, 1)
            mix = jnp.dot(
                weights.reshape(group * own_rows, length).astype(BF16),
                values[:, h * HD : (h + 1) * HD],
                preferred_element_type=F32,
            )
            mix = (mix / denominator).astype(BF16)
            for g, head in enumerate(heads):
                mixed[i * own_rows : (i + 1) * own_rows, head : head + HD] = mix[g * own_rows : (g + 1) * own_rows]
    product = jnp.dot(mixed[...], weight_ref[...], preferred_element_type=F32)
    span = blocks // 2 * own_rows
    for i, out in enumerate(outs):
        out[...] = product[i * span : (i + 1) * span].astype(out.dtype)


def attend(place, after, lens, sets, kv_width, weight, ks, tp_count, blocks):
    chips, own_rows = len(sets), sets[0][0].shape[0]
    length = 2 * chips * own_rows
    depth, width = weight.shape
    span = blocks // 2 * own_rows
    rows = len(ks) * span
    need = 2 * depth * width + chips * own_rows * depth * 2 + rows * (depth * 4 + width * 16) + 24 * 8 * own_rows * length
    return pl.pallas_call(
        lambda *refs: attend_kernel([len(one) for one in sets], tp_count, own_rows, kv_width, ks, blocks, *refs),
        out_shape=[jax.ShapeDtypeStruct((span, width), F32 if k == 0 else BF16) for k in ks],
        in_specs=[SMEM, ANY] + [VMEM] * (2 + sum(len(one) for one in sets)),
        out_specs=[VMEM] * len(ks),
        scratch_shapes=[
            pltpu.VMEM((rows, depth), BF16),
            pltpu.VMEM((length, kv_width), BF16),
            pltpu.VMEM((length, kv_width), BF16),
            pltpu.VMEM((rows, depth), BF16),
        ],
        compiler_params=pltpu.CompilerParams(vmem_limit_bytes=need + (8 << 20)),
        name="attend",
    )(place, after, lens, weight, *[part for one in sets for part in one])


def update_kernel(blocks, own_rows, place_ref, after_ref, stream_ref, stream_sib_ref, *refs):
    sums, out_ref = refs[:-1], refs[-1]
    core = lax.rem(place_ref[0], 2)
    width = stream_ref.shape[1]
    for b in range(blocks // 2):
        source = pl.ds(pl.multiple_of((2 * b + core) * own_rows, own_rows), own_rows)
        target = slice(b * own_rows, (b + 1) * own_rows)
        for side, part in enumerate((stream_ref, stream_sib_ref)):
            columns = slice(side * width, (side + 1) * width)
            total = part[source, :].astype(F32)
            for one in sums:
                total += one[target, columns].astype(F32)
            out_ref[target, columns] = total.astype(BF16)


def update(place, after, stream, stream_sib, sums, blocks, own_rows):
    return pl.pallas_call(
        lambda *refs: update_kernel(blocks, own_rows, *refs),
        out_shape=jax.ShapeDtypeStruct(sums[0].shape, BF16),
        in_specs=[SMEM, ANY] + [VMEM] * (2 + len(sums)),
        out_specs=VMEM,
        compiler_params=pltpu.CompilerParams(vmem_limit_bytes=6 << 20),
        name="update",
    )(place, after, stream, stream_sib, *sums)


def stage_kernel(place_ref, own_ref, sib_ref, both_ref, mark_ref, sems):
    ranks = sems.shape[1]
    part, width = own_ref.shape[0] // ranks, own_ref.shape[1]
    mark_ref[...] = jnp.zeros(mark_ref.shape, F32)
    if width % 128:
        for k in range(ranks):
            source = pl.ds(pl.multiple_of((place_ref[0] ^ k) * part, part), part) if ranks > 1 else slice(0, part)
            both_ref[k * part : (k + 1) * part, :width] = own_ref[source, :]
            both_ref[k * part : (k + 1) * part, width:] = sib_ref[source, :]
        return
    copies = []
    for k in range(ranks):
        source = pl.ds(pl.multiple_of((place_ref[0] ^ k) * part, part), part) if ranks > 1 else slice(0, part)
        target = slice(k * part, (k + 1) * part)
        copies.append(pltpu.make_async_copy(own_ref.at[source], both_ref.at[target, :width], sems.at[0, k]))
        copies.append(pltpu.make_async_copy(sib_ref.at[source], both_ref.at[target, width:], sems.at[1, k]))
    for copy in copies:
        copy.start()
    for copy in copies:
        copy.wait()


def stage(place, own, sib, ranks):
    depth, width = own.shape
    return pl.pallas_call(
        stage_kernel,
        out_shape=[jax.ShapeDtypeStruct((depth, 2 * width), BF16), jax.ShapeDtypeStruct((8, 128), F32)],
        in_specs=[SMEM] + [VMEM if width % 128 else HBM] * 2,
        out_specs=[VMEM, VMEM],
        scratch_shapes=[pltpu.SemaphoreType.DMA((2, ranks))],
        compiler_params=pltpu.CompilerParams(vmem_limit_bytes=(8 if width % 128 else 4) * depth * width + (4 << 20)),
        name="stage",
    )(place, own, sib)


def score_kernel(chips, tp_count, own_rows, blocks, first, place_ref, tokens_ref, gain_ref, head_ref, *refs):
    pieces, out_ref, normed = refs[:-2], refs[-2], refs[-1]
    spans = len(pieces) // chips
    ctx, tp = place_ref[0], place_ref[1]
    ranks = 2 * chips
    part, vocab = head_ref.shape[0] // ranks, head_ref.shape[1] // 2
    span_rows = pieces[0].shape[0]
    squares = [jnp.zeros((span_rows, 1), F32)] * spans
    for j in range(chips):
        gain = jnp.concatenate([gain_ref[pl.ds(ctx ^ (2 * j), 1), :], gain_ref[pl.ds(ctx ^ (2 * j + 1), 1), :]], axis=1)
        for s in range(spans):
            wide = pieces[s * chips + j][...].astype(F32)
            squares[s] += jnp.sum(wide * wide, axis=1, keepdims=True)
            normed[s * span_rows : (s + 1) * span_rows, 2 * j * part : 2 * (j + 1) * part] = (wide * gain).astype(BF16)
    square = jnp.concatenate(squares, axis=0)
    inverse = lax.rsqrt(square * (1.0 / (ranks * part)) + EPSILON)
    logits = jnp.dot(normed[...], head_ref[...], preferred_element_type=F32) * inverse
    rows = logits.shape[0]
    column = lax.broadcasted_iota(jnp.int32, (1, 2 * vocab), 1)
    offset = jnp.where(column < vocab, (ctx * tp_count + tp) * vocab, ((ctx ^ 1) * tp_count + tp) * vocab - vocab)
    owners = [
        (tp ^ k) * blocks + 2 * b + lax.rem(ctx, 2) for k in range(first, first + spans) for b in range(blocks // 2)
    ]
    length = tokens_ref.shape[1]
    line = lax.broadcasted_iota(jnp.int32, (own_rows, length), 1) - lax.broadcasted_iota(jnp.int32, (own_rows, length), 0)
    tokens = jnp.concatenate(
        [
            jnp.sum(jnp.where(line == owner * own_rows, tokens_ref[...], 0), axis=1, keepdims=True)
            for owner in owners
        ],
        axis=0,
    )
    highest = jnp.max(logits, axis=1, keepdims=True)
    total = jnp.sum(jnp.exp(logits - highest), axis=1, keepdims=True)
    target = jnp.sum(jnp.where(column + offset == tokens, logits, 0.0), axis=1, keepdims=True)
    lane = lax.broadcasted_iota(jnp.int32, (rows, 128), 1)
    packed = jnp.where(lane == 0, highest, jnp.where(lane == 1, total, jnp.where(lane == 2, target, 0.0)))
    turned = packed.T[:8]
    out_ref[...] = jnp.zeros(out_ref.shape, F32)
    for i, owner in enumerate(owners):
        tile = turned[:, i * own_rows : (i + 1) * own_rows]
        for k in range(tp_count):
            out_ref[pl.ds(owner * tp_count + k, 1), :, :own_rows] = tile[None]


def score(place, tokens, gain, head, spans, first, tp_count, own_rows, blocks):
    chips = len(spans[0])
    rows = len(spans) * spans[0][0].shape[0]
    depth, vocab = head.shape
    need = 2 * depth * vocab + rows * depth * 6 + rows * vocab * 4 * 8
    return pl.pallas_call(
        lambda *refs: score_kernel(chips, tp_count, own_rows, blocks, first, *refs),
        out_shape=jax.ShapeDtypeStruct((2 * chips * tp_count, 8, 128), F32),
        in_specs=[SMEM] + [VMEM] * (3 + len(spans) * chips),
        out_specs=VMEM,
        scratch_shapes=[pltpu.VMEM((rows, depth), BF16)],
        compiler_params=pltpu.CompilerParams(vmem_limit_bytes=need + (12 << 20)),
        name="score",
    )(place, tokens, gain, head, *[piece for span in spans for piece in span])


def merge_kernel(chips, tp_count, place_ref, policy_ref, stats_ref, logprob_ref, penalty_ref):
    parity = lax.rem(place_ref[0], 2)
    own_rows = policy_ref.shape[1]
    tiles = [
        stats_ref[(2 * j + parity) * tp_count + k] for j in range(chips) for k in range(tp_count)
    ]
    highest = tiles[0][0:1]
    for tile in tiles[1:]:
        highest = jnp.maximum(highest, tile[0:1])
    total = jnp.zeros_like(highest)
    target = jnp.zeros_like(highest)
    for tile in tiles:
        total += tile[1:2] * jnp.exp(tile[0:1] - highest)
        target += tile[2:3]
    logprob = (target - (highest + jnp.log(total)))[:, :own_rows]
    ratio = logprob - policy_ref[...]
    logprob_ref[...] = logprob
    penalty_ref[...] = jnp.minimum(jnp.exp(ratio) - ratio - 1.0, CEILING)


def merge(place, policy, stats, chips, tp_count):
    shape = jax.ShapeDtypeStruct(policy.shape, F32)
    return pl.pallas_call(
        lambda *refs: merge_kernel(chips, tp_count, *refs),
        out_shape=[shape, shape],
        in_specs=[SMEM, VMEM, VMEM],
        out_specs=[VMEM, VMEM],
        compiler_params=pltpu.CompilerParams(vmem_limit_bytes=4 << 20),
        name="merge",
    )(place, policy, stats)


def local(
    queries,
    key_rows,
    value_rows,
    out_weight,
    stream,
    final_gain,
    head_weight,
    token_ids,
    policy_logprob,
    doc_lengths,
    slab_start,
):
    ctx_count, tp_count = lax.axis_size("ctx"), lax.axis_size("tp")
    ctx, tp = lax.axis_index("ctx"), lax.axis_index("tp")
    chips = ctx_count // 2
    own_rows = queries.shape[0]
    blocks = ctx_count // tp_count
    mid = tp_count // 2
    place = jnp.stack([ctx, tp, slab_start[0]]).astype(jnp.int32)

    kv = [key_rows, value_rows, swap(key_rows, "ctx", 1), swap(value_rows, "ctx", 1)]
    kv = jnp.concatenate(kv, axis=1)
    kv, out_weight, stream = lax.optimization_barrier((kv, out_weight, stream))
    sets = list(zip(sides(queries, chips), sides(kv, chips)))
    if len(sets) < chips:
        half, inner = queries.shape[1] // 2, kv.shape[1] // 2
        below = jnp.concatenate([sets[2][0][:, :half], sets[2][1][:, :inner]], axis=1)
        above = jnp.concatenate([sets[1][0][:, half:], sets[1][1][:, inner:]], axis=1)
        sets.append((swap(below, "ctx", 2), swap(above, "ctx", 4)))
    out_sibling = swap(out_weight, "ctx", 1)
    stream_sibling = swap(stream, "ctx", 1)
    weight, mark = stage(place, out_weight, out_sibling, 1)
    mark, stream_sibling = lax.optimization_barrier((mark, stream_sibling))

    lens, kv_width = doc_lengths[None], key_rows.shape[1]
    far = attend(place, mark, lens, sets, kv_width, weight, range(mid, tp_count), tp_count, blocks)
    head_weight, *far = lax.optimization_barrier((head_weight, *far))
    head_sibling = swap(head_weight, "ctx", 1)
    near = attend(place, far[0], lens, sets, kv_width, weight, range(mid), tp_count, blocks)
    sums = [*near, *far]
    received = [swap(sums[k], "tp", k) for k in range(1, tp_count)]
    head_sibling, gain, tokens, sums[0] = lax.optimization_barrier((head_sibling, final_gain, token_ids, sums[0]))
    head, mark = stage(place, head_weight, head_sibling, ctx_count)
    gain, tokens = gain.astype(F32).reshape(ctx_count, -1), tokens[None]
    mark, gain, tokens = lax.optimization_barrier((mark, gain, tokens))
    updated = update(place, mark, stream, stream_sibling, [sums[0]] + received, blocks, own_rows)
    pieces, spans = [updated], []
    for k in range(1, tp_count):
        step = k & -k
        pieces.append(swap(pieces[k - step], "tp", step))
    for k, piece in enumerate(pieces):
        if k >= 2:
            piece, spans[k - 2] = lax.optimization_barrier((piece, spans[k - 2]))
        found = sides(piece, chips)
        spans.append(corners(found, k % 2))
    stats = score(place, tokens, gain, head, spans[:mid], 0, tp_count, own_rows, blocks) + score(
        place, tokens, gain, head, spans[mid:], mid, tp_count, own_rows, blocks
    )
    stats = lax.all_to_all(stats, ("ctx", "tp"), 0, 0, tiled=True)
    logprob, penalty = merge(place, policy_logprob[None], stats, chips, tp_count)
    return (logprob[0], penalty[0])


def solution(mesh):
    placed = (
        P("ctx", "tp"),
        P("ctx", "tp"),
        P("ctx", "tp"),
        P("tp", "ctx"),
        P("tp", "ctx"),
        P(),
        P(None, ("ctx", "tp")),
        P(),
        P("ctx"),
        P(),
        P(),
    )
    return jax.shard_map(
        local, mesh=mesh, in_specs=placed, out_specs=(P("ctx"), P("ctx")), check_vma=False
    )
```

time: 116 us -> 100 us (0.86)
  waiting for transfers between devices: 50 us -> 21.6 us
  starting transfers between devices: 27.7 us -> 37.8 us
  Pallas kernels: 14.4 us -> 17.7 us
  local copies, waits for them, and re-layouts: 10.5 us -> 8.13 us
  other arithmetic: 0.93 us -> 2.29 us
    ppermute x25 -> x29, waiting for transfers between devices: 50 us -> 21.6 us  [swap(): return lax.ppermute(x, axis, [(i, i ^ k) for i in range(size)])]
    ppermute x25 -> x29, starting transfers between devices: 27.7 us -> 37.8 us  [swap(): return lax.ppermute(x, axis, [(i, i ^ k) for i in range(size)])]
    pallas_call x1 -> x5, Pallas kernels: 7.33 us -> 12 us  [the longest x2 8.39 us: attend(): pl.pallas_call(lambda *refs: attend_kernel([len(one) for one in sets], tp...]
    concatenate x2 -> x3, other arithmetic: 0.76 us -> 2.18 us  [the longest x1 0.78 us: local(): kv = jnp.concatenate(kv, axis=1)]
    pallas_call x1 -> x2, Pallas kernels: 5.55 us -> 4.56 us  [score(): pl.pallas_call(lambda *refs: score_kernel(chips, tp_count, own_rows, bloc...]
    unnamed x22 -> x28, local copies, waits for them, and re-layouts: 7.77 us -> 8.07 us
  transfers between devices with their start and end apart: 25 -> 29, of which waited for: 14 -> 10; matrix products, arithmetic and copies ran while one was open for 4% -> 2% of each run, Pallas kernels for 6% -> 9%
where the time goes in v2:
time: 100 us; the launch traced here: 99.7 us
  starting transfers between devices  37.8 us (38%)
  waiting for transfers between devices  21.6 us (22%)
  Pallas kernels  17.7 us (18%)
  blocking collectives  10.7 us (11%)
  local copies, waits for them, and re-layouts  8.13 us (8%)
  other arithmetic  2.29 us (2%)
  between operations  1.53 us (2%)
    ppermute x29, starting transfers between devices, swap(): return lax.ppermute(x, axis, [(i, i ^ k) for i in range(size)])  37.8 us
    ppermute x29, waiting for transfers between devices, swap(): return lax.ppermute(x, axis, [(i, i ^ k) for i in range(size)])  21.6 us
    all_to_all x1, blocking collectives, local(): stats = lax.all_to_all(stats, ('ctx', 'tp'), 0, 0, tiled=True)  10.7 us
    pallas_call x2, Pallas kernels, attend(): pl.pallas_call(lambda *refs: attend_kernel([len(one) for one in sets], tp...  8.39 us
    unnamed x28, local copies, waits for them, and re-layouts  8.07 us
    pallas_call x2, Pallas kernels, score(): pl.pallas_call(lambda *refs: score_kernel(chips, tp_count, own_rows, bloc...  4.56 us
    pallas_call x2, Pallas kernels, stage(): pl.pallas_call(stage_kernel, out_shape=[jax.ShapeDtypeStruct((depth, 2 *...  2.56 us
  transfers between devices with their start and end apart: 29, of which 10 were waited for; matrix products, arithmetic and copies ran while one was open for 2% of the time, Pallas kernels for 9%

profile of v2, /device:TPU:0, one launch (start us, length us, event | category | flops | bytes accessed | tf_op | source)
XLA Modules:
  0.0 99.7 jit_solution(11650442524875514243)
XLA Ops:
  0.6 0.0 copy-start.4
  0.7 0.5 collective-permute-start
  1.2 0.1 collective-permute-start.1
  1.2 1.0 collective-permute-done
  2.2 0.3 collective-permute-done.1
  2.6 0.8 pad_maximum_fusion.2.refs_5_
  3.4 0.2 collective-permute-start.2
  3.6 2.9 %collective-permute-start.6 = (bf16[64,2048]{1,0:T(8,128)(2,1)}, bf16[64,2048]{1,0:T(8,128)(2,1)S(1)}, u32[]{:S(2)}, u32[]{:S(2)}) collective-permute-start(bf16[64,2048]{1,0:T(8,128)(2,1)} %refs_4_.3), channel_id=1, source_target_pairs={{0,16},{4,20},{8,24},{12,28},{16,0},{20,4},{24,8},{28,12},{1,17},{... | collective-permute-start | bytes 786440 | tf_op jit(solution)/shard_map/ppermute | solution.py:22
  6.5 0.0 collective-permute-start.7
  6.5 2.0 %collective-permute-start.5 = (bf16[64,1024]{1,0:T(8,128)(2,1)S(1)}, bf16[64,1024]{1,0:T(8,128)(2,1)S(1)}, u32[]{:S(2)}, u32[]{:S(2)}) collective-permute-start(bf16[64,1024]{1,0:T(8,128)(2,1)S(1)} %pad_maximum_fusion.2.refs_5_), channel_id=1, source_target_pairs={{0,8},{4,12},{8,0},{12,4},{16,24},{20,28},{24,16},{28,20},{1,9},{5... | collective-permute-start | bytes 393224 | tf_op jit(solution)/shard_map/ppermute | solution.py:22
  8.5 0.1 collective-permute-start.4
  8.5 7.6 %collective-permute-done.7.refs_9_ = bf16[64,1024]{1,0:T(8,128)(2,1)S(1)} collective-permute-done((bf16[64,1024]{1,0:T(8,128)(2,1)S(1)}, bf16[64,1024]{1,0:T(8,128)(2,1)S(1)}, u32[]{:S(2)}, u32[]{:S(2)}) %collective-permute-start.7) | collective-permute-done | bytes 131104 | tf_op jit(solution)/shard_map/ppermute | solution.py:22
  16.1 0.0 collective-permute-done.5.refs_7_
  16.2 0.0 collective-permute-done.6.refs_8_
  16.2 0.7 pad_maximum_fusion
  16.9 1.7 %collective-permute-start.8 = (bf16[64,1536]{1,0:T(8,128)(2,1)}, bf16[64,1536]{1,0:T(8,128)(2,1)}, u32[]{:S(2)}, u32[]{:S(2)}) collective-permute-start(bf16[64,1536]{1,0:T(8,128)(2,1)} %pad_maximum_fusion), channel_id=1, source_target_pairs={{0,8},{4,12},{8,0},{12,4},{16,24},{20,28},{24,16},{28,20},{1,9},{5... | collective-permute-start | bytes 589832 | tf_op jit(solution)/shard_map/ppermute | solution.py:22
  18.6 0.7 pad_maximum_fusion.1
  19.3 1.5 %collective-permute-start.9 = (bf16[64,1536]{1,0:T(8,128)(2,1)}, bf16[64,1536]{1,0:T(8,128)(2,1)}, u32[]{:S(2)}, u32[]{:S(2)}) collective-permute-start(bf16[64,1536]{1,0:T(8,128)(2,1)} %pad_maximum_fusion.1), channel_id=1, source_target_pairs={{0,16},{4,20},{8,24},{12,28},{16,0},{20,4},{24,8},{28,12},{1,17},{... | collective-permute-start | bytes 589832 | tf_op jit(solution)/shard_map/ppermute | solution.py:22
  20.9 0.0 collective-permute-start.3
  21.5 0.1 pad_add_fusion.place_ref.refs_0_
  21.6 1.7 %copy-done.3 = bf16[2048,640]{1,0:T(8,128)(2,1)S(1)} copy-done((bf16[2048,640]{1,0:T(8,128)(2,1)S(1)}, bf16[2048,640]{1,0:T(8,128)(2,1)}, u32[]{:S(2)}) %copy-start.3) | copy-done | bytes 2621464
  23.3 1.0 %stage.2 = (bf16[2048,1280]{1,0:T(8,128)(2,1)S(1)}, f32[8,128]{1,0:T(8,128)S(1)}) custom-call(s32[3]{0:T(128)S(1)} %pad_add_fusion.place_ref.refs_0_, bf16[2048,640]{1,0:T(8,128)(2,1)S(1)} %copy-done.3, bf16[2048,640]{1,0:T(8,128)(2,1)S(1)} %collective-permute-done.2.sib_ref), custom_call_target="tpu_custom_call" | custom-call | tf_op jit(solution)/shard_map/stage/pallas_call | solution.py:178
  24.4 0.0 copy-start.2
  24.4 0.0 collective-permute-done.8.refs_10_
  24.4 1.1 %collective-permute-done.9.refs_11_ = bf16[64,1536]{1,0:T(8,128)(2,1)} collective-permute-done((bf16[64,1536]{1,0:T(8,128)(2,1)}, bf16[64,1536]{1,0:T(8,128)(2,1)}, u32[]{:S(2)}, u32[]{:S(2)}) %collective-permute-start.9) | collective-permute-done | bytes 196640 | tf_op jit(solution)/shard_map/ppermute | solution.py:22
  25.5 4.1 %attend.2 = (bf16[64,1280]{1,0:T(8,128)(2,1)S(1)}, bf16[64,1280]{1,0:T(8,128)(2,1)S(1)}) custom-call(s32[3]{0:T(128)S(1)} %pad_add_fusion.place_ref.refs_0_, f32[8,128]{1,0:T(8,128)S(1)} %get-tuple-element.40.refs_1_, s32[1,64]{1,0:T(1,128)S(1)} %bitcast.9, bf16[2048,1280]{1,0:T(8,128)(2,1)S(1)} %get-tuple-element.41.refs_3_, ...), custom_call_target="tpu_custom_call" | custom-call | tf_op jit(solution)/shard_map/attend/pallas_call | solution.py:112
  29.7 0.1 collective-permute-start.10
  29.8 2.7 %collective-permute-start.12 = (bf16[64,1280]{1,0:T(8,128)(2,1)S(1)}, bf16[64,1280]{1,0:T(8,128)(2,1)S(1)}, u32[]{:S(2)}, u32[]{:S(2)}) collective-permute-start(bf16[64,1280]{1,0:T(8,128)(2,1)S(1)} %get-tuple-element.46.refs_1_), channel_id=1, source_target_pairs={{0,2},{1,3},{2,0},{3,1},{4,6},{5,7},{6,4},{7,5},{8,10},{9,11},{10,... | collective-permute-start | bytes 491528 | tf_op jit(solution)/shard_map/ppermute | solution.py:22
  32.4 4.3 %attend.3 = (f32[64,1280]{1,0:T(8,128)S(1)}, bf16[64,1280]{1,0:T(8,128)(2,1)S(1)}) custom-call(s32[3]{0:T(128)S(1)} %pad_add_fusion.place_ref.refs_0_, bf16[64,1280]{1,0:T(8,128)(2,1)S(1)} %get-tuple-element.46.refs_1_, s32[1,64]{1,0:T(1,128)S(1)} %bitcast.10, bf16[2048,1280]{1,0:T(8,128)(2,1)S(1)} %get-tuple-element.41.refs_3_, ...), custom_call_target="tpu_custom_call" | custom-call | tf_op jit(solution)/shard_map/attend/pallas_call | solution.py:112
  36.7 1.6 %collective-permute-start.11 = (bf16[64,1280]{1,0:T(8,128)(2,1)S(1)}, bf16[64,1280]{1,0:T(8,128)(2,1)S(1)}, u32[]{:S(2)}, u32[]{:S(2)}) collective-permute-start(bf16[64,1280]{1,0:T(8,128)(2,1)S(1)} %get-tuple-element.58), channel_id=1, source_target_pairs={{0,1},{1,0},{2,3},{3,2},{4,5},{5,4},{6,7},{7,6},{8,9},{9,8},{10,11... | collective-permute-start | bytes 491528 | tf_op jit(solution)/shard_map/ppermute | solution.py:22
  38.3 0.2 collective-permute-start.13
  38.5 0.0 collective-permute-done.10.sib_ref
  38.6 1.5 %stage.3 = (bf16[5120,768]{1,0:T(8,128)(2,1)S(1)}, f32[8,128]{1,0:T(8,128)S(1)}) custom-call(s32[3]{0:T(128)S(1)} %pad_add_fusion.place_ref.refs_0_, bf16[5120,384]{1,0:T(8,128)(2,1)S(1)} %copy-done.2, bf16[5120,384]{1,0:T(8,128)(2,1)S(1)} %collective-permute-done.10.sib_ref), custom_call_target="tpu_custom_call" | custom-call | tf_op jit(solution)/shard_map/stage/pallas_call | solution.py:178
  40.1 3.1 %copy-done = bf16[5120,768]{1,0:T(8,128)(2,1)} copy-done((bf16[5120,768]{1,0:T(8,128)(2,1)}, bf16[5120,768]{1,0:T(8,128)(2,1)S(1)}, u32[]{:S(2)}) %copy-start) | copy-done | bytes 7864344
  43.2 4.6 %collective-permute-done.11.refs_5_ = bf16[64,1280]{1,0:T(8,128)(2,1)S(1)} collective-permute-done((bf16[64,1280]{1,0:T(8,128)(2,1)S(1)}, bf16[64,1280]{1,0:T(8,128)(2,1)S(1)}, u32[]{:S(2)}, u32[]{:S(2)}) %collective-permute-start.11) | collective-permute-done | bytes 163872 | tf_op jit(solution)/shard_map/ppermute | solution.py:22
  47.8 1.0 %update.1.refs_4_ = bf16[64,1280]{1,0:T(8,128)(2,1)S(1)} custom-call(s32[3]{0:T(128)S(1)} %pad_add_fusion.place_ref.refs_0_, f32[8,128]{1,0:T(8,128)S(1)} %get-tuple-element.55.refs_1_, bf16[128,640]{1,0:T(8,128)(2,1)S(1)} %copy-done.9, bf16[128,640]{1,0:T(8,128)(2,1)} %collective-permute-done.3.refs_3_, f32[64,1280]{1,0:T(8,128)S(1)} %get-tuple-element.57.refs_4_, ...), custom_call_target="tpu_custom_call" | custom-call | tf_op jit(solution)/shard_map/update/pallas_call | solution.py:144
  48.9 0.8 collective-permute-start.19
  49.6 1.5 %collective-permute-start.16 = (bf16[64,1280]{1,0:T(8,128)(2,1)S(1)}, bf16[64,1280]{1,0:T(8,128)(2,1)S(1)}, u32[]{:S(2)}, u32[]{:S(2)}) collective-permute-start(bf16[64,1280]{1,0:T(8,128)(2,1)S(1)} %update.1.refs_4_), channel_id=1, source_target_pairs={{0,16},{4,20},{8,24},{12,28},{16,0},{20,4},{24,8},{28,12},{1,17},{... | collective-permute-start | bytes 491528 | tf_op jit(solution)/shard_map/ppermute | solution.py:22
  51.1 3.3 %collective-permute-start.14 = (bf16[64,1280]{1,0:T(8,128)(2,1)S(1)}, bf16[64,1280]{1,0:T(8,128)(2,1)S(1)}, u32[]{:S(2)}, u32[]{:S(2)}) collective-permute-start(bf16[64,1280]{1,0:T(8,128)(2,1)S(1)} %update.1.refs_4_), channel_id=1, source_target_pairs={{0,2},{1,3},{2,0},{3,1},{4,6},{5,7},{6,4},{7,5},{8,10},{9,11},{10,... | collective-permute-start | bytes 491528 | tf_op jit(solution)/shard_map/ppermute | solution.py:22
  54.4 2.3 %collective-permute-done.19.refs_8_ = bf16[64,1280]{1,0:T(8,128)(2,1)S(1)} collective-permute-done((bf16[64,1280]{1,0:T(8,128)(2,1)S(1)}, bf16[64,1280]{1,0:T(8,128)(2,1)S(1)}, u32[]{:S(2)}, u32[]{:S(2)}) %collective-permute-start.19) | collective-permute-done | bytes 163872 | tf_op jit(solution)/shard_map/ppermute | solution.py:22
  56.8 0.7 collective-permute-start.20
  57.5 1.3 %collective-permute-start.15 = (bf16[64,1280]{1,0:T(8,128)(2,1)S(1)}, bf16[64,1280]{1,0:T(8,128)(2,1)S(1)}, u32[]{:S(2)}, u32[]{:S(2)}) collective-permute-start(bf16[64,1280]{1,0:T(8,128)(2,1)S(1)} %update.1.refs_4_), channel_id=1, source_target_pairs={{0,8},{4,12},{8,0},{12,4},{16,24},{20,28},{24,16},{28,20},{1,9},{5... | collective-permute-start | bytes 491528 | tf_op jit(solution)/shard_map/ppermute | solution.py:22
  58.8 0.0 collective-permute-done.16.refs_6_
  58.8 0.7 collective-permute-start.17
  59.5 2.9 %collective-permute-start.21 = (bf16[64,1280]{1,0:T(8,128)(2,1)S(1)}, bf16[64,1280]{1,0:T(8,128)(2,1)S(1)}, u32[]{:S(2)}, u32[]{:S(2)}) collective-permute-start(bf16[64,1280]{1,0:T(8,128)(2,1)S(1)} %collective-permute-done.19.refs_8_), channel_id=1, source_target_pairs={{0,16},{4,20},{8,24},{12,28},{16,0},{20,4},{24,8},{28,12},{1,17},{... | collective-permute-start | bytes 491528 | tf_op jit(solution)/shard_map/ppermute | solution.py:22
  62.5 1.4 %collective-permute-done.20.refs_9_ = bf16[64,1280]{1,0:T(8,128)(2,1)S(1)} collective-permute-done((bf16[64,1280]{1,0:T(8,128)(2,1)S(1)}, bf16[64,1280]{1,0:T(8,128)(2,1)S(1)}, u32[]{:S(2)}, u32[]{:S(2)}) %collective-permute-start.20) | collective-permute-done | bytes 163872 | tf_op jit(solution)/shard_map/ppermute | solution.py:22
  63.9 3.2 %collective-permute-start.22 = (bf16[64,1280]{1,0:T(8,128)(2,1)S(1)}, bf16[64,1280]{1,0:T(8,128)(2,1)S(1)}, u32[]{:S(2)}, u32[]{:S(2)}) collective-permute-start(bf16[64,1280]{1,0:T(8,128)(2,1)S(1)} %collective-permute-done.20.refs_9_), channel_id=1, source_target_pairs={{0,16},{4,20},{8,24},{12,28},{16,0},{20,4},{24,8},{28,12},{1,17},{... | collective-permute-start | bytes 491528 | tf_op jit(solution)/shard_map/ppermute | solution.py:22
  67.0 0.3 collective-permute-done.17.refs_7_
  67.4 4.1 %collective-permute-start.24 = (bf16[64,1280]{1,0:T(8,128)(2,1)S(1)}, bf16[64,1280]{1,0:T(8,128)(2,1)S(1)}, u32[]{:S(2)}, u32[]{:S(2)}) collective-permute-start(bf16[64,1280]{1,0:T(8,128)(2,1)S(1)} %collective-permute-done.14.refs_4_), channel_id=1, source_target_pairs={{0,16},{4,20},{8,24},{12,28},{16,0},{20,4},{24,8},{28,12},{1,17},{... | collective-permute-start | bytes 491528 | tf_op jit(solution)/shard_map/ppermute | solution.py:22
  71.5 0.0 collective-permute-done.18.refs_8_
  71.5 0.6 collective-permute-start.26
  72.1 1.5 %collective-permute-start.23 = (bf16[64,1280]{1,0:T(8,128)(2,1)S(1)}, bf16[64,1280]{1,0:T(8,128)(2,1)S(1)}, u32[]{:S(2)}, u32[]{:S(2)}) collective-permute-start(bf16[64,1280]{1,0:T(8,128)(2,1)S(1)} %collective-permute-done.14.refs_4_), channel_id=1, source_target_pairs={{0,8},{4,12},{8,0},{12,4},{16,24},{20,28},{24,16},{28,20},{1,9},{5... | collective-permute-start | bytes 491528 | tf_op jit(solution)/shard_map/ppermute | solution.py:22
  73.6 1.5 %collective-permute-start.27 = (bf16[64,1280]{1,0:T(8,128)(2,1)S(1)}, bf16[64,1280]{1,0:T(8,128)(2,1)S(1)}, u32[]{:S(2)}, u32[]{:S(2)}) collective-permute-start(bf16[64,1280]{1,0:T(8,128)(2,1)S(1)} %collective-permute-done.18.refs_8_), channel_id=1, source_target_pairs={{0,16},{4,20},{8,24},{12,28},{16,0},{20,4},{24,8},{28,12},{1,17},{... | collective-permute-start | bytes 491528 | tf_op jit(solution)/shard_map/ppermute | solution.py:22
  75.1 1.5 %collective-permute-done.24.refs_6_ = bf16[64,1280]{1,0:T(8,128)(2,1)S(1)} collective-permute-done((bf16[64,1280]{1,0:T(8,128)(2,1)S(1)}, bf16[64,1280]{1,0:T(8,128)(2,1)S(1)}, u32[]{:S(2)}, u32[]{:S(2)}) %collective-permute-start.24) | collective-permute-done | bytes 163872 | tf_op jit(solution)/shard_map/ppermute | solution.py:22
  76.5 0.5 collective-permute-start.25
  77.1 1.4 %collective-permute-done.26.refs_9_ = bf16[64,1280]{1,0:T(8,128)(2,1)S(1)} collective-permute-done((bf16[64,1280]{1,0:T(8,128)(2,1)S(1)}, bf16[64,1280]{1,0:T(8,128)(2,1)S(1)}, u32[]{:S(2)}, u32[]{:S(2)}) %collective-permute-start.26) | collective-permute-done | bytes 163872 | tf_op jit(solution)/shard_map/ppermute | solution.py:22
  78.5 1.6 %collective-permute-start.28 = (bf16[64,1280]{1,0:T(8,128)(2,1)S(1)}, bf16[64,1280]{1,0:T(8,128)(2,1)S(1)}, u32[]{:S(2)}, u32[]{:S(2)}) collective-permute-start(bf16[64,1280]{1,0:T(8,128)(2,1)S(1)} %collective-permute-done.26.refs_9_), channel_id=1, source_target_pairs={{0,16},{4,20},{8,24},{12,28},{16,0},{20,4},{24,8},{28,12},{1,17},{... | collective-permute-start | bytes 491528 | tf_op jit(solution)/shard_map/ppermute | solution.py:22
  80.0 3.2 %copy-done.1 = bf16[5120,768]{1,0:T(8,128)(2,1)S(1)} copy-done((bf16[5120,768]{1,0:T(8,128)(2,1)S(1)}, bf16[5120,768]{1,0:T(8,128)(2,1)}, u32[]{:S(2)}) %copy-start.1) | copy-done | bytes 7864344
  83.3 2.3 %score.2 = f32[32,8,128]{2,1,0:T(8,128)S(1)} custom-call(s32[3]{0:T(128)S(1)} %pad_add_fusion.place_ref.refs_0_, s32[1,512]{1,0:T(1,128)S(1)} %bitcast.7, f32[8,640]{1,0:T(8,128)S(1)} %reshape.13.refs_2_, bf16[5120,768]{1,0:T(8,128)(2,1)S(1)} %copy-done.1, bf16[64,1280]{1,0:T(8,128)(2,1)S(1)} %update.1.refs_4_, ...), custom_call_target="tpu_custom_call" | custom-call | tf_op jit(solution)/shard_map/score/pallas_call | solution.py:239
  85.6 0.0 collective-permute-done.27.refs_10_
  85.6 0.0 collective-permute-done.28.refs_11_
  85.6 2.3 %score.3 = f32[32,8,128]{2,1,0:T(8,128)S(1)} custom-call(s32[3]{0:T(128)S(1)} %pad_add_fusion.place_ref.refs_0_, s32[1,512]{1,0:T(1,128)S(1)} %bitcast.8, f32[8,640]{1,0:T(8,128)S(1)} %reshape.13.refs_2_, bf16[5120,768]{1,0:T(8,128)(2,1)S(1)} %copy-done.1, bf16[64,1280]{1,0:T(8,128)(2,1)S(1)} %collective-permute-done.14.refs_4_, ...), custom_call_target="tpu_custom_call" | custom-call | tf_op jit(solution)/shard_map/score/pallas_call | solution.py:239
  87.9 10.7 %all_to_all.5.refs_2_ = f32[32,8,128]{2,1,0:T(8,128)S(1)} all-to-all(f32[32,8,128]{2,1,0:T(8,128)S(1)} %add.3), channel_id=1, replica_groups=mesh['ctx'=8,'tp'=4] {'ctx','tp'}, dimensions={0} | all-to-all | bytes 262144 | tf_op jit(solution)/shard_map/all_to_all | solution.py:341
  98.6 1.1 %merge.1 = (f32[1,64]{1,0:T(1,128)}, f32[1,64]{1,0:T(1,128)}) custom-call(s32[3]{0:T(128)S(1)} %pad_add_fusion.place_ref.refs_0_, f32[1,64]{1,0:T(1,128)S(1)} %bitcast.11, f32[32,8,128]{2,1,0:T(8,128)S(1)} %all_to_all.5.refs_2_), custom_call_target="tpu_custom_call" | custom-call | tf_op jit(solution)/shard_map/merge/pallas_call | solution.py:272
  (41 shorter events, 0.2 us)
Async XLA Ops:
  0.6 24.9 %copy-start.4 = (bf16[64,2048]{1,0:T(8,128)(2,1)S(1)}, bf16[64,2048]{1,0:T(8,128)(2,1)}, u32[]{:S(2)}) copy-start(bf16[64,2048]{1,0:T(8,128)(2,1)} %refs_4_.3) | copy-start | bytes 786436
  0.6 24.9 %copy-start.11 = (s32[64]{0:T(128)S(1)}, s32[64]{0:T(128)}, u32[]{:S(2)}) copy-start(s32[64]{0:T(128)} %param.20) | copy-start | bytes 772
  0.7 1.6 %collective-permute-start = (bf16[64,256]{1,0:T(8,128)(2,1)}, bf16[64,256]{1,0:T(8,128)(2,1)S(1)}, u32[]{:S(2)}, u32[]{:S(2)}) collective-permute-start(bf16[64,256]{1,0:T(8,128)(2,1)} %param.12), channel_id=1, source_target_pairs={{0,4},{4,0},{8,12},{12,8},{16,20},{20,16},{24,28},{28,24},{1,5},{5... | collective-permute-start | bytes 98312 | tf_op jit(solution)/shard_map/ppermute | solution.py:22
  1.2 1.4 %collective-permute-start.1 = (bf16[64,256]{1,0:T(8,128)(2,1)}, bf16[64,256]{1,0:T(8,128)(2,1)S(1)}, u32[]{:S(2)}, u32[]{:S(2)}) collective-permute-start(bf16[64,256]{1,0:T(8,128)(2,1)} %param.13), channel_id=1, source_target_pairs={{0,4},{4,0},{8,12},{12,8},{16,20},{20,16},{24,28},{28,24},{1,5},{5... | collective-permute-start | bytes 98312 | tf_op jit(solution)/shard_map/ppermute | solution.py:22
  3.4 18.2 %collective-permute-start.2 = (bf16[2048,640]{1,0:T(8,128)(2,1)}, bf16[2048,640]{1,0:T(8,128)(2,1)S(1)}, u32[]{:S(2)}, u32[]{:S(2)}) collective-permute-start(bf16[2048,640]{1,0:T(8,128)(2,1)} %own_ref), channel_id=1, source_target_pairs={{0,4},{4,0},{8,12},{12,8},{16,20},{20,16},{24,28},{28,24},{1,5},{5... | collective-permute-start | bytes 7864328 | tf_op jit(solution)/shard_map/ppermute | solution.py:22
  3.6 12.6 %collective-permute-start.6 = (bf16[64,2048]{1,0:T(8,128)(2,1)}, bf16[64,2048]{1,0:T(8,128)(2,1)S(1)}, u32[]{:S(2)}, u32[]{:S(2)}) collective-permute-start(bf16[64,2048]{1,0:T(8,128)(2,1)} %refs_4_.3), channel_id=1, source_target_pairs={{0,16},{4,20},{8,24},{12,28},{16,0},{20,4},{24,8},{28,12},{1,17},{... | collective-permute-start | bytes 786440 | tf_op jit(solution)/shard_map/ppermute | solution.py:22
  6.5 9.6 %collective-permute-start.7 = (bf16[64,1024]{1,0:T(8,128)(2,1)S(1)}, bf16[64,1024]{1,0:T(8,128)(2,1)S(1)}, u32[]{:S(2)}, u32[]{:S(2)}) collective-permute-start(bf16[64,1024]{1,0:T(8,128)(2,1)S(1)} %pad_maximum_fusion.2.refs_5_), channel_id=1, source_target_pairs={{0,16},{4,20},{8,24},{12,28},{16,0},{20,4},{24,8},{28,12},{1,17},{... | collective-permute-start | bytes 393224 | tf_op jit(solution)/shard_map/ppermute | solution.py:22
  6.5 9.6 %collective-permute-start.5 = (bf16[64,1024]{1,0:T(8,128)(2,1)S(1)}, bf16[64,1024]{1,0:T(8,128)(2,1)S(1)}, u32[]{:S(2)}, u32[]{:S(2)}) collective-permute-start(bf16[64,1024]{1,0:T(8,128)(2,1)S(1)} %pad_maximum_fusion.2.refs_5_), channel_id=1, source_target_pairs={{0,8},{4,12},{8,0},{12,4},{16,24},{20,28},{24,16},{28,20},{1,9},{5... | collective-permute-start | bytes 393224 | tf_op jit(solution)/shard_map/ppermute | solution.py:22
  8.5 10.1 %collective-permute-start.4 = (bf16[64,2048]{1,0:T(8,128)(2,1)}, bf16[64,2048]{1,0:T(8,128)(2,1)S(1)}, u32[]{:S(2)}, u32[]{:S(2)}) collective-permute-start(bf16[64,2048]{1,0:T(8,128)(2,1)} %refs_4_.3), channel_id=1, source_target_pairs={{0,8},{4,12},{8,0},{12,4},{16,24},{20,28},{24,16},{28,20},{1,9},{5... | collective-permute-start | bytes 786440 | tf_op jit(solution)/shard_map/ppermute | solution.py:22
  16.1 2.5 %copy-start.5 = (bf16[64,1024]{1,0:T(8,128)(2,1)}, bf16[64,1024]{1,0:T(8,128)(2,1)S(1)}, u32[]{:S(2)}) copy-start(bf16[64,1024]{1,0:T(8,128)(2,1)S(1)} %collective-permute-done.7.refs_9_) | copy-start | bytes 393220
  16.1 2.5 %copy-start.7 = (bf16[64,1024]{1,0:T(8,128)(2,1)}, bf16[64,1024]{1,0:T(8,128)(2,1)S(1)}, u32[]{:S(2)}) copy-start(bf16[64,1024]{1,0:T(8,128)(2,1)S(1)} %collective-permute-done.5.refs_7_) | copy-start | bytes 393220
  16.9 7.5 %collective-permute-start.8 = (bf16[64,1536]{1,0:T(8,128)(2,1)}, bf16[64,1536]{1,0:T(8,128)(2,1)}, u32[]{:S(2)}, u32[]{:S(2)}) collective-permute-start(bf16[64,1536]{1,0:T(8,128)(2,1)} %pad_maximum_fusion), channel_id=1, source_target_pairs={{0,8},{4,12},{8,0},{12,4},{16,24},{20,28},{24,16},{28,20},{1,9},{5... | collective-permute-start | bytes 589832 | tf_op jit(solution)/shard_map/ppermute | solution.py:22
  19.3 6.2 %collective-permute-start.9 = (bf16[64,1536]{1,0:T(8,128)(2,1)}, bf16[64,1536]{1,0:T(8,128)(2,1)}, u32[]{:S(2)}, u32[]{:S(2)}) collective-permute-start(bf16[64,1536]{1,0:T(8,128)(2,1)} %pad_maximum_fusion.1), channel_id=1, source_target_pairs={{0,16},{4,20},{8,24},{12,28},{16,0},{20,4},{24,8},{28,12},{1,17},{... | collective-permute-start | bytes 589832 | tf_op jit(solution)/shard_map/ppermute | solution.py:22
  20.9 3.5 %collective-permute-start.3 = (bf16[128,640]{1,0:T(8,128)(2,1)}, bf16[128,640]{1,0:T(8,128)(2,1)}, u32[]{:S(2)}, u32[]{:S(2)}) collective-permute-start(bf16[128,640]{1,0:T(8,128)(2,1)} %refs_2_), channel_id=1, source_target_pairs={{0,4},{4,0},{8,12},{12,8},{16,20},{20,16},{24,28},{28,24},{1,5},{5... | collective-permute-start | bytes 491528 | tf_op jit(solution)/shard_map/ppermute | solution.py:22
  21.6 1.7 %copy-start.3 = (bf16[2048,640]{1,0:T(8,128)(2,1)S(1)}, bf16[2048,640]{1,0:T(8,128)(2,1)}, u32[]{:S(2)}) copy-start(bf16[2048,640]{1,0:T(8,128)(2,1)} %own_ref) | copy-start | bytes 7864324
  23.3 2.2 %copy-start.6 = (bf16[64,1024]{1,0:T(8,128)(2,1)S(1)}, bf16[64,1024]{1,0:T(8,128)(2,1)}, u32[]{:S(2)}) copy-start(bf16[64,1024]{1,0:T(8,128)(2,1)} %copy-done.5) | copy-start | bytes 393220
  23.3 2.2 %copy-start.8 = (bf16[64,1024]{1,0:T(8,128)(2,1)S(1)}, bf16[64,1024]{1,0:T(8,128)(2,1)}, u32[]{:S(2)}) copy-start(bf16[64,1024]{1,0:T(8,128)(2,1)} %copy-done.7) | copy-start | bytes 393220
  24.4 5.3 %copy-start.2 = (bf16[5120,384]{1,0:T(8,128)(2,1)S(1)}, bf16[5120,384]{1,0:T(8,128)(2,1)}, u32[]{:S(2)}) copy-start(bf16[5120,384]{1,0:T(8,128)(2,1)} %own_ref.1) | copy-start | bytes 11796484
  29.7 8.9 %collective-permute-start.10 = (bf16[5120,384]{1,0:T(8,128)(2,1)S(1)}, bf16[5120,384]{1,0:T(8,128)(2,1)S(1)}, u32[]{:S(2)}, u32[]{:S(2)}) collective-permute-start(bf16[5120,384]{1,0:T(8,128)(2,1)S(1)} %copy-done.2), channel_id=1, source_target_pairs={{0,4},{4,0},{8,12},{12,8},{16,20},{20,16},{24,28},{28,24},{1,5},{5... | collective-permute-start | bytes 11796488 | tf_op jit(solution)/shard_map/ppermute | solution.py:22
  29.8 18.1 %collective-permute-start.12 = (bf16[64,1280]{1,0:T(8,128)(2,1)S(1)}, bf16[64,1280]{1,0:T(8,128)(2,1)S(1)}, u32[]{:S(2)}, u32[]{:S(2)}) collective-permute-start(bf16[64,1280]{1,0:T(8,128)(2,1)S(1)} %get-tuple-element.46.refs_1_), channel_id=1, source_target_pairs={{0,2},{1,3},{2,0},{3,1},{4,6},{5,7},{6,4},{7,5},{8,10},{9,11},{10,... | collective-permute-start | bytes 491528 | tf_op jit(solution)/shard_map/ppermute | solution.py:22
  36.7 11.1 %collective-permute-start.11 = (bf16[64,1280]{1,0:T(8,128)(2,1)S(1)}, bf16[64,1280]{1,0:T(8,128)(2,1)S(1)}, u32[]{:S(2)}, u32[]{:S(2)}) collective-permute-start(bf16[64,1280]{1,0:T(8,128)(2,1)S(1)} %get-tuple-element.58), channel_id=1, source_target_pairs={{0,1},{1,0},{2,3},{3,2},{4,5},{5,4},{6,7},{7,6},{8,9},{9,8},{10,11... | collective-permute-start | bytes 491528 | tf_op jit(solution)/shard_map/ppermute | solution.py:22
  38.3 9.5 %collective-permute-start.13 = (bf16[64,1280]{1,0:T(8,128)(2,1)S(1)}, bf16[64,1280]{1,0:T(8,128)(2,1)S(1)}, u32[]{:S(2)}, u32[]{:S(2)}) collective-permute-start(bf16[64,1280]{1,0:T(8,128)(2,1)S(1)} %get-tuple-element.59), channel_id=1, source_target_pairs={{0,3},{1,2},{2,1},{3,0},{4,7},{5,6},{6,5},{7,4},{8,11},{9,10},{10,... | collective-permute-start | bytes 491528 | tf_op jit(solution)/shard_map/ppermute | solution.py:22
  38.5 4.6 %copy-start.13 = (bf16[5120]{0:T(1024)(128)(2,1)S(1)}, bf16[5120]{0:T(1024)(128)(2,1)}, u32[]{:S(2)}) copy-start(bf16[5120]{0:T(1024)(128)(2,1)} %param.16) | copy-start | bytes 30724
  38.6 9.3 %copy-start.9 = (bf16[128,640]{1,0:T(8,128)(2,1)S(1)}, bf16[128,640]{1,0:T(8,128)(2,1)}, u32[]{:S(2)}) copy-start(bf16[128,640]{1,0:T(8,128)(2,1)} %refs_2_) | copy-start | bytes 491524
  38.6 41.5 %copy-start.10 = (s32[512]{0:T(512)S(1)}, s32[512]{0:T(512)}, u32[]{:S(2)}) copy-start(s32[512]{0:T(512)} %param.18) | copy-start | bytes 6148
  40.1 3.1 %copy-start = (bf16[5120,768]{1,0:T(8,128)(2,1)}, bf16[5120,768]{1,0:T(8,128)(2,1)S(1)}, u32[]{:S(2)}) copy-start(bf16[5120,768]{1,0:T(8,128)(2,1)S(1)} %get-tuple-element.54.refs_3_) | copy-start | bytes 23592964
  48.9 7.9 %collective-permute-start.19 = (bf16[64,1280]{1,0:T(8,128)(2,1)S(1)}, bf16[64,1280]{1,0:T(8,128)(2,1)S(1)}, u32[]{:S(2)}, u32[]{:S(2)}) collective-permute-start(bf16[64,1280]{1,0:T(8,128)(2,1)S(1)} %update.1.refs_4_), channel_id=1, source_target_pairs={{0,1},{1,0},{2,3},{3,2},{4,5},{5,4},{6,7},{7,6},{8,9},{9,8},{10,11... | collective-permute-start | bytes 491528 | tf_op jit(solution)/shard_map/ppermute | solution.py:22
  49.6 9.2 %collective-permute-start.16 = (bf16[64,1280]{1,0:T(8,128)(2,1)S(1)}, bf16[64,1280]{1,0:T(8,128)(2,1)S(1)}, u32[]{:S(2)}, u32[]{:S(2)}) collective-permute-start(bf16[64,1280]{1,0:T(8,128)(2,1)S(1)} %update.1.refs_4_), channel_id=1, source_target_pairs={{0,16},{4,20},{8,24},{12,28},{16,0},{20,4},{24,8},{28,12},{1,17},{... | collective-permute-start | bytes 491528 | tf_op jit(solution)/shard_map/ppermute | solution.py:22
  51.1 11.4 %collective-permute-start.14 = (bf16[64,1280]{1,0:T(8,128)(2,1)S(1)}, bf16[64,1280]{1,0:T(8,128)(2,1)S(1)}, u32[]{:S(2)}, u32[]{:S(2)}) collective-permute-start(bf16[64,1280]{1,0:T(8,128)(2,1)S(1)} %update.1.refs_4_), channel_id=1, source_target_pairs={{0,2},{1,3},{2,0},{3,1},{4,6},{5,7},{6,4},{7,5},{8,10},{9,11},{10,... | collective-permute-start | bytes 491528 | tf_op jit(solution)/shard_map/ppermute | solution.py:22
  56.8 7.1 %collective-permute-start.20 = (bf16[64,1280]{1,0:T(8,128)(2,1)S(1)}, bf16[64,1280]{1,0:T(8,128)(2,1)S(1)}, u32[]{:S(2)}, u32[]{:S(2)}) collective-permute-start(bf16[64,1280]{1,0:T(8,128)(2,1)S(1)} %collective-permute-done.19.refs_8_), channel_id=1, source_target_pairs={{0,8},{4,12},{8,0},{12,4},{16,24},{20,28},{24,16},{28,20},{1,9},{5... | collective-permute-start | bytes 491528 | tf_op jit(solution)/shard_map/ppermute | solution.py:22
  57.5 9.5 %collective-permute-start.15 = (bf16[64,1280]{1,0:T(8,128)(2,1)S(1)}, bf16[64,1280]{1,0:T(8,128)(2,1)S(1)}, u32[]{:S(2)}, u32[]{:S(2)}) collective-permute-start(bf16[64,1280]{1,0:T(8,128)(2,1)S(1)} %update.1.refs_4_), channel_id=1, source_target_pairs={{0,8},{4,12},{8,0},{12,4},{16,24},{20,28},{24,16},{28,20},{1,9},{5... | collective-permute-start | bytes 491528 | tf_op jit(solution)/shard_map/ppermute | solution.py:22
  58.8 8.6 %collective-permute-start.17 = (bf16[64,1280]{1,0:T(8,128)(2,1)S(1)}, bf16[64,1280]{1,0:T(8,128)(2,1)S(1)}, u32[]{:S(2)}, u32[]{:S(2)}) collective-permute-start(bf16[64,1280]{1,0:T(8,128)(2,1)S(1)} %collective-permute-done.16.refs_6_), channel_id=1, source_target_pairs={{0,8},{4,12},{8,0},{12,4},{16,24},{20,28},{24,16},{28,20},{1,9},{5... | collective-permute-start | bytes 491528 | tf_op jit(solution)/shard_map/ppermute | solution.py:22
  59.5 12.0 %collective-permute-start.21 = (bf16[64,1280]{1,0:T(8,128)(2,1)S(1)}, bf16[64,1280]{1,0:T(8,128)(2,1)S(1)}, u32[]{:S(2)}, u32[]{:S(2)}) collective-permute-start(bf16[64,1280]{1,0:T(8,128)(2,1)S(1)} %collective-permute-done.19.refs_8_), channel_id=1, source_target_pairs={{0,16},{4,20},{8,24},{12,28},{16,0},{20,4},{24,8},{28,12},{1,17},{... | collective-permute-start | bytes 491528 | tf_op jit(solution)/shard_map/ppermute | solution.py:22
  62.5 9.0 %collective-permute-start.18 = (bf16[64,1280]{1,0:T(8,128)(2,1)S(1)}, bf16[64,1280]{1,0:T(8,128)(2,1)S(1)}, u32[]{:S(2)}, u32[]{:S(2)}) collective-permute-start(bf16[64,1280]{1,0:T(8,128)(2,1)S(1)} %collective-permute-done.14.refs_4_), channel_id=1, source_target_pairs={{0,1},{1,0},{2,3},{3,2},{4,5},{5,4},{6,7},{7,6},{8,9},{9,8},{10,11... | collective-permute-start | bytes 491528 | tf_op jit(solution)/shard_map/ppermute | solution.py:22
  63.9 7.6 %collective-permute-start.22 = (bf16[64,1280]{1,0:T(8,128)(2,1)S(1)}, bf16[64,1280]{1,0:T(8,128)(2,1)S(1)}, u32[]{:S(2)}, u32[]{:S(2)}) collective-permute-start(bf16[64,1280]{1,0:T(8,128)(2,1)S(1)} %collective-permute-done.20.refs_9_), channel_id=1, source_target_pairs={{0,16},{4,20},{8,24},{12,28},{16,0},{20,4},{24,8},{28,12},{1,17},{... | collective-permute-start | bytes 491528 | tf_op jit(solution)/shard_map/ppermute | solution.py:22
  67.4 9.2 %collective-permute-start.24 = (bf16[64,1280]{1,0:T(8,128)(2,1)S(1)}, bf16[64,1280]{1,0:T(8,128)(2,1)S(1)}, u32[]{:S(2)}, u32[]{:S(2)}) collective-permute-start(bf16[64,1280]{1,0:T(8,128)(2,1)S(1)} %collective-permute-done.14.refs_4_), channel_id=1, source_target_pairs={{0,16},{4,20},{8,24},{12,28},{16,0},{20,4},{24,8},{28,12},{1,17},{... | collective-permute-start | bytes 491528 | tf_op jit(solution)/shard_map/ppermute | solution.py:22
  71.5 6.9 %collective-permute-start.26 = (bf16[64,1280]{1,0:T(8,128)(2,1)S(1)}, bf16[64,1280]{1,0:T(8,128)(2,1)S(1)}, u32[]{:S(2)}, u32[]{:S(2)}) collective-permute-start(bf16[64,1280]{1,0:T(8,128)(2,1)S(1)} %collective-permute-done.18.refs_8_), channel_id=1, source_target_pairs={{0,8},{4,12},{8,0},{12,4},{16,24},{20,28},{24,16},{28,20},{1,9},{5... | collective-permute-start | bytes 491528 | tf_op jit(solution)/shard_map/ppermute | solution.py:22
  72.1 13.4 %collective-permute-start.23 = (bf16[64,1280]{1,0:T(8,128)(2,1)S(1)}, bf16[64,1280]{1,0:T(8,128)(2,1)S(1)}, u32[]{:S(2)}, u32[]{:S(2)}) collective-permute-start(bf16[64,1280]{1,0:T(8,128)(2,1)S(1)} %collective-permute-done.14.refs_4_), channel_id=1, source_target_pairs={{0,8},{4,12},{8,0},{12,4},{16,24},{20,28},{24,16},{28,20},{1,9},{5... | collective-permute-start | bytes 491528 | tf_op jit(solution)/shard_map/ppermute | solution.py:22
  73.6 12.0 %collective-permute-start.27 = (bf16[64,1280]{1,0:T(8,128)(2,1)S(1)}, bf16[64,1280]{1,0:T(8,128)(2,1)S(1)}, u32[]{:S(2)}, u32[]{:S(2)}) collective-permute-start(bf16[64,1280]{1,0:T(8,128)(2,1)S(1)} %collective-permute-done.18.refs_8_), channel_id=1, source_target_pairs={{0,16},{4,20},{8,24},{12,28},{16,0},{20,4},{24,8},{28,12},{1,17},{... | collective-permute-start | bytes 491528 | tf_op jit(solution)/shard_map/ppermute | solution.py:22
  76.5 9.0 %collective-permute-start.25 = (bf16[64,1280]{1,0:T(8,128)(2,1)S(1)}, bf16[64,1280]{1,0:T(8,128)(2,1)S(1)}, u32[]{:S(2)}, u32[]{:S(2)}) collective-permute-start(bf16[64,1280]{1,0:T(8,128)(2,1)S(1)} %collective-permute-done.24.refs_6_), channel_id=1, source_target_pairs={{0,8},{4,12},{8,0},{12,4},{16,24},{20,28},{24,16},{28,20},{1,9},{5... | collective-permute-start | bytes 491528 | tf_op jit(solution)/shard_map/ppermute | solution.py:22
  78.5 7.1 %collective-permute-start.28 = (bf16[64,1280]{1,0:T(8,128)(2,1)S(1)}, bf16[64,1280]{1,0:T(8,128)(2,1)S(1)}, u32[]{:S(2)}, u32[]{:S(2)}) collective-permute-start(bf16[64,1280]{1,0:T(8,128)(2,1)S(1)} %collective-permute-done.26.refs_9_), channel_id=1, source_target_pairs={{0,16},{4,20},{8,24},{12,28},{16,0},{20,4},{24,8},{28,12},{1,17},{... | collective-permute-start | bytes 491528 | tf_op jit(solution)/shard_map/ppermute | solution.py:22
  80.0 3.2 %copy-start.1 = (bf16[5120,768]{1,0:T(8,128)(2,1)S(1)}, bf16[5120,768]{1,0:T(8,128)(2,1)}, u32[]{:S(2)}) copy-start(bf16[5120,768]{1,0:T(8,128)(2,1)} %copy-done) | copy-start | bytes 23592964
  85.5 13.1 %copy-start.12 = (f32[64]{0:T(128)S(1)}, f32[64]{0:T(128)}, u32[]{:S(2)}) copy-start(f32[64]{0:T(128)} %param.19) | copy-start | bytes 772

commit v3 on v2

--- a/solution.py
+++ b/solution.py
@@ -34,10 +34,9 @@
     return [*found, swap(found[2 - turn], "ctx", 2 + 2 * turn)]
 
 
-def attend_kernel(counts, tp_count, own_rows, kv_width, ks, blocks, place_ref, after_ref, lens_ref, weight_ref, *refs):
-    chips, total = len(counts), sum(counts)
-    outs = refs[total : total + len(ks)]
-    queries, keys, values, mixed = refs[total + len(ks) :]
+def attend_kernel(chips, tp_count, own_rows, kv_width, ks, blocks, place_ref, after_ref, lens_ref, weight_ref, *refs):
+    outs = refs[2 * chips : 2 * chips + len(ks)]
+    queries, keys, values, mixed = refs[2 * chips + len(ks) :]
     ctx, tp, slab_start = place_ref[0], place_ref[1], place_ref[2]
     kv_heads = kv_width // HD
     depth = queries.shape[1]
@@ -45,27 +44,17 @@
     length = keys.shape[0]
     owners = [(tp ^ k) * blocks + 2 * b + lax.rem(ctx, 2) for k in ks for b in range(blocks // 2)]
     for j in range(chips):
-        parts = refs[sum(counts[:j]) : sum(counts[: j + 1])]
-        if parts[0].shape[1] == depth:
-            spans = [(parts[0], 0, 0, depth)]
-            own, sib, start = parts[1], parts[1], 2 * kv_width
-            at = 0
-        else:
-            half = depth // 2
-            spans = [(parts[0], 0, 0, half), (parts[1], 0, half, half)]
-            own, sib, start = parts[0], parts[1], half
-            at = half
+        asked, kv = refs[2 * j], refs[2 * j + 1]
         own_at = pl.ds(pl.multiple_of((ctx ^ (2 * j)) * own_rows, own_rows), own_rows)
         sib_at = pl.ds(pl.multiple_of((ctx ^ (2 * j + 1)) * own_rows, own_rows), own_rows)
-        for rows, part, first in ((own_at, own, at), (sib_at, sib, start)):
-            keys[rows, :] = part[:, first : first + kv_width]
-            values[rows, :] = part[:, first + kv_width : first + 2 * kv_width]
+        for rows, first in ((own_at, 0), (sib_at, 2 * kv_width)):
+            keys[rows, :] = kv[:, first : first + kv_width]
+            values[rows, :] = kv[:, first + kv_width : first + 2 * kv_width]
         for i, owner in enumerate(owners):
 
             @pl.when(owner == (ctx ^ (2 * j)))
-            def _(spans=spans, i=i):
-                for part, first, target, width in spans:
-                    queries[i * own_rows : (i + 1) * own_rows, target : target + width] = part[:, first : first + width]
+            def _(asked=asked, i=i):
+                queries[i * own_rows : (i + 1) * own_rows, :] = asked[...]
 
     count = lens_ref.shape[1]
     first = lax.broadcasted_iota(jnp.int32, (count, count), 0)
@@ -110,9 +99,9 @@
     rows = len(ks) * span
     need = 2 * depth * width + chips * own_rows * depth * 2 + rows * (depth * 4 + width * 16) + 24 * 8 * own_rows * length
     return pl.pallas_call(
-        lambda *refs: attend_kernel([len(one) for one in sets], tp_count, own_rows, kv_width, ks, blocks, *refs),
+        lambda *refs: attend_kernel(chips, tp_count, own_rows, kv_width, ks, blocks, *refs),
         out_shape=[jax.ShapeDtypeStruct((span, width), F32 if k == 0 else BF16) for k in ks],
-        in_specs=[SMEM, ANY] + [VMEM] * (2 + sum(len(one) for one in sets)),
+        in_specs=[SMEM, ANY] + [VMEM] * (2 + 2 * chips),
         out_specs=[VMEM] * len(ks),
         scratch_shapes=[
             pltpu.VMEM((rows, depth), BF16),
@@ -126,7 +115,8 @@
 
 
 def update_kernel(blocks, own_rows, place_ref, after_ref, stream_ref, stream_sib_ref, *refs):
-    sums, out_ref = refs[:-1], refs[-1]
+    sums, out_ref, mark_ref = refs[:-2], refs[-2], refs[-1]
+    mark_ref[...] = jnp.zeros(mark_ref.shape, F32)
     core = lax.rem(place_ref[0], 2)
     width = stream_ref.shape[1]
     for b in range(blocks // 2):
@@ -143,9 +133,9 @@
 def update(place, after, stream, stream_sib, sums, blocks, own_rows):
     return pl.pallas_call(
         lambda *refs: update_kernel(blocks, own_rows, *refs),
-        out_shape=jax.ShapeDtypeStruct(sums[0].shape, BF16),
+        out_shape=[jax.ShapeDtypeStruct(sums[0].shape, BF16), jax.ShapeDtypeStruct((8, 128), F32)],
         in_specs=[SMEM, ANY] + [VMEM] * (2 + len(sums)),
-        out_specs=VMEM,
+        out_specs=[VMEM, VMEM],
         compiler_params=pltpu.CompilerParams(vmem_limit_bytes=6 << 20),
         name="update",
     )(place, after, stream, stream_sib, *sums)
@@ -186,7 +176,7 @@
     )(place, own, sib)
 
 
-def score_kernel(chips, tp_count, own_rows, blocks, first, place_ref, tokens_ref, gain_ref, head_ref, *refs):
+def score_kernel(chips, tp_count, own_rows, blocks, first, place_ref, after_ref, ready_ref, tokens_ref, gain_ref, head_ref, *refs):
     pieces, out_ref, normed = refs[:-2], refs[-2], refs[-1]
     spans = len(pieces) // chips
     ctx, tp = place_ref[0], place_ref[1]
@@ -231,7 +221,7 @@
             out_ref[pl.ds(owner * tp_count + k, 1), :, :own_rows] = tile[None]
 
 
-def score(place, tokens, gain, head, spans, first, tp_count, own_rows, blocks):
+def score(place, after, ready, tokens, gain, head, spans, first, tp_count, own_rows, blocks):
     chips = len(spans[0])
     rows = len(spans) * spans[0][0].shape[0]
     depth, vocab = head.shape
@@ -239,12 +229,12 @@
     return pl.pallas_call(
         lambda *refs: score_kernel(chips, tp_count, own_rows, blocks, first, *refs),
         out_shape=jax.ShapeDtypeStruct((2 * chips * tp_count, 8, 128), F32),
-        in_specs=[SMEM] + [VMEM] * (3 + len(spans) * chips),
+        in_specs=[SMEM, ANY, ANY] + [VMEM] * (3 + len(spans) * chips),
         out_specs=VMEM,
         scratch_shapes=[pltpu.VMEM((rows, depth), BF16)],
         compiler_params=pltpu.CompilerParams(vmem_limit_bytes=need + (12 << 20)),
         name="score",
-    )(place, tokens, gain, head, *[piece for span in spans for piece in span])
+    )(place, after, ready, tokens, gain, head, *[piece for span in spans for piece in span])
 
 
 def merge_kernel(chips, tp_count, place_ref, policy_ref, stats_ref, logprob_ref, penalty_ref):
@@ -300,19 +290,16 @@
     mid = tp_count // 2
     place = jnp.stack([ctx, tp, slab_start[0]]).astype(jnp.int32)
 
+    asked = sides(queries, chips)
     kv = [key_rows, value_rows, swap(key_rows, "ctx", 1), swap(value_rows, "ctx", 1)]
     kv = jnp.concatenate(kv, axis=1)
     kv, out_weight, stream = lax.optimization_barrier((kv, out_weight, stream))
-    sets = list(zip(sides(queries, chips), sides(kv, chips)))
-    if len(sets) < chips:
-        half, inner = queries.shape[1] // 2, kv.shape[1] // 2
-        below = jnp.concatenate([sets[2][0][:, :half], sets[2][1][:, :inner]], axis=1)
-        above = jnp.concatenate([sets[1][0][:, half:], sets[1][1][:, inner:]], axis=1)
-        sets.append((swap(below, "ctx", 2), swap(above, "ctx", 4)))
-    out_sibling = swap(out_weight, "ctx", 1)
-    stream_sibling = swap(stream, "ctx", 1)
+    out_sibling, stream_sibling = swap(out_weight, "ctx", 1), swap(stream, "ctx", 1)
     weight, mark = stage(place, out_weight, out_sibling, 1)
+    later, mark = lax.optimization_barrier((kv, mark))
+    around = [kv] + [swap(kv if j < 2 else later, "ctx", 2 * j) for j in range(1, 3 if chips == 4 else chips)]
     mark, stream_sibling = lax.optimization_barrier((mark, stream_sibling))
+    sets = list(zip(corners(asked, 0), corners(around, 1)))
 
     lens, kv_width = doc_lengths[None], key_rows.shape[1]
     far = attend(place, mark, lens, sets, kv_width, weight, range(mid, tp_count), tp_count, blocks)
@@ -321,22 +308,23 @@
     near = attend(place, far[0], lens, sets, kv_width, weight, range(mid), tp_count, blocks)
     sums = [*near, *far]
     received = [swap(sums[k], "tp", k) for k in range(1, tp_count)]
-    head_sibling, gain, tokens, sums[0] = lax.optimization_barrier((head_sibling, final_gain, token_ids, sums[0]))
-    head, mark = stage(place, head_weight, head_sibling, ctx_count)
+    gain, tokens, sums[0] = lax.optimization_barrier((final_gain, token_ids, sums[0]))
     gain, tokens = gain.astype(F32).reshape(ctx_count, -1), tokens[None]
-    mark, gain, tokens = lax.optimization_barrier((mark, gain, tokens))
-    updated = update(place, mark, stream, stream_sibling, [sums[0]] + received, blocks, own_rows)
+    sums[0], gain, tokens, head_sibling = lax.optimization_barrier((sums[0], gain, tokens, head_sibling))
+    updated, mark = update(place, sums[0], stream, stream_sibling, [sums[0]] + received, blocks, own_rows)
+    here, mark, head_sibling = lax.optimization_barrier((updated, swap(mark, "ctx", 1), head_sibling))
+    head, ready = stage(place, head_weight, head_sibling, ctx_count)
     pieces, spans = [updated], []
     for k in range(1, tp_count):
         step = k & -k
+        if step < k:
+            pieces[k - step], ready = lax.optimization_barrier((pieces[k - step], ready))
         pieces.append(swap(pieces[k - step], "tp", step))
-    for k, piece in enumerate(pieces):
-        if k >= 2:
-            piece, spans[k - 2] = lax.optimization_barrier((piece, spans[k - 2]))
-        found = sides(piece, chips)
-        spans.append(corners(found, k % 2))
-    stats = score(place, tokens, gain, head, spans[:mid], 0, tp_count, own_rows, blocks) + score(
-        place, tokens, gain, head, spans[mid:], mid, tp_count, own_rows, blocks
+    for k, piece in enumerate([here] + pieces[1:]):
+        spans.append(sides(piece, chips))
+    spans = [corners(span, k % 2) for k, span in enumerate(spans)]
+    stats = score(place, mark, ready, tokens, gain, head, spans[:mid], 0, tp_count, own_rows, blocks) + score(
+        place, mark, ready, tokens, gain, head, spans[mid:], mid, tp_count, own_rows, blocks
     )
     stats = lax.all_to_all(stats, ("ctx", "tp"), 0, 0, tiled=True)
     logprob, penalty = merge(place, policy_logprob[None], stats, chips, tp_count)

time: 100 us -> 95.3 us (0.953)
  waiting for transfers between devices: 21.6 us -> 32.6 us
  starting transfers between devices: 37.8 us -> 28.2 us
  local copies, waits for them, and re-layouts: 8.13 us -> 2.48 us
  other arithmetic: 2.29 us -> 0.89 us
  Pallas kernels: 17.7 us -> 19 us
    ppermute x29 -> x30, waiting for transfers between devices: 21.6 us -> 32.6 us  [swap(): return lax.ppermute(x, axis, [(i, i ^ k) for i in range(size)])]
    ppermute x29 -> x30, starting transfers between devices: 37.8 us -> 28.2 us  [swap(): return lax.ppermute(x, axis, [(i, i ^ k) for i in range(size)])]
    unnamed x28 -> x18, local copies, waits for them, and re-layouts: 8.07 us -> 2.46 us
    pallas_call x2, Pallas kernels: 2.56 us -> 4.92 us  [stage(): pl.pallas_call(stage_kernel, out_shape=[jax.ShapeDtypeStruct((depth, 2 *...]
    concatenate x2 -> x0, other arithmetic: 1.4 us -> none  [the longest x1 0.71 us: local(): jnp.concatenate([sets[1][0][:, half:], sets[1][1][:, inner:]], axis=1)]
  transfers between devices with their start and end apart: 29 -> 30, of which waited for: 10 -> 16; matrix products, arithmetic and copies ran while one was open for 2% -> 0% of each run, Pallas kernels for 9% -> 12%
where the time goes in v3:
time: 95.3 us; the launch traced here: 95 us
  waiting for transfers between devices  32.6 us (34%)
  starting transfers between devices  28.2 us (30%)
  Pallas kernels  19 us (20%)
  blocking collectives  10.4 us (11%)
  local copies, waits for them, and re-layouts  2.48 us (3%)
  between operations  1.44 us (2%)
    ppermute x30, waiting for transfers between devices, swap(): return lax.ppermute(x, axis, [(i, i ^ k) for i in range(size)])  32.6 us
    ppermute x30, starting transfers between devices, swap(): return lax.ppermute(x, axis, [(i, i ^ k) for i in range(size)])  28.2 us
    all_to_all x1, blocking collectives, local(): stats = lax.all_to_all(stats, ('ctx', 'tp'), 0, 0, tiled=True)  10.4 us
    pallas_call x2, Pallas kernels, attend(): pl.pallas_call(lambda *refs: attend_kernel(chips, tp_count, own_rows, kv_...  7.92 us
    pallas_call x2, Pallas kernels, stage(): pl.pallas_call(stage_kernel, out_shape=[jax.ShapeDtypeStruct((depth, 2 *...  4.92 us
    pallas_call x2, Pallas kernels, score(): pl.pallas_call(lambda *refs: score_kernel(chips, tp_count, own_rows, bloc...  4.41 us
    unnamed x18, local copies, waits for them, and re-layouts  2.46 us
  transfers between devices with their start and end apart: 30, of which 16 were waited for; matrix products, arithmetic and copies ran while one was open for 0% of the time, Pallas kernels for 12%

profile of v3, /device:TPU:0, one launch (start us, length us, event | category | flops | bytes accessed | tf_op | source)
XLA Modules:
  0.0 95.0 jit_solution(12039842655096711056)
XLA Ops:
  0.6 0.0 copy-start.1
  0.7 0.5 collective-permute-start
  1.2 0.1 collective-permute-start.1
  1.2 1.0 %collective-permute-done = bf16[64,256]{1,0:T(8,128)(2,1)S(1)} collective-permute-done((bf16[64,256]{1,0:T(8,128)(2,1)}, bf16[64,256]{1,0:T(8,128)(2,1)S(1)}, u32[]{:S(2)}, u32[]{:S(2)}) %collective-permute-start) | collective-permute-done | bytes 32800 | tf_op jit(solution)/shard_map/ppermute | solution.py:22
  2.2 0.3 collective-permute-done.1
  2.6 0.8 pad_maximum_fusion.refs_5_
  3.4 0.2 collective-permute-start.2
  3.6 2.9 %collective-permute-start.6 = (bf16[64,2048]{1,0:T(8,128)(2,1)}, bf16[64,2048]{1,0:T(8,128)(2,1)S(1)}, u32[]{:S(2)}, u32[]{:S(2)}) collective-permute-start(bf16[64,2048]{1,0:T(8,128)(2,1)} %refs_4_.3), channel_id=1, source_target_pairs={{0,16},{4,20},{8,24},{12,28},{16,0},{20,4},{24,8},{28,12},{1,17},{... | collective-permute-start | bytes 786440 | tf_op jit(solution)/shard_map/ppermute | solution.py:22
  6.5 1.5 %collective-permute-start.5 = (bf16[64,1024]{1,0:T(8,128)(2,1)S(1)}, bf16[64,1024]{1,0:T(8,128)(2,1)}, u32[]{:S(2)}, u32[]{:S(2)}) collective-permute-start(bf16[64,1024]{1,0:T(8,128)(2,1)S(1)} %pad_maximum_fusion.refs_5_), channel_id=1, source_target_pairs={{0,8},{4,12},{8,0},{12,4},{16,24},{20,28},{24,16},{28,20},{1,9},{5... | collective-permute-start | bytes 393224 | tf_op jit(solution)/shard_map/ppermute | solution.py:22
  8.0 0.5 collective-permute-start.4
  8.5 4.8 %collective-permute-done.6.refs_8_ = bf16[64,2048]{1,0:T(8,128)(2,1)S(1)} collective-permute-done((bf16[64,2048]{1,0:T(8,128)(2,1)}, bf16[64,2048]{1,0:T(8,128)(2,1)S(1)}, u32[]{:S(2)}, u32[]{:S(2)}) %collective-permute-start.6) | collective-permute-done | bytes 262176 | tf_op jit(solution)/shard_map/ppermute | solution.py:22
  13.3 1.7 %collective-permute-start.8 = (bf16[64,2048]{1,0:T(8,128)(2,1)S(1)}, bf16[64,2048]{1,0:T(8,128)(2,1)}, u32[]{:S(2)}, u32[]{:S(2)}) collective-permute-start(bf16[64,2048]{1,0:T(8,128)(2,1)S(1)} %collective-permute-done.6.refs_8_), channel_id=1, source_target_pairs={{0,8},{4,12},{8,0},{12,4},{16,24},{20,28},{24,16},{28,20},{1,9},{5... | collective-permute-start | bytes 786440 | tf_op jit(solution)/shard_map/ppermute | solution.py:22
  15.7 0.1 collective-permute-start.3
  15.8 0.1 pad_add_fusion.place_ref.refs_0_
  15.8 0.0 collective-permute-done.5.refs_7_
  15.8 1.5 %collective-permute-start.9 = (bf16[64,1024]{1,0:T(8,128)(2,1)}, bf16[64,1024]{1,0:T(8,128)(2,1)S(1)}, u32[]{:S(2)}, u32[]{:S(2)}) collective-permute-start(bf16[64,1024]{1,0:T(8,128)(2,1)} %collective-permute-done.5.refs_7_), channel_id=1, source_target_pairs={{0,16},{4,20},{8,24},{12,28},{16,0},{20,4},{24,8},{28,12},{1,17},{... | collective-permute-start | bytes 393224 | tf_op jit(solution)/shard_map/ppermute | solution.py:22
  17.4 1.7 %copy-done = bf16[2048,640]{1,0:T(8,128)(2,1)S(1)} copy-done((bf16[2048,640]{1,0:T(8,128)(2,1)S(1)}, bf16[2048,640]{1,0:T(8,128)(2,1)}, u32[]{:S(2)}) %copy-start) | copy-done | bytes 2621464
  19.1 1.0 %stage.2 = (bf16[2048,1280]{1,0:T(8,128)(2,1)S(1)}, f32[8,128]{1,0:T(8,128)S(1)}) custom-call(s32[3]{0:T(128)S(1)} %pad_add_fusion.place_ref.refs_0_, bf16[2048,640]{1,0:T(8,128)(2,1)S(1)} %copy-done, bf16[2048,640]{1,0:T(8,128)(2,1)S(1)} %collective-permute-done.2.sib_ref), custom_call_target="tpu_custom_call" | custom-call | tf_op jit(solution)/shard_map/stage/pallas_call | solution.py:168
  20.1 0.6 collective-permute-start.7
  20.7 0.7 copy-done.3
  21.4 0.0 collective-permute-done.4.refs_6_
  21.4 0.6 collective-permute-done.9.refs_11_
  22.0 1.1 %collective-permute-done.8.refs_10_ = bf16[64,2048]{1,0:T(8,128)(2,1)} collective-permute-done((bf16[64,2048]{1,0:T(8,128)(2,1)S(1)}, bf16[64,2048]{1,0:T(8,128)(2,1)}, u32[]{:S(2)}, u32[]{:S(2)}) %collective-permute-start.8) | collective-permute-done | bytes 262176 | tf_op jit(solution)/shard_map/ppermute | solution.py:22
  23.1 2.7 %collective-permute-done.7.refs_9_ = bf16[64,1024]{1,0:T(8,128)(2,1)S(1)} collective-permute-done((bf16[64,1024]{1,0:T(8,128)(2,1)S(1)}, bf16[64,1024]{1,0:T(8,128)(2,1)S(1)}, u32[]{:S(2)}, u32[]{:S(2)}) %collective-permute-start.7) | collective-permute-done | bytes 131104 | tf_op jit(solution)/shard_map/ppermute | solution.py:22
  25.8 4.0 %attend.2 = (bf16[64,1280]{1,0:T(8,128)(2,1)S(1)}, bf16[64,1280]{1,0:T(8,128)(2,1)S(1)}) custom-call(s32[3]{0:T(128)S(1)} %pad_add_fusion.place_ref.refs_0_, f32[8,128]{1,0:T(8,128)S(1)} %get-tuple-element.41.refs_1_, s32[1,64]{1,0:T(1,128)S(1)} %bitcast.9, bf16[2048,1280]{1,0:T(8,128)(2,1)S(1)} %get-tuple-element.42.refs_3_, ...), custom_call_target="tpu_custom_call" | custom-call | tf_op jit(solution)/shard_map/attend/pallas_call | solution.py:101
  29.8 0.0 copy-start.8
  29.8 0.0 copy-start.2
  29.8 0.1 collective-permute-start.10
  29.9 2.7 %collective-permute-start.12 = (bf16[64,1280]{1,0:T(8,128)(2,1)S(1)}, bf16[64,1280]{1,0:T(8,128)(2,1)S(1)}, u32[]{:S(2)}, u32[]{:S(2)}) collective-permute-start(bf16[64,1280]{1,0:T(8,128)(2,1)S(1)} %get-tuple-element.46.refs_1_), channel_id=1, source_target_pairs={{0,2},{1,3},{2,0},{3,1},{4,6},{5,7},{6,4},{7,5},{8,10},{9,11},{10,... | collective-permute-start | bytes 491528 | tf_op jit(solution)/shard_map/ppermute | solution.py:22
  32.6 4.0 %attend.3 = (f32[64,1280]{1,0:T(8,128)S(1)}, bf16[64,1280]{1,0:T(8,128)(2,1)S(1)}) custom-call(s32[3]{0:T(128)S(1)} %pad_add_fusion.place_ref.refs_0_, bf16[64,1280]{1,0:T(8,128)(2,1)S(1)} %get-tuple-element.46.refs_1_, s32[1,64]{1,0:T(1,128)S(1)} %bitcast.10, bf16[2048,1280]{1,0:T(8,128)(2,1)S(1)} %get-tuple-element.42.refs_3_, ...), custom_call_target="tpu_custom_call" | custom-call | tf_op jit(solution)/shard_map/attend/pallas_call | solution.py:101
  36.5 1.6 %collective-permute-start.11 = (bf16[64,1280]{1,0:T(8,128)(2,1)S(1)}, bf16[64,1280]{1,0:T(8,128)(2,1)S(1)}, u32[]{:S(2)}, u32[]{:S(2)}) collective-permute-start(bf16[64,1280]{1,0:T(8,128)(2,1)S(1)} %get-tuple-element.54), channel_id=1, source_target_pairs={{0,1},{1,0},{2,3},{3,2},{4,5},{5,4},{6,7},{7,6},{8,9},{9,8},{10,11... | collective-permute-start | bytes 491528 | tf_op jit(solution)/shard_map/ppermute | solution.py:22
  38.2 0.2 collective-permute-start.13
  38.4 9.5 %collective-permute-done.11.refs_5_ = bf16[64,1280]{1,0:T(8,128)(2,1)S(1)} collective-permute-done((bf16[64,1280]{1,0:T(8,128)(2,1)S(1)}, bf16[64,1280]{1,0:T(8,128)(2,1)S(1)}, u32[]{:S(2)}, u32[]{:S(2)}) %collective-permute-start.11) | collective-permute-done | bytes 163872 | tf_op jit(solution)/shard_map/ppermute | solution.py:22
  48.0 0.7 update.1
  48.6 2.7 %collective-permute-start.15 = (bf16[64,1280]{1,0:T(8,128)(2,1)S(1)}, bf16[64,1280]{1,0:T(8,128)(2,1)S(1)}, u32[]{:S(2)}, u32[]{:S(2)}) collective-permute-start(bf16[64,1280]{1,0:T(8,128)(2,1)S(1)} %get-tuple-element.66.refs_6_), channel_id=1, source_target_pairs={{0,2},{1,3},{2,0},{3,1},{4,6},{5,7},{6,4},{7,5},{8,10},{9,11},{10,... | collective-permute-start | bytes 491528 | tf_op jit(solution)/shard_map/ppermute | solution.py:22
  51.3 1.1 %collective-permute-start.19 = (bf16[64,1280]{1,0:T(8,128)(2,1)S(1)}, bf16[64,1280]{1,0:T(8,128)(2,1)S(1)}, u32[]{:S(2)}, u32[]{:S(2)}) collective-permute-start(bf16[64,1280]{1,0:T(8,128)(2,1)S(1)} %get-tuple-element.66.refs_6_), channel_id=1, source_target_pairs={{0,1},{1,0},{2,3},{3,2},{4,5},{5,4},{6,7},{7,6},{8,9},{9,8},{10,11... | collective-permute-start | bytes 491528 | tf_op jit(solution)/shard_map/ppermute | solution.py:22
  52.4 0.0 collective-permute-done.14.refs_1_
  52.5 0.5 collective-permute-start.17
  53.0 0.5 collective-permute-start.16
  53.5 3.9 %stage.3 = (bf16[5120,768]{1,0:T(8,128)(2,1)S(1)}, f32[8,128]{1,0:T(8,128)S(1)}) custom-call(s32[3]{0:T(128)S(1)} %pad_add_fusion.place_ref.refs_0_, bf16[5120,384]{1,0:T(8,128)(2,1)} %own_ref.1, bf16[5120,384]{1,0:T(8,128)(2,1)} %collective-permute-done.10.sib_ref), custom_call_target="tpu_custom_call" | custom-call | tf_op jit(solution)/shard_map/stage/pallas_call | solution.py:168
  57.4 1.9 %collective-permute-done.15.refs_6_ = bf16[64,1280]{1,0:T(8,128)(2,1)S(1)} collective-permute-done((bf16[64,1280]{1,0:T(8,128)(2,1)S(1)}, bf16[64,1280]{1,0:T(8,128)(2,1)S(1)}, u32[]{:S(2)}, u32[]{:S(2)}) %collective-permute-start.15) | collective-permute-done | bytes 163872 | tf_op jit(solution)/shard_map/ppermute | solution.py:22
  59.4 1.7 %collective-permute-done.19.refs_10_ = bf16[64,1280]{1,0:T(8,128)(2,1)S(1)} collective-permute-done((bf16[64,1280]{1,0:T(8,128)(2,1)S(1)}, bf16[64,1280]{1,0:T(8,128)(2,1)S(1)}, u32[]{:S(2)}, u32[]{:S(2)}) %collective-permute-start.19) | collective-permute-done | bytes 163872 | tf_op jit(solution)/shard_map/ppermute | solution.py:22
  61.1 0.5 collective-permute-start.20
  61.6 0.5 collective-permute-start.24
  62.1 1.5 %collective-permute-start.21 = (bf16[64,1280]{1,0:T(8,128)(2,1)S(1)}, bf16[64,1280]{1,0:T(8,128)(2,1)S(1)}, u32[]{:S(2)}, u32[]{:S(2)}) collective-permute-start(bf16[64,1280]{1,0:T(8,128)(2,1)S(1)} %collective-permute-done.19.refs_10_), channel_id=1, source_target_pairs={{0,16},{4,20},{8,24},{12,28},{16,0},{20,4},{24,8},{28,12},{1,17},{... | collective-permute-start | bytes 491528 | tf_op jit(solution)/shard_map/ppermute | solution.py:22
  63.7 1.5 %collective-permute-start.18 = (bf16[64,1280]{1,0:T(8,128)(2,1)S(1)}, bf16[64,1280]{1,0:T(8,128)(2,1)S(1)}, u32[]{:S(2)}, u32[]{:S(2)}) collective-permute-start(bf16[64,1280]{1,0:T(8,128)(2,1)S(1)} %collective-permute-done.17.refs_8_), channel_id=1, source_target_pairs={{0,8},{4,12},{8,0},{12,4},{16,24},{20,28},{24,16},{28,20},{1,9},{5... | collective-permute-start | bytes 491528 | tf_op jit(solution)/shard_map/ppermute | solution.py:22
  65.2 0.0 collective-permute-done.26.refs_10_
  65.2 0.5 collective-permute-start.27
  65.7 2.5 %collective-permute-done.20.refs_11_ = bf16[64,1280]{1,0:T(8,128)(2,1)S(1)} collective-permute-done((bf16[64,1280]{1,0:T(8,128)(2,1)S(1)}, bf16[64,1280]{1,0:T(8,128)(2,1)S(1)}, u32[]{:S(2)}, u32[]{:S(2)}) %collective-permute-start.20) | collective-permute-done | bytes 163872 | tf_op jit(solution)/shard_map/ppermute | solution.py:22
  68.2 0.5 collective-permute-start.22
  68.7 0.1 collective-permute-done.24.refs_8_
  68.8 1.5 %collective-permute-start.23 = (bf16[64,1280]{1,0:T(8,128)(2,1)S(1)}, bf16[64,1280]{1,0:T(8,128)(2,1)S(1)}, u32[]{:S(2)}, u32[]{:S(2)}) collective-permute-start(bf16[64,1280]{1,0:T(8,128)(2,1)S(1)} %collective-permute-done.15.refs_6_), channel_id=1, source_target_pairs={{0,8},{4,12},{8,0},{12,4},{16,24},{20,28},{24,16},{28,20},{1,9},{5... | collective-permute-start | bytes 491528 | tf_op jit(solution)/shard_map/ppermute | solution.py:22
  70.3 2.0 %collective-permute-done.21.refs_12_ = bf16[64,1280]{1,0:T(8,128)(2,1)S(1)} collective-permute-done((bf16[64,1280]{1,0:T(8,128)(2,1)S(1)}, bf16[64,1280]{1,0:T(8,128)(2,1)S(1)}, u32[]{:S(2)}, u32[]{:S(2)}) %collective-permute-start.21) | collective-permute-done | bytes 163872 | tf_op jit(solution)/shard_map/ppermute | solution.py:22
  72.3 0.5 collective-permute-start.28
  72.8 1.5 %collective-permute-start.25 = (bf16[64,1280]{1,0:T(8,128)(2,1)S(1)}, bf16[64,1280]{1,0:T(8,128)(2,1)S(1)}, u32[]{:S(2)}, u32[]{:S(2)}) collective-permute-start(bf16[64,1280]{1,0:T(8,128)(2,1)S(1)} %collective-permute-done.24.refs_8_), channel_id=1, source_target_pairs={{0,8},{4,12},{8,0},{12,4},{16,24},{20,28},{24,16},{28,20},{1,9},{5... | collective-permute-start | bytes 491528 | tf_op jit(solution)/shard_map/ppermute | solution.py:22
  74.3 1.0 %collective-permute-done.27.refs_11_ = bf16[64,1280]{1,0:T(8,128)(2,1)S(1)} collective-permute-done((bf16[64,1280]{1,0:T(8,128)(2,1)S(1)}, bf16[64,1280]{1,0:T(8,128)(2,1)S(1)}, u32[]{:S(2)}, u32[]{:S(2)}) %collective-permute-start.27) | collective-permute-done | bytes 163872 | tf_op jit(solution)/shard_map/ppermute | solution.py:22
  75.2 0.6 collective-permute-start.29
  75.8 2.2 %score.2 = f32[32,8,128]{2,1,0:T(8,128)S(1)} custom-call(s32[3]{0:T(128)S(1)} %pad_add_fusion.place_ref.refs_0_, f32[8,128]{1,0:T(8,128)S(1)} %collective-permute-done.14.refs_1_, f32[8,128]{1,0:T(8,128)S(1)} %get-tuple-element.62.refs_2_, s32[1,512]{1,0:T(1,128)S(1)} %bitcast.7, f32[8,640]{1,0:T(8,128)S(1)} %reshape.13.refs_4_, ...), custom_call_target="tpu_custom_call" | custom-call | tf_op jit(solution)/shard_map/score/pallas_call | solution.py:229
  78.0 0.7 collective-permute-done.23.refs_7_
  78.7 2.2 %collective-permute-done.25.refs_9_ = bf16[64,1280]{1,0:T(8,128)(2,1)S(1)} collective-permute-done((bf16[64,1280]{1,0:T(8,128)(2,1)S(1)}, bf16[64,1280]{1,0:T(8,128)(2,1)S(1)}, u32[]{:S(2)}, u32[]{:S(2)}) %collective-permute-start.25) | collective-permute-done | bytes 163872 | tf_op jit(solution)/shard_map/ppermute | solution.py:22
  81.0 0.2 collective-permute-done.29.refs_13_
  81.2 2.2 %score.3 = f32[32,8,128]{2,1,0:T(8,128)S(1)} custom-call(s32[3]{0:T(128)S(1)} %pad_add_fusion.place_ref.refs_0_, f32[8,128]{1,0:T(8,128)S(1)} %collective-permute-done.14.refs_1_, f32[8,128]{1,0:T(8,128)S(1)} %get-tuple-element.62.refs_2_, s32[1,512]{1,0:T(1,128)S(1)} %bitcast.8, f32[8,640]{1,0:T(8,128)S(1)} %reshape.13.refs_4_, ...), custom_call_target="tpu_custom_call" | custom-call | tf_op jit(solution)/shard_map/score/pallas_call | solution.py:229
  83.5 10.4 %all_to_all.5.refs_2_ = f32[32,8,128]{2,1,0:T(8,128)S(1)} all-to-all(f32[32,8,128]{2,1,0:T(8,128)S(1)} %add.3), channel_id=1, replica_groups=mesh['ctx'=8,'tp'=4] {'ctx','tp'}, dimensions={0} | all-to-all | bytes 262144 | tf_op jit(solution)/shard_map/all_to_all | solution.py:329
  93.9 1.1 %merge.1 = (f32[1,64]{1,0:T(1,128)}, f32[1,64]{1,0:T(1,128)}) custom-call(s32[3]{0:T(128)S(1)} %pad_add_fusion.place_ref.refs_0_, f32[1,64]{1,0:T(1,128)S(1)} %bitcast.11, f32[32,8,128]{2,1,0:T(8,128)S(1)} %all_to_all.5.refs_2_), custom_call_target="tpu_custom_call" | custom-call | tf_op jit(solution)/shard_map/merge/pallas_call | solution.py:262
  (27 shorter events, 0.1 us)
Async XLA Ops:
  0.6 25.2 %copy-start.1 = (bf16[64,2048]{1,0:T(8,128)(2,1)S(1)}, bf16[64,2048]{1,0:T(8,128)(2,1)}, u32[]{:S(2)}) copy-start(bf16[64,2048]{1,0:T(8,128)(2,1)} %refs_4_.3) | copy-start | bytes 786436
  0.6 25.2 %copy-start.6 = (s32[64]{0:T(128)S(1)}, s32[64]{0:T(128)}, u32[]{:S(2)}) copy-start(s32[64]{0:T(128)} %param.20) | copy-start | bytes 772
  0.7 1.6 %collective-permute-start = (bf16[64,256]{1,0:T(8,128)(2,1)}, bf16[64,256]{1,0:T(8,128)(2,1)S(1)}, u32[]{:S(2)}, u32[]{:S(2)}) collective-permute-start(bf16[64,256]{1,0:T(8,128)(2,1)} %param.12), channel_id=1, source_target_pairs={{0,4},{4,0},{8,12},{12,8},{16,20},{20,16},{24,28},{28,24},{1,5},{5... | collective-permute-start | bytes 98312 | tf_op jit(solution)/shard_map/ppermute | solution.py:22
  1.2 1.4 %collective-permute-start.1 = (bf16[64,256]{1,0:T(8,128)(2,1)}, bf16[64,256]{1,0:T(8,128)(2,1)S(1)}, u32[]{:S(2)}, u32[]{:S(2)}) collective-permute-start(bf16[64,256]{1,0:T(8,128)(2,1)} %param.13), channel_id=1, source_target_pairs={{0,4},{4,0},{8,12},{12,8},{16,20},{20,16},{24,28},{28,24},{1,5},{5... | collective-permute-start | bytes 98312 | tf_op jit(solution)/shard_map/ppermute | solution.py:22
  3.4 14.0 %collective-permute-start.2 = (bf16[2048,640]{1,0:T(8,128)(2,1)}, bf16[2048,640]{1,0:T(8,128)(2,1)S(1)}, u32[]{:S(2)}, u32[]{:S(2)}) collective-permute-start(bf16[2048,640]{1,0:T(8,128)(2,1)} %own_ref), channel_id=1, source_target_pairs={{0,4},{4,0},{8,12},{12,8},{16,20},{20,16},{24,28},{28,24},{1,5},{5... | collective-permute-start | bytes 7864328 | tf_op jit(solution)/shard_map/ppermute | solution.py:22
  3.6 9.7 %collective-permute-start.6 = (bf16[64,2048]{1,0:T(8,128)(2,1)}, bf16[64,2048]{1,0:T(8,128)(2,1)S(1)}, u32[]{:S(2)}, u32[]{:S(2)}) collective-permute-start(bf16[64,2048]{1,0:T(8,128)(2,1)} %refs_4_.3), channel_id=1, source_target_pairs={{0,16},{4,20},{8,24},{12,28},{16,0},{20,4},{24,8},{28,12},{1,17},{... | collective-permute-start | bytes 786440 | tf_op jit(solution)/shard_map/ppermute | solution.py:22
  6.5 9.4 %collective-permute-start.5 = (bf16[64,1024]{1,0:T(8,128)(2,1)S(1)}, bf16[64,1024]{1,0:T(8,128)(2,1)}, u32[]{:S(2)}, u32[]{:S(2)}) collective-permute-start(bf16[64,1024]{1,0:T(8,128)(2,1)S(1)} %pad_maximum_fusion.refs_5_), channel_id=1, source_target_pairs={{0,8},{4,12},{8,0},{12,4},{16,24},{20,28},{24,16},{28,20},{1,9},{5... | collective-permute-start | bytes 393224 | tf_op jit(solution)/shard_map/ppermute | solution.py:22
  8.0 13.4 %collective-permute-start.4 = (bf16[64,2048]{1,0:T(8,128)(2,1)}, bf16[64,2048]{1,0:T(8,128)(2,1)S(1)}, u32[]{:S(2)}, u32[]{:S(2)}) collective-permute-start(bf16[64,2048]{1,0:T(8,128)(2,1)} %refs_4_.3), channel_id=1, source_target_pairs={{0,8},{4,12},{8,0},{12,4},{16,24},{20,28},{24,16},{28,20},{1,9},{5... | collective-permute-start | bytes 786440 | tf_op jit(solution)/shard_map/ppermute | solution.py:22
  13.3 9.8 %collective-permute-start.8 = (bf16[64,2048]{1,0:T(8,128)(2,1)S(1)}, bf16[64,2048]{1,0:T(8,128)(2,1)}, u32[]{:S(2)}, u32[]{:S(2)}) collective-permute-start(bf16[64,2048]{1,0:T(8,128)(2,1)S(1)} %collective-permute-done.6.refs_8_), channel_id=1, source_target_pairs={{0,8},{4,12},{8,0},{12,4},{16,24},{20,28},{24,16},{28,20},{1,9},{5... | collective-permute-start | bytes 786440 | tf_op jit(solution)/shard_map/ppermute | solution.py:22
  15.7 5.0 %collective-permute-start.3 = (bf16[128,640]{1,0:T(8,128)(2,1)}, bf16[128,640]{1,0:T(8,128)(2,1)S(1)}, u32[]{:S(2)}, u32[]{:S(2)}) collective-permute-start(bf16[128,640]{1,0:T(8,128)(2,1)} %refs_2_), channel_id=1, source_target_pairs={{0,4},{4,0},{8,12},{12,8},{16,20},{20,16},{24,28},{28,24},{1,5},{5... | collective-permute-start | bytes 491528 | tf_op jit(solution)/shard_map/ppermute | solution.py:22
  15.8 6.1 %collective-permute-start.9 = (bf16[64,1024]{1,0:T(8,128)(2,1)}, bf16[64,1024]{1,0:T(8,128)(2,1)S(1)}, u32[]{:S(2)}, u32[]{:S(2)}) collective-permute-start(bf16[64,1024]{1,0:T(8,128)(2,1)} %collective-permute-done.5.refs_7_), channel_id=1, source_target_pairs={{0,16},{4,20},{8,24},{12,28},{16,0},{20,4},{24,8},{28,12},{1,17},{... | collective-permute-start | bytes 393224 | tf_op jit(solution)/shard_map/ppermute | solution.py:22
  17.4 1.7 %copy-start = (bf16[2048,640]{1,0:T(8,128)(2,1)S(1)}, bf16[2048,640]{1,0:T(8,128)(2,1)}, u32[]{:S(2)}) copy-start(bf16[2048,640]{1,0:T(8,128)(2,1)} %own_ref) | copy-start | bytes 7864324
  20.1 5.7 %collective-permute-start.7 = (bf16[64,1024]{1,0:T(8,128)(2,1)S(1)}, bf16[64,1024]{1,0:T(8,128)(2,1)S(1)}, u32[]{:S(2)}, u32[]{:S(2)}) collective-permute-start(bf16[64,1024]{1,0:T(8,128)(2,1)S(1)} %pad_maximum_fusion.refs_5_), channel_id=1, source_target_pairs={{0,16},{4,20},{8,24},{12,28},{16,0},{20,4},{24,8},{28,12},{1,17},{... | collective-permute-start | bytes 393224 | tf_op jit(solution)/shard_map/ppermute | solution.py:22
  20.7 0.7 copy-start.3
  29.8 8.6 %copy-start.8 = (bf16[5120]{0:T(1024)(128)(2,1)S(1)}, bf16[5120]{0:T(1024)(128)(2,1)}, u32[]{:S(2)}) copy-start(bf16[5120]{0:T(1024)(128)(2,1)} %param.16) | copy-start | bytes 30724
  29.8 18.2 %copy-start.2 = (bf16[128,640]{1,0:T(8,128)(2,1)S(1)}, bf16[128,640]{1,0:T(8,128)(2,1)}, u32[]{:S(2)}) copy-start(bf16[128,640]{1,0:T(8,128)(2,1)} %refs_2_) | copy-start | bytes 491524
  29.8 18.2 %copy-start.4 = (bf16[128,640]{1,0:T(8,128)(2,1)S(1)}, bf16[128,640]{1,0:T(8,128)(2,1)}, u32[]{:S(2)}) copy-start(bf16[128,640]{1,0:T(8,128)(2,1)} %copy-done.3) | copy-start | bytes 491524
  29.8 8.6 %collective-permute-start.10 = (bf16[5120,384]{1,0:T(8,128)(2,1)}, bf16[5120,384]{1,0:T(8,128)(2,1)}, u32[]{:S(2)}, u32[]{:S(2)}) collective-permute-start(bf16[5120,384]{1,0:T(8,128)(2,1)} %own_ref.1), channel_id=1, source_target_pairs={{0,4},{4,0},{8,12},{12,8},{16,20},{20,16},{24,28},{28,24},{1,5},{5... | collective-permute-start | bytes 11796488 | tf_op jit(solution)/shard_map/ppermute | solution.py:22
  29.9 18.0 %collective-permute-start.12 = (bf16[64,1280]{1,0:T(8,128)(2,1)S(1)}, bf16[64,1280]{1,0:T(8,128)(2,1)S(1)}, u32[]{:S(2)}, u32[]{:S(2)}) collective-permute-start(bf16[64,1280]{1,0:T(8,128)(2,1)S(1)} %get-tuple-element.46.refs_1_), channel_id=1, source_target_pairs={{0,2},{1,3},{2,0},{3,1},{4,6},{5,7},{6,4},{7,5},{8,10},{9,11},{10,... | collective-permute-start | bytes 491528 | tf_op jit(solution)/shard_map/ppermute | solution.py:22
  36.5 11.4 %collective-permute-start.11 = (bf16[64,1280]{1,0:T(8,128)(2,1)S(1)}, bf16[64,1280]{1,0:T(8,128)(2,1)S(1)}, u32[]{:S(2)}, u32[]{:S(2)}) collective-permute-start(bf16[64,1280]{1,0:T(8,128)(2,1)S(1)} %get-tuple-element.54), channel_id=1, source_target_pairs={{0,1},{1,0},{2,3},{3,2},{4,5},{5,4},{6,7},{7,6},{8,9},{9,8},{10,11... | collective-permute-start | bytes 491528 | tf_op jit(solution)/shard_map/ppermute | solution.py:22
  38.2 9.8 %collective-permute-start.13 = (bf16[64,1280]{1,0:T(8,128)(2,1)S(1)}, bf16[64,1280]{1,0:T(8,128)(2,1)S(1)}, u32[]{:S(2)}, u32[]{:S(2)}) collective-permute-start(bf16[64,1280]{1,0:T(8,128)(2,1)S(1)} %get-tuple-element.55), channel_id=1, source_target_pairs={{0,3},{1,2},{2,1},{3,0},{4,7},{5,6},{6,5},{7,4},{8,11},{9,10},{10,... | collective-permute-start | bytes 491528 | tf_op jit(solution)/shard_map/ppermute | solution.py:22
  48.6 10.7 %collective-permute-start.15 = (bf16[64,1280]{1,0:T(8,128)(2,1)S(1)}, bf16[64,1280]{1,0:T(8,128)(2,1)S(1)}, u32[]{:S(2)}, u32[]{:S(2)}) collective-permute-start(bf16[64,1280]{1,0:T(8,128)(2,1)S(1)} %get-tuple-element.66.refs_6_), channel_id=1, source_target_pairs={{0,2},{1,3},{2,0},{3,1},{4,6},{5,7},{6,4},{7,5},{8,10},{9,11},{10,... | collective-permute-start | bytes 491528 | tf_op jit(solution)/shard_map/ppermute | solution.py:22
  51.3 24.5 %copy-start.5 = (s32[512]{0:T(512)S(1)}, s32[512]{0:T(512)}, u32[]{:S(2)}) copy-start(s32[512]{0:T(512)} %param.18) | copy-start | bytes 6148
  51.3 1.2 %collective-permute-start.14 = (f32[8,128]{1,0:T(8,128)S(1)}, f32[8,128]{1,0:T(8,128)S(1)}, u32[]{:S(2)}, u32[]{:S(2)}) collective-permute-start(f32[8,128]{1,0:T(8,128)S(1)} %get-tuple-element.57), channel_id=1, source_target_pairs={{0,4},{4,0},{8,12},{12,8},{16,20},{20,16},{24,28},{28,24},{1,5},{5... | collective-permute-start | bytes 12296 | tf_op jit(solution)/shard_map/ppermute | solution.py:22
  51.3 9.8 %collective-permute-start.19 = (bf16[64,1280]{1,0:T(8,128)(2,1)S(1)}, bf16[64,1280]{1,0:T(8,128)(2,1)S(1)}, u32[]{:S(2)}, u32[]{:S(2)}) collective-permute-start(bf16[64,1280]{1,0:T(8,128)(2,1)S(1)} %get-tuple-element.66.refs_6_), channel_id=1, source_target_pairs={{0,1},{1,0},{2,3},{3,2},{4,5},{5,4},{6,7},{7,6},{8,9},{9,8},{10,11... | collective-permute-start | bytes 491528 | tf_op jit(solution)/shard_map/ppermute | solution.py:22
  52.5 9.7 %collective-permute-start.17 = (bf16[64,1280]{1,0:T(8,128)(2,1)S(1)}, bf16[64,1280]{1,0:T(8,128)(2,1)S(1)}, u32[]{:S(2)}, u32[]{:S(2)}) collective-permute-start(bf16[64,1280]{1,0:T(8,128)(2,1)S(1)} %get-tuple-element.66.refs_6_), channel_id=1, source_target_pairs={{0,16},{4,20},{8,24},{12,28},{16,0},{20,4},{24,8},{28,12},{1,17},{... | collective-permute-start | bytes 491528 | tf_op jit(solution)/shard_map/ppermute | solution.py:22
  53.0 10.7 %collective-permute-start.16 = (bf16[64,1280]{1,0:T(8,128)(2,1)S(1)}, bf16[64,1280]{1,0:T(8,128)(2,1)S(1)}, u32[]{:S(2)}, u32[]{:S(2)}) collective-permute-start(bf16[64,1280]{1,0:T(8,128)(2,1)S(1)} %get-tuple-element.66.refs_6_), channel_id=1, source_target_pairs={{0,8},{4,12},{8,0},{12,4},{16,24},{20,28},{24,16},{28,20},{1,9},{5... | collective-permute-start | bytes 491528 | tf_op jit(solution)/shard_map/ppermute | solution.py:22
  59.4 5.8 %collective-permute-start.26 = (bf16[64,1280]{1,0:T(8,128)(2,1)S(1)}, bf16[64,1280]{1,0:T(8,128)(2,1)S(1)}, u32[]{:S(2)}, u32[]{:S(2)}) collective-permute-start(bf16[64,1280]{1,0:T(8,128)(2,1)S(1)} %collective-permute-done.15.refs_6_), channel_id=1, source_target_pairs={{0,1},{1,0},{2,3},{3,2},{4,5},{5,4},{6,7},{7,6},{8,9},{9,8},{10,11... | collective-permute-start | bytes 491528 | tf_op jit(solution)/shard_map/ppermute | solution.py:22
  61.1 7.1 %collective-permute-start.20 = (bf16[64,1280]{1,0:T(8,128)(2,1)S(1)}, bf16[64,1280]{1,0:T(8,128)(2,1)S(1)}, u32[]{:S(2)}, u32[]{:S(2)}) collective-permute-start(bf16[64,1280]{1,0:T(8,128)(2,1)S(1)} %collective-permute-done.19.refs_10_), channel_id=1, source_target_pairs={{0,8},{4,12},{8,0},{12,4},{16,24},{20,28},{24,16},{28,20},{1,9},{5... | collective-permute-start | bytes 491528 | tf_op jit(solution)/shard_map/ppermute | solution.py:22
  61.6 7.1 %collective-permute-start.24 = (bf16[64,1280]{1,0:T(8,128)(2,1)S(1)}, bf16[64,1280]{1,0:T(8,128)(2,1)S(1)}, u32[]{:S(2)}, u32[]{:S(2)}) collective-permute-start(bf16[64,1280]{1,0:T(8,128)(2,1)S(1)} %collective-permute-done.15.refs_6_), channel_id=1, source_target_pairs={{0,16},{4,20},{8,24},{12,28},{16,0},{20,4},{24,8},{28,12},{1,17},{... | collective-permute-start | bytes 491528 | tf_op jit(solution)/shard_map/ppermute | solution.py:22
  62.1 10.1 %collective-permute-start.21 = (bf16[64,1280]{1,0:T(8,128)(2,1)S(1)}, bf16[64,1280]{1,0:T(8,128)(2,1)S(1)}, u32[]{:S(2)}, u32[]{:S(2)}) collective-permute-start(bf16[64,1280]{1,0:T(8,128)(2,1)S(1)} %collective-permute-done.19.refs_10_), channel_id=1, source_target_pairs={{0,16},{4,20},{8,24},{12,28},{16,0},{20,4},{24,8},{28,12},{1,17},{... | collective-permute-start | bytes 491528 | tf_op jit(solution)/shard_map/ppermute | solution.py:22
  63.7 9.1 %collective-permute-start.18 = (bf16[64,1280]{1,0:T(8,128)(2,1)S(1)}, bf16[64,1280]{1,0:T(8,128)(2,1)S(1)}, u32[]{:S(2)}, u32[]{:S(2)}) collective-permute-start(bf16[64,1280]{1,0:T(8,128)(2,1)S(1)} %collective-permute-done.17.refs_8_), channel_id=1, source_target_pairs={{0,8},{4,12},{8,0},{12,4},{16,24},{20,28},{24,16},{28,20},{1,9},{5... | collective-permute-start | bytes 491528 | tf_op jit(solution)/shard_map/ppermute | solution.py:22
  65.2 10.0 %collective-permute-start.27 = (bf16[64,1280]{1,0:T(8,128)(2,1)S(1)}, bf16[64,1280]{1,0:T(8,128)(2,1)S(1)}, u32[]{:S(2)}, u32[]{:S(2)}) collective-permute-start(bf16[64,1280]{1,0:T(8,128)(2,1)S(1)} %collective-permute-done.26.refs_10_), channel_id=1, source_target_pairs={{0,8},{4,12},{8,0},{12,4},{16,24},{20,28},{24,16},{28,20},{1,9},{5... | collective-permute-start | bytes 491528 | tf_op jit(solution)/shard_map/ppermute | solution.py:22
  68.2 7.6 %collective-permute-start.22 = (bf16[64,1280]{1,0:T(8,128)(2,1)S(1)}, bf16[64,1280]{1,0:T(8,128)(2,1)S(1)}, u32[]{:S(2)}, u32[]{:S(2)}) collective-permute-start(bf16[64,1280]{1,0:T(8,128)(2,1)S(1)} %collective-permute-done.20.refs_11_), channel_id=1, source_target_pairs={{0,16},{4,20},{8,24},{12,28},{16,0},{20,4},{24,8},{28,12},{1,17},{... | collective-permute-start | bytes 491528 | tf_op jit(solution)/shard_map/ppermute | solution.py:22
  68.8 10.0 %collective-permute-start.23 = (bf16[64,1280]{1,0:T(8,128)(2,1)S(1)}, bf16[64,1280]{1,0:T(8,128)(2,1)S(1)}, u32[]{:S(2)}, u32[]{:S(2)}) collective-permute-start(bf16[64,1280]{1,0:T(8,128)(2,1)S(1)} %collective-permute-done.15.refs_6_), channel_id=1, source_target_pairs={{0,8},{4,12},{8,0},{12,4},{16,24},{20,28},{24,16},{28,20},{1,9},{5... | collective-permute-start | bytes 491528 | tf_op jit(solution)/shard_map/ppermute | solution.py:22
  72.3 8.7 %collective-permute-start.28 = (bf16[64,1280]{1,0:T(8,128)(2,1)S(1)}, bf16[64,1280]{1,0:T(8,128)(2,1)S(1)}, u32[]{:S(2)}, u32[]{:S(2)}) collective-permute-start(bf16[64,1280]{1,0:T(8,128)(2,1)S(1)} %collective-permute-done.26.refs_10_), channel_id=1, source_target_pairs={{0,16},{4,20},{8,24},{12,28},{16,0},{20,4},{24,8},{28,12},{1,17},{... | collective-permute-start | bytes 491528 | tf_op jit(solution)/shard_map/ppermute | solution.py:22
  72.8 8.2 %collective-permute-start.25 = (bf16[64,1280]{1,0:T(8,128)(2,1)S(1)}, bf16[64,1280]{1,0:T(8,128)(2,1)S(1)}, u32[]{:S(2)}, u32[]{:S(2)}) collective-permute-start(bf16[64,1280]{1,0:T(8,128)(2,1)S(1)} %collective-permute-done.24.refs_8_), channel_id=1, source_target_pairs={{0,8},{4,12},{8,0},{12,4},{16,24},{20,28},{24,16},{28,20},{1,9},{5... | collective-permute-start | bytes 491528 | tf_op jit(solution)/shard_map/ppermute | solution.py:22
  75.2 6.0 %collective-permute-start.29 = (bf16[64,1280]{1,0:T(8,128)(2,1)S(1)}, bf16[64,1280]{1,0:T(8,128)(2,1)S(1)}, u32[]{:S(2)}, u32[]{:S(2)}) collective-permute-start(bf16[64,1280]{1,0:T(8,128)(2,1)S(1)} %collective-permute-done.27.refs_11_), channel_id=1, source_target_pairs={{0,16},{4,20},{8,24},{12,28},{16,0},{20,4},{24,8},{28,12},{1,17},{... | collective-permute-start | bytes 491528 | tf_op jit(solution)/shard_map/ppermute | solution.py:22
  78.0 15.8 %copy-start.7 = (f32[64]{0:T(128)S(1)}, f32[64]{0:T(128)}, u32[]{:S(2)}) copy-start(f32[64]{0:T(128)} %param.19) | copy-start | bytes 772

commit v4 on v3

--- a/solution.py
+++ b/solution.py
@@ -6,6 +6,7 @@
 from jax.sharding import PartitionSpec as P
 
 HD = 128
+LOG2E = 1.4426950408889634
 EPSILON = 1e-06
 CEILING = 10.0
 NEGATIVE = -1e30
@@ -25,7 +26,8 @@
 def sides(piece, chips):
     if chips != 4:
         return [piece] + [swap(piece, "ctx", 2 * j) for j in range(1, chips)]
-    return [piece, swap(piece, "ctx", 2), swap(piece, "ctx", 4)]
+    far = swap(piece, "ctx", 4)
+    return [piece, swap(piece, "ctx", 2), far]
 
 
 def corners(found, turn):
@@ -43,18 +45,23 @@
     group = depth // kv_width
     length = keys.shape[0]
     owners = [(tp ^ k) * blocks + 2 * b + lax.rem(ctx, 2) for k in ks for b in range(blocks // 2)]
+    half = depth // 2
+    for h in range(kv_heads):
+        values[:, (2 * h + 1) * HD : 2 * (h + 1) * HD] = jnp.ones((length, HD), BF16)
     for j in range(chips):
-        asked, kv = refs[2 * j], refs[2 * j + 1]
+        low, high = refs[2 * j], refs[2 * j + 1]
         own_at = pl.ds(pl.multiple_of((ctx ^ (2 * j)) * own_rows, own_rows), own_rows)
         sib_at = pl.ds(pl.multiple_of((ctx ^ (2 * j + 1)) * own_rows, own_rows), own_rows)
-        for rows, first in ((own_at, 0), (sib_at, 2 * kv_width)):
-            keys[rows, :] = kv[:, first : first + kv_width]
-            values[rows, :] = kv[:, first + kv_width : first + 2 * kv_width]
+        for rows, first in ((own_at, half), (sib_at, half + kv_width)):
+            keys[rows, :] = low[:, first : first + kv_width]
+            for h in range(kv_heads):
+                values[rows, 2 * h * HD : (2 * h + 1) * HD] = high[:, first + h * HD : first + (h + 1) * HD]
         for i, owner in enumerate(owners):
 
             @pl.when(owner == (ctx ^ (2 * j)))
-            def _(asked=asked, i=i):
-                queries[i * own_rows : (i + 1) * own_rows, :] = asked[...]
+            def _(low=low, high=high, i=i):
+                queries[i * own_rows : (i + 1) * own_rows, :half] = low[:, :half]
+                queries[i * own_rows : (i + 1) * own_rows, half:] = high[:, :half]
 
     count = lens_ref.shape[1]
     first = lax.broadcasted_iota(jnp.int32, (count, count), 0)
@@ -75,14 +82,13 @@
             ).reshape(group, own_rows, length)
             scores = jnp.where(allowed, scores, NEGATIVE)
             highest = jnp.max(scores, axis=2, keepdims=True)
-            weights = jnp.exp((scores - highest) * HD ** (-0.5))
-            denominator = jnp.sum(weights, axis=2, keepdims=True).reshape(group * own_rows, 1)
+            weights = jnp.exp2((scores - highest) * (HD ** (-0.5) * LOG2E))
             mix = jnp.dot(
                 weights.reshape(group * own_rows, length).astype(BF16),
-                values[:, h * HD : (h + 1) * HD],
+                values[:, 2 * h * HD : 2 * (h + 1) * HD],
                 preferred_element_type=F32,
             )
-            mix = (mix / denominator).astype(BF16)
+            mix = (mix[:, :HD] / mix[:, HD:]).astype(BF16)
             for g, head in enumerate(heads):
                 mixed[i * own_rows : (i + 1) * own_rows, head : head + HD] = mix[g * own_rows : (g + 1) * own_rows]
     product = jnp.dot(mixed[...], weight_ref[...], preferred_element_type=F32)
@@ -106,7 +112,7 @@
         scratch_shapes=[
             pltpu.VMEM((rows, depth), BF16),
             pltpu.VMEM((length, kv_width), BF16),
-            pltpu.VMEM((length, kv_width), BF16),
+            pltpu.VMEM((length, 2 * kv_width), BF16),
             pltpu.VMEM((rows, depth), BF16),
         ],
         compiler_params=pltpu.CompilerParams(vmem_limit_bytes=need + (8 << 20)),
@@ -290,16 +296,14 @@
     mid = tp_count // 2
     place = jnp.stack([ctx, tp, slab_start[0]]).astype(jnp.int32)
 
-    asked = sides(queries, chips)
-    kv = [key_rows, value_rows, swap(key_rows, "ctx", 1), swap(value_rows, "ctx", 1)]
-    kv = jnp.concatenate(kv, axis=1)
-    kv, out_weight, stream = lax.optimization_barrier((kv, out_weight, stream))
+    half = queries.shape[1] // 2
+    low = jnp.concatenate([queries[:, :half], key_rows, swap(key_rows, "ctx", 1)], axis=1)
+    high = jnp.concatenate([queries[:, half:], value_rows, swap(value_rows, "ctx", 1)], axis=1)
+    low, high, out_weight, stream = lax.optimization_barrier((low, high, out_weight, stream))
+    sets = list(zip(corners(sides(low, chips), 0), corners(sides(high, chips), 1)))
     out_sibling, stream_sibling = swap(out_weight, "ctx", 1), swap(stream, "ctx", 1)
     weight, mark = stage(place, out_weight, out_sibling, 1)
-    later, mark = lax.optimization_barrier((kv, mark))
-    around = [kv] + [swap(kv if j < 2 else later, "ctx", 2 * j) for j in range(1, 3 if chips == 4 else chips)]
     mark, stream_sibling = lax.optimization_barrier((mark, stream_sibling))
-    sets = list(zip(corners(asked, 0), corners(around, 1)))
 
     lens, kv_width = doc_lengths[None], key_rows.shape[1]
     far = attend(place, mark, lens, sets, kv_width, weight, range(mid, tp_count), tp_count, blocks)

time: 95.3 us -> 93.1 us (0.977)
  waiting for transfers between devices: 32.6 us -> 29 us
    ppermute x30, waiting for transfers between devices: 32.6 us -> 29 us  [swap(): return lax.ppermute(x, axis, [(i, i ^ k) for i in range(size)])]
    slice x0 -> x1, local copies, waits for them, and re-layouts: none -> 0.98 us  [local(): queries[:, half:]]
    unnamed x18 -> x12, local copies, waits for them, and re-layouts: 2.46 us -> 1.77 us
  transfers between devices with their start and end apart: 30 -> 30, of which waited for: 16 -> 13; matrix products, arithmetic and copies ran while one was open for 0% -> 2% of each run, Pallas kernels for 12% -> 12%
where the time goes in v4:
time: 93.1 us; the launch traced here: 92.6 us
  waiting for transfers between devices  29 us (31%)
  starting transfers between devices  28.1 us (30%)
  Pallas kernels  19.6 us (21%)
  blocking collectives  10.1 us (11%)
  local copies, waits for them, and re-layouts  2.77 us (3%)
  other arithmetic  1.66 us (2%)
  between operations  1.45 us (2%)
    ppermute x30, waiting for transfers between devices, swap(): return lax.ppermute(x, axis, [(i, i ^ k) for i in range(size)])  29 us
    ppermute x30, starting transfers between devices, swap(): return lax.ppermute(x, axis, [(i, i ^ k) for i in range(size)])  28.1 us
    all_to_all x1, blocking collectives, local(): stats = lax.all_to_all(stats, ('ctx', 'tp'), 0, 0, tiled=True)  10.1 us
    pallas_call x2, Pallas kernels, attend(): pl.pallas_call(lambda *refs: attend_kernel(chips, tp_count, own_rows, kv_...  8.01 us
    pallas_call x2, Pallas kernels, stage(): pl.pallas_call(stage_kernel, out_shape=[jax.ShapeDtypeStruct((depth, 2 *...  4.92 us
    pallas_call x2, Pallas kernels, score(): pl.pallas_call(lambda *refs: score_kernel(chips, tp_count, own_rows, bloc...  4.5 us
  transfers between devices with their start and end apart: 30, of which 13 were waited for; matrix products, arithmetic and copies ran while one was open for 2% of the time, Pallas kernels for 12%

profile of v4, /device:TPU:0, one launch (start us, length us, event | category | flops | bytes accessed | tf_op | source)
XLA Modules:
  0.0 92.6 jit_solution(4599631497275781145)
XLA Ops:
  0.6 0.5 collective-permute-start
  1.2 0.1 collective-permute-start.1
  1.2 1.0 %fusion = (bf16[64,1024]{1,0:T(8,128)(2,1)S(1)}, bf16[64,1024]{1,0:T(8,128)(2,1)S(1)}) fusion(bf16[64,2048]{1,0:T(8,128)(2,1)} %param.11), kind=kLoop, calls=%fused_computation.3 | loop fusion | bytes 524288 | tf_op jit(solution)/shard_map/slice | solution.py:301
  2.2 0.0 collective-permute-done
  2.2 0.8 pad_maximum_fusion.refs_4_
  3.0 0.8 pad_maximum_fusion.1.refs_5_
  3.8 0.5 collective-permute-start.2
  4.3 2.6 %collective-permute-start.6 = (bf16[64,1536]{1,0:T(8,128)(2,1)S(1)}, bf16[64,1536]{1,0:T(8,128)(2,1)S(1)}, u32[]{:S(2)}, u32[]{:S(2)}) collective-permute-start(bf16[64,1536]{1,0:T(8,128)(2,1)S(1)} %pad_maximum_fusion.refs_4_), channel_id=1, source_target_pairs={{0,16},{4,20},{8,24},{12,28},{16,0},{20,4},{24,8},{28,12},{1,17},{... | collective-permute-start | bytes 589832 | tf_op jit(solution)/shard_map/ppermute | solution.py:23
  6.9 1.5 %collective-permute-start.5 = (bf16[64,1536]{1,0:T(8,128)(2,1)S(1)}, bf16[64,1536]{1,0:T(8,128)(2,1)S(1)}, u32[]{:S(2)}, u32[]{:S(2)}) collective-permute-start(bf16[64,1536]{1,0:T(8,128)(2,1)S(1)} %pad_maximum_fusion.1.refs_5_), channel_id=1, source_target_pairs={{0,8},{4,12},{8,0},{12,4},{16,24},{20,28},{24,16},{28,20},{1,9},{5... | collective-permute-start | bytes 589832 | tf_op jit(solution)/shard_map/ppermute | solution.py:23
  8.4 0.5 collective-permute-start.4
  8.9 0.1 collective-permute-start.7
  9.0 3.6 %collective-permute-done.6.refs_8_ = bf16[64,1536]{1,0:T(8,128)(2,1)S(1)} collective-permute-done((bf16[64,1536]{1,0:T(8,128)(2,1)S(1)}, bf16[64,1536]{1,0:T(8,128)(2,1)S(1)}, u32[]{:S(2)}, u32[]{:S(2)}) %collective-permute-start.6) | collective-permute-done | bytes 196640 | tf_op jit(solution)/shard_map/ppermute | solution.py:23
  12.6 1.9 %collective-permute-start.8 = (bf16[64,1536]{1,0:T(8,128)(2,1)S(1)}, bf16[64,1536]{1,0:T(8,128)(2,1)}, u32[]{:S(2)}, u32[]{:S(2)}) collective-permute-start(bf16[64,1536]{1,0:T(8,128)(2,1)S(1)} %collective-permute-done.6.refs_8_), channel_id=1, source_target_pairs={{0,8},{4,12},{8,0},{12,4},{16,24},{20,28},{24,16},{28,20},{1,9},{5... | collective-permute-start | bytes 589832 | tf_op jit(solution)/shard_map/ppermute | solution.py:23
  14.6 0.1 collective-permute-done.5.refs_7_
  14.6 1.5 %collective-permute-start.9 = (bf16[64,1536]{1,0:T(8,128)(2,1)S(1)}, bf16[64,1536]{1,0:T(8,128)(2,1)}, u32[]{:S(2)}, u32[]{:S(2)}) collective-permute-start(bf16[64,1536]{1,0:T(8,128)(2,1)S(1)} %collective-permute-done.5.refs_7_), channel_id=1, source_target_pairs={{0,16},{4,20},{8,24},{12,28},{16,0},{20,4},{24,8},{28,12},{1,17},{... | collective-permute-start | bytes 589832 | tf_op jit(solution)/shard_map/ppermute | solution.py:23
  16.1 0.0 collective-permute-done.2.sib_ref
  16.1 0.0 collective-permute-start.3
  16.7 0.1 pad_add_fusion.place_ref.refs_0_
  16.8 1.7 %copy-done = bf16[2048,640]{1,0:T(8,128)(2,1)S(1)} copy-done((bf16[2048,640]{1,0:T(8,128)(2,1)S(1)}, bf16[2048,640]{1,0:T(8,128)(2,1)}, u32[]{:S(2)}) %copy-start) | copy-done | bytes 2621464
  18.6 1.0 %stage.2 = (bf16[2048,1280]{1,0:T(8,128)(2,1)S(1)}, f32[8,128]{1,0:T(8,128)S(1)}) custom-call(s32[3]{0:T(128)S(1)} %pad_add_fusion.place_ref.refs_0_, bf16[2048,640]{1,0:T(8,128)(2,1)S(1)} %copy-done, bf16[2048,640]{1,0:T(8,128)(2,1)S(1)} %collective-permute-done.2.sib_ref), custom_call_target="tpu_custom_call" | custom-call | tf_op jit(solution)/shard_map/stage/pallas_call | solution.py:174
  19.6 0.0 collective-permute-done.3.refs_3_
  19.6 0.0 collective-permute-done.4.refs_6_
  19.6 2.8 %collective-permute-done.8.refs_10_ = bf16[64,1536]{1,0:T(8,128)(2,1)} collective-permute-done((bf16[64,1536]{1,0:T(8,128)(2,1)S(1)}, bf16[64,1536]{1,0:T(8,128)(2,1)}, u32[]{:S(2)}, u32[]{:S(2)}) %collective-permute-start.8) | collective-permute-done | bytes 196640 | tf_op jit(solution)/shard_map/ppermute | solution.py:23
  22.4 0.0 collective-permute-done.9.refs_11_
  22.4 4.0 %attend.2 = (bf16[64,1280]{1,0:T(8,128)(2,1)S(1)}, bf16[64,1280]{1,0:T(8,128)(2,1)S(1)}) custom-call(s32[3]{0:T(128)S(1)} %pad_add_fusion.place_ref.refs_0_, f32[8,128]{1,0:T(8,128)S(1)} %get-tuple-element.38.refs_1_, s32[1,64]{1,0:T(1,128)S(1)} %bitcast.9, bf16[2048,1280]{1,0:T(8,128)(2,1)S(1)} %get-tuple-element.39.refs_3_, ...), custom_call_target="tpu_custom_call" | custom-call | tf_op jit(solution)/shard_map/attend/pallas_call | solution.py:107
  26.4 0.0 copy-start.5
  26.4 0.0 copy-start.1
  26.4 0.1 collective-permute-start.10
  26.5 2.7 %collective-permute-start.12 = (bf16[64,1280]{1,0:T(8,128)(2,1)S(1)}, bf16[64,1280]{1,0:T(8,128)(2,1)S(1)}, u32[]{:S(2)}, u32[]{:S(2)}) collective-permute-start(bf16[64,1280]{1,0:T(8,128)(2,1)S(1)} %get-tuple-element.44.refs_1_), channel_id=1, source_target_pairs={{0,2},{1,3},{2,0},{3,1},{4,6},{5,7},{6,4},{7,5},{8,10},{9,11},{10,... | collective-permute-start | bytes 491528 | tf_op jit(solution)/shard_map/ppermute | solution.py:23
  29.2 4.0 %attend.3 = (f32[64,1280]{1,0:T(8,128)S(1)}, bf16[64,1280]{1,0:T(8,128)(2,1)S(1)}) custom-call(s32[3]{0:T(128)S(1)} %pad_add_fusion.place_ref.refs_0_, bf16[64,1280]{1,0:T(8,128)(2,1)S(1)} %get-tuple-element.44.refs_1_, s32[1,64]{1,0:T(1,128)S(1)} %bitcast.10, bf16[2048,1280]{1,0:T(8,128)(2,1)S(1)} %get-tuple-element.39.refs_3_, ...), custom_call_target="tpu_custom_call" | custom-call | tf_op jit(solution)/shard_map/attend/pallas_call | solution.py:107
  33.2 1.6 %collective-permute-start.11 = (bf16[64,1280]{1,0:T(8,128)(2,1)S(1)}, bf16[64,1280]{1,0:T(8,128)(2,1)S(1)}, u32[]{:S(2)}, u32[]{:S(2)}) collective-permute-start(bf16[64,1280]{1,0:T(8,128)(2,1)S(1)} %get-tuple-element.52), channel_id=1, source_target_pairs={{0,1},{1,0},{2,3},{3,2},{4,5},{5,4},{6,7},{7,6},{8,9},{9,8},{10,11... | collective-permute-start | bytes 491528 | tf_op jit(solution)/shard_map/ppermute | solution.py:23
  34.8 0.2 collective-permute-start.13
  35.1 9.5 %collective-permute-done.11.refs_5_ = bf16[64,1280]{1,0:T(8,128)(2,1)S(1)} collective-permute-done((bf16[64,1280]{1,0:T(8,128)(2,1)S(1)}, bf16[64,1280]{1,0:T(8,128)(2,1)S(1)}, u32[]{:S(2)}, u32[]{:S(2)}) %collective-permute-start.11) | collective-permute-done | bytes 163872 | tf_op jit(solution)/shard_map/ppermute | solution.py:23
  44.6 1.0 %update.1 = (bf16[64,1280]{1,0:T(8,128)(2,1)S(1)}, f32[8,128]{1,0:T(8,128)S(1)}) custom-call(s32[3]{0:T(128)S(1)} %pad_add_fusion.place_ref.refs_0_, f32[64,1280]{1,0:T(8,128)S(1)} %get-tuple-element.50.refs_1_.refs_4_, bf16[128,640]{1,0:T(8,128)(2,1)S(1)} %copy-done.1, bf16[128,640]{1,0:T(8,128)(2,1)} %collective-permute-done.3.refs_3_, ...), custom_call_target="tpu_custom_call" | custom-call | tf_op jit(solution)/shard_map/update/pallas_call | solution.py:140
  45.6 2.7 %collective-permute-start.15 = (bf16[64,1280]{1,0:T(8,128)(2,1)S(1)}, bf16[64,1280]{1,0:T(8,128)(2,1)S(1)}, u32[]{:S(2)}, u32[]{:S(2)}) collective-permute-start(bf16[64,1280]{1,0:T(8,128)(2,1)S(1)} %get-tuple-element.64.refs_6_), channel_id=1, source_target_pairs={{0,2},{1,3},{2,0},{3,1},{4,6},{5,7},{6,4},{7,5},{8,10},{9,11},{10,... | collective-permute-start | bytes 491528 | tf_op jit(solution)/shard_map/ppermute | solution.py:23
  48.3 1.2 %collective-permute-start.19 = (bf16[64,1280]{1,0:T(8,128)(2,1)S(1)}, bf16[64,1280]{1,0:T(8,128)(2,1)S(1)}, u32[]{:S(2)}, u32[]{:S(2)}) collective-permute-start(bf16[64,1280]{1,0:T(8,128)(2,1)S(1)} %get-tuple-element.64.refs_6_), channel_id=1, source_target_pairs={{0,1},{1,0},{2,3},{3,2},{4,5},{5,4},{6,7},{7,6},{8,9},{9,8},{10,11... | collective-permute-start | bytes 491528 | tf_op jit(solution)/shard_map/ppermute | solution.py:23
  49.5 0.5 collective-permute-start.17
  50.0 1.5 %collective-permute-start.16 = (bf16[64,1280]{1,0:T(8,128)(2,1)S(1)}, bf16[64,1280]{1,0:T(8,128)(2,1)S(1)}, u32[]{:S(2)}, u32[]{:S(2)}) collective-permute-start(bf16[64,1280]{1,0:T(8,128)(2,1)S(1)} %get-tuple-element.64.refs_6_), channel_id=1, source_target_pairs={{0,8},{4,12},{8,0},{12,4},{16,24},{20,28},{24,16},{28,20},{1,9},{5... | collective-permute-start | bytes 491528 | tf_op jit(solution)/shard_map/ppermute | solution.py:23
  51.5 3.9 %stage.3 = (bf16[5120,768]{1,0:T(8,128)(2,1)S(1)}, f32[8,128]{1,0:T(8,128)S(1)}) custom-call(s32[3]{0:T(128)S(1)} %pad_add_fusion.place_ref.refs_0_, bf16[5120,384]{1,0:T(8,128)(2,1)} %own_ref.1, bf16[5120,384]{1,0:T(8,128)(2,1)} %collective-permute-done.10.sib_ref), custom_call_target="tpu_custom_call" | custom-call | tf_op jit(solution)/shard_map/stage/pallas_call | solution.py:174
  55.4 1.0 %collective-permute-done.15.refs_6_ = bf16[64,1280]{1,0:T(8,128)(2,1)S(1)} collective-permute-done((bf16[64,1280]{1,0:T(8,128)(2,1)S(1)}, bf16[64,1280]{1,0:T(8,128)(2,1)S(1)}, u32[]{:S(2)}, u32[]{:S(2)}) %collective-permute-start.15) | collective-permute-done | bytes 163872 | tf_op jit(solution)/shard_map/ppermute | solution.py:23
  56.4 0.3 collective-permute-start.26
  56.6 1.4 %collective-permute-done.19.refs_10_ = bf16[64,1280]{1,0:T(8,128)(2,1)S(1)} collective-permute-done((bf16[64,1280]{1,0:T(8,128)(2,1)S(1)}, bf16[64,1280]{1,0:T(8,128)(2,1)S(1)}, u32[]{:S(2)}, u32[]{:S(2)}) %collective-permute-start.19) | collective-permute-done | bytes 163872 | tf_op jit(solution)/shard_map/ppermute | solution.py:23
  58.0 1.5 %collective-permute-start.20 = (bf16[64,1280]{1,0:T(8,128)(2,1)S(1)}, bf16[64,1280]{1,0:T(8,128)(2,1)S(1)}, u32[]{:S(2)}, u32[]{:S(2)}) collective-permute-start(bf16[64,1280]{1,0:T(8,128)(2,1)S(1)} %collective-permute-done.19.refs_10_), channel_id=1, source_target_pairs={{0,8},{4,12},{8,0},{12,4},{16,24},{20,28},{24,16},{28,20},{1,9},{5... | collective-permute-start | bytes 491528 | tf_op jit(solution)/shard_map/ppermute | solution.py:23
  59.5 0.5 collective-permute-start.24
  60.0 1.6 %collective-permute-start.21 = (bf16[64,1280]{1,0:T(8,128)(2,1)S(1)}, bf16[64,1280]{1,0:T(8,128)(2,1)S(1)}, u32[]{:S(2)}, u32[]{:S(2)}) collective-permute-start(bf16[64,1280]{1,0:T(8,128)(2,1)S(1)} %collective-permute-done.19.refs_10_), channel_id=1, source_target_pairs={{0,16},{4,20},{8,24},{12,28},{16,0},{20,4},{24,8},{28,12},{1,17},{... | collective-permute-start | bytes 491528 | tf_op jit(solution)/shard_map/ppermute | solution.py:23
  61.6 0.5 collective-permute-start.18
  62.1 0.0 collective-permute-done.26.refs_10_
  62.1 1.5 %collective-permute-start.27 = (bf16[64,1280]{1,0:T(8,128)(2,1)S(1)}, bf16[64,1280]{1,0:T(8,128)(2,1)S(1)}, u32[]{:S(2)}, u32[]{:S(2)}) collective-permute-start(bf16[64,1280]{1,0:T(8,128)(2,1)S(1)} %collective-permute-done.26.refs_10_), channel_id=1, source_target_pairs={{0,8},{4,12},{8,0},{12,4},{16,24},{20,28},{24,16},{28,20},{1,9},{5... | collective-permute-start | bytes 491528 | tf_op jit(solution)/shard_map/ppermute | solution.py:23
  63.6 1.0 %collective-permute-done.20.refs_11_ = bf16[64,1280]{1,0:T(8,128)(2,1)S(1)} collective-permute-done((bf16[64,1280]{1,0:T(8,128)(2,1)S(1)}, bf16[64,1280]{1,0:T(8,128)(2,1)S(1)}, u32[]{:S(2)}, u32[]{:S(2)}) %collective-permute-start.20) | collective-permute-done | bytes 163872 | tf_op jit(solution)/shard_map/ppermute | solution.py:23
  64.6 0.6 collective-permute-start.22
  65.2 1.5 %collective-permute-done.24.refs_8_ = bf16[64,1280]{1,0:T(8,128)(2,1)S(1)} collective-permute-done((bf16[64,1280]{1,0:T(8,128)(2,1)S(1)}, bf16[64,1280]{1,0:T(8,128)(2,1)S(1)}, u32[]{:S(2)}, u32[]{:S(2)}) %collective-permute-start.24) | collective-permute-done | bytes 163872 | tf_op jit(solution)/shard_map/ppermute | solution.py:23
  66.7 0.5 collective-permute-start.23
  67.2 3.0 %collective-permute-done.21.refs_12_ = bf16[64,1280]{1,0:T(8,128)(2,1)S(1)} collective-permute-done((bf16[64,1280]{1,0:T(8,128)(2,1)S(1)}, bf16[64,1280]{1,0:T(8,128)(2,1)S(1)}, u32[]{:S(2)}, u32[]{:S(2)}) %collective-permute-start.21) | collective-permute-done | bytes 163872 | tf_op jit(solution)/shard_map/ppermute | solution.py:23
  70.2 0.5 collective-permute-start.28
  70.6 0.6 collective-permute-start.25
  71.2 1.0 %collective-permute-done.27.refs_11_ = bf16[64,1280]{1,0:T(8,128)(2,1)S(1)} collective-permute-done((bf16[64,1280]{1,0:T(8,128)(2,1)S(1)}, bf16[64,1280]{1,0:T(8,128)(2,1)S(1)}, u32[]{:S(2)}, u32[]{:S(2)}) %collective-permute-start.27) | collective-permute-done | bytes 163872 | tf_op jit(solution)/shard_map/ppermute | solution.py:23
  72.2 0.5 collective-permute-start.29
  72.7 1.0 %collective-permute-done.22.refs_13_ = bf16[64,1280]{1,0:T(8,128)(2,1)S(1)} collective-permute-done((bf16[64,1280]{1,0:T(8,128)(2,1)S(1)}, bf16[64,1280]{1,0:T(8,128)(2,1)S(1)}, u32[]{:S(2)}, u32[]{:S(2)}) %collective-permute-start.22) | collective-permute-done | bytes 163872 | tf_op jit(solution)/shard_map/ppermute | solution.py:23
  73.7 2.3 %score.2 = f32[32,8,128]{2,1,0:T(8,128)S(1)} custom-call(s32[3]{0:T(128)S(1)} %pad_add_fusion.place_ref.refs_0_, f32[8,128]{1,0:T(8,128)S(1)} %collective-permute-done.14.refs_1_, f32[8,128]{1,0:T(8,128)S(1)} %get-tuple-element.60.refs_2_, s32[1,512]{1,0:T(1,128)S(1)} %bitcast.7, f32[8,640]{1,0:T(8,128)S(1)} %reshape.13.refs_4_, ...), custom_call_target="tpu_custom_call" | custom-call | tf_op jit(solution)/shard_map/score/pallas_call | solution.py:235
  75.9 2.0 %collective-permute-done.25.refs_9_ = bf16[64,1280]{1,0:T(8,128)(2,1)S(1)} collective-permute-done((bf16[64,1280]{1,0:T(8,128)(2,1)S(1)}, bf16[64,1280]{1,0:T(8,128)(2,1)S(1)}, u32[]{:S(2)}, u32[]{:S(2)}) %collective-permute-start.25) | collective-permute-done | bytes 163872 | tf_op jit(solution)/shard_map/ppermute | solution.py:23
  77.9 1.2 %collective-permute-done.29.refs_13_ = bf16[64,1280]{1,0:T(8,128)(2,1)S(1)} collective-permute-done((bf16[64,1280]{1,0:T(8,128)(2,1)S(1)}, bf16[64,1280]{1,0:T(8,128)(2,1)S(1)}, u32[]{:S(2)}, u32[]{:S(2)}) %collective-permute-start.29) | collective-permute-done | bytes 163872 | tf_op jit(solution)/shard_map/ppermute | solution.py:23
  79.1 2.2 %score.3 = f32[32,8,128]{2,1,0:T(8,128)S(1)} custom-call(s32[3]{0:T(128)S(1)} %pad_add_fusion.place_ref.refs_0_, f32[8,128]{1,0:T(8,128)S(1)} %collective-permute-done.14.refs_1_, f32[8,128]{1,0:T(8,128)S(1)} %get-tuple-element.60.refs_2_, s32[1,512]{1,0:T(1,128)S(1)} %bitcast.8, f32[8,640]{1,0:T(8,128)S(1)} %reshape.13.refs_4_, ...), custom_call_target="tpu_custom_call" | custom-call | tf_op jit(solution)/shard_map/score/pallas_call | solution.py:235
  81.4 10.1 %all_to_all.5.refs_2_ = f32[32,8,128]{2,1,0:T(8,128)S(1)} all-to-all(f32[32,8,128]{2,1,0:T(8,128)S(1)} %add.3), channel_id=1, replica_groups=mesh['ctx'=8,'tp'=4] {'ctx','tp'}, dimensions={0} | all-to-all | bytes 262144 | tf_op jit(solution)/shard_map/all_to_all | solution.py:333
  91.5 1.1 %merge.1 = (f32[1,64]{1,0:T(1,128)}, f32[1,64]{1,0:T(1,128)}) custom-call(s32[3]{0:T(128)S(1)} %pad_add_fusion.place_ref.refs_0_, f32[1,64]{1,0:T(1,128)S(1)} %bitcast.11, f32[32,8,128]{2,1,0:T(8,128)S(1)} %all_to_all.5.refs_2_), custom_call_target="tpu_custom_call" | custom-call | tf_op jit(solution)/shard_map/merge/pallas_call | solution.py:268
  (23 shorter events, 0.1 us)
Async XLA Ops:
  0.6 21.8 %copy-start.3 = (s32[64]{0:T(128)S(1)}, s32[64]{0:T(128)}, u32[]{:S(2)}) copy-start(s32[64]{0:T(128)} %param.20) | copy-start | bytes 772
  0.6 1.6 %collective-permute-start = (bf16[64,256]{1,0:T(8,128)(2,1)}, bf16[64,256]{1,0:T(8,128)(2,1)S(1)}, u32[]{:S(2)}, u32[]{:S(2)}) collective-permute-start(bf16[64,256]{1,0:T(8,128)(2,1)} %param.12), channel_id=1, source_target_pairs={{0,4},{4,0},{8,12},{12,8},{16,20},{20,16},{24,28},{28,24},{1,5},{5... | collective-permute-start | bytes 98312 | tf_op jit(solution)/shard_map/ppermute | solution.py:23
  1.2 1.9 %collective-permute-start.1 = (bf16[64,256]{1,0:T(8,128)(2,1)}, bf16[64,256]{1,0:T(8,128)(2,1)S(1)}, u32[]{:S(2)}, u32[]{:S(2)}) collective-permute-start(bf16[64,256]{1,0:T(8,128)(2,1)} %param.13), channel_id=1, source_target_pairs={{0,4},{4,0},{8,12},{12,8},{16,20},{20,16},{24,28},{28,24},{1,5},{5... | collective-permute-start | bytes 98312 | tf_op jit(solution)/shard_map/ppermute | solution.py:23
  3.8 12.3 %collective-permute-start.2 = (bf16[2048,640]{1,0:T(8,128)(2,1)}, bf16[2048,640]{1,0:T(8,128)(2,1)S(1)}, u32[]{:S(2)}, u32[]{:S(2)}) collective-permute-start(bf16[2048,640]{1,0:T(8,128)(2,1)} %own_ref), channel_id=1, source_target_pairs={{0,4},{4,0},{8,12},{12,8},{16,20},{20,16},{24,28},{28,24},{1,5},{5... | collective-permute-start | bytes 7864328 | tf_op jit(solution)/shard_map/ppermute | solution.py:23
  4.3 8.4 %collective-permute-start.6 = (bf16[64,1536]{1,0:T(8,128)(2,1)S(1)}, bf16[64,1536]{1,0:T(8,128)(2,1)S(1)}, u32[]{:S(2)}, u32[]{:S(2)}) collective-permute-start(bf16[64,1536]{1,0:T(8,128)(2,1)S(1)} %pad_maximum_fusion.refs_4_), channel_id=1, source_target_pairs={{0,16},{4,20},{8,24},{12,28},{16,0},{20,4},{24,8},{28,12},{1,17},{... | collective-permute-start | bytes 589832 | tf_op jit(solution)/shard_map/ppermute | solution.py:23
  6.9 7.7 %collective-permute-start.5 = (bf16[64,1536]{1,0:T(8,128)(2,1)S(1)}, bf16[64,1536]{1,0:T(8,128)(2,1)S(1)}, u32[]{:S(2)}, u32[]{:S(2)}) collective-permute-start(bf16[64,1536]{1,0:T(8,128)(2,1)S(1)} %pad_maximum_fusion.1.refs_5_), channel_id=1, source_target_pairs={{0,8},{4,12},{8,0},{12,4},{16,24},{20,28},{24,16},{28,20},{1,9},{5... | collective-permute-start | bytes 589832 | tf_op jit(solution)/shard_map/ppermute | solution.py:23
  8.4 11.2 %collective-permute-start.4 = (bf16[64,1536]{1,0:T(8,128)(2,1)S(1)}, bf16[64,1536]{1,0:T(8,128)(2,1)}, u32[]{:S(2)}, u32[]{:S(2)}) collective-permute-start(bf16[64,1536]{1,0:T(8,128)(2,1)S(1)} %pad_maximum_fusion.refs_4_), channel_id=1, source_target_pairs={{0,8},{4,12},{8,0},{12,4},{16,24},{20,28},{24,16},{28,20},{1,9},{5... | collective-permute-start | bytes 589832 | tf_op jit(solution)/shard_map/ppermute | solution.py:23
  8.9 10.7 %collective-permute-start.7 = (bf16[64,1536]{1,0:T(8,128)(2,1)S(1)}, bf16[64,1536]{1,0:T(8,128)(2,1)}, u32[]{:S(2)}, u32[]{:S(2)}) collective-permute-start(bf16[64,1536]{1,0:T(8,128)(2,1)S(1)} %pad_maximum_fusion.1.refs_5_), channel_id=1, source_target_pairs={{0,16},{4,20},{8,24},{12,28},{16,0},{20,4},{24,8},{28,12},{1,17},{... | collective-permute-start | bytes 589832 | tf_op jit(solution)/shard_map/ppermute | solution.py:23
  12.6 9.7 %collective-permute-start.8 = (bf16[64,1536]{1,0:T(8,128)(2,1)S(1)}, bf16[64,1536]{1,0:T(8,128)(2,1)}, u32[]{:S(2)}, u32[]{:S(2)}) collective-permute-start(bf16[64,1536]{1,0:T(8,128)(2,1)S(1)} %collective-permute-done.6.refs_8_), channel_id=1, source_target_pairs={{0,8},{4,12},{8,0},{12,4},{16,24},{20,28},{24,16},{28,20},{1,9},{5... | collective-permute-start | bytes 589832 | tf_op jit(solution)/shard_map/ppermute | solution.py:23
  14.6 7.8 %collective-permute-start.9 = (bf16[64,1536]{1,0:T(8,128)(2,1)S(1)}, bf16[64,1536]{1,0:T(8,128)(2,1)}, u32[]{:S(2)}, u32[]{:S(2)}) collective-permute-start(bf16[64,1536]{1,0:T(8,128)(2,1)S(1)} %collective-permute-done.5.refs_7_), channel_id=1, source_target_pairs={{0,16},{4,20},{8,24},{12,28},{16,0},{20,4},{24,8},{28,12},{1,17},{... | collective-permute-start | bytes 589832 | tf_op jit(solution)/shard_map/ppermute | solution.py:23
  16.1 3.5 %collective-permute-start.3 = (bf16[128,640]{1,0:T(8,128)(2,1)}, bf16[128,640]{1,0:T(8,128)(2,1)}, u32[]{:S(2)}, u32[]{:S(2)}) collective-permute-start(bf16[128,640]{1,0:T(8,128)(2,1)} %refs_2_), channel_id=1, source_target_pairs={{0,4},{4,0},{8,12},{12,8},{16,20},{20,16},{24,28},{28,24},{1,5},{5... | collective-permute-start | bytes 491528 | tf_op jit(solution)/shard_map/ppermute | solution.py:23
  16.8 1.7 %copy-start = (bf16[2048,640]{1,0:T(8,128)(2,1)S(1)}, bf16[2048,640]{1,0:T(8,128)(2,1)}, u32[]{:S(2)}) copy-start(bf16[2048,640]{1,0:T(8,128)(2,1)} %own_ref) | copy-start | bytes 7864324
  26.4 8.6 %copy-start.5 = (bf16[5120]{0:T(1024)(128)(2,1)S(1)}, bf16[5120]{0:T(1024)(128)(2,1)}, u32[]{:S(2)}) copy-start(bf16[5120]{0:T(1024)(128)(2,1)} %param.16) | copy-start | bytes 30724
  26.4 18.1 %copy-start.1 = (bf16[128,640]{1,0:T(8,128)(2,1)S(1)}, bf16[128,640]{1,0:T(8,128)(2,1)}, u32[]{:S(2)}) copy-start(bf16[128,640]{1,0:T(8,128)(2,1)} %refs_2_) | copy-start | bytes 491524
  26.4 8.6 %collective-permute-start.10 = (bf16[5120,384]{1,0:T(8,128)(2,1)}, bf16[5120,384]{1,0:T(8,128)(2,1)}, u32[]{:S(2)}, u32[]{:S(2)}) collective-permute-start(bf16[5120,384]{1,0:T(8,128)(2,1)} %own_ref.1), channel_id=1, source_target_pairs={{0,4},{4,0},{8,12},{12,8},{16,20},{20,16},{24,28},{28,24},{1,5},{5... | collective-permute-start | bytes 11796488 | tf_op jit(solution)/shard_map/ppermute | solution.py:23
  26.5 18.0 %collective-permute-start.12 = (bf16[64,1280]{1,0:T(8,128)(2,1)S(1)}, bf16[64,1280]{1,0:T(8,128)(2,1)S(1)}, u32[]{:S(2)}, u32[]{:S(2)}) collective-permute-start(bf16[64,1280]{1,0:T(8,128)(2,1)S(1)} %get-tuple-element.44.refs_1_), channel_id=1, source_target_pairs={{0,2},{1,3},{2,0},{3,1},{4,6},{5,7},{6,4},{7,5},{8,10},{9,11},{10,... | collective-permute-start | bytes 491528 | tf_op jit(solution)/shard_map/ppermute | solution.py:23
  33.2 11.4 %collective-permute-start.11 = (bf16[64,1280]{1,0:T(8,128)(2,1)S(1)}, bf16[64,1280]{1,0:T(8,128)(2,1)S(1)}, u32[]{:S(2)}, u32[]{:S(2)}) collective-permute-start(bf16[64,1280]{1,0:T(8,128)(2,1)S(1)} %get-tuple-element.52), channel_id=1, source_target_pairs={{0,1},{1,0},{2,3},{3,2},{4,5},{5,4},{6,7},{7,6},{8,9},{9,8},{10,11... | collective-permute-start | bytes 491528 | tf_op jit(solution)/shard_map/ppermute | solution.py:23
  34.8 9.7 %collective-permute-start.13 = (bf16[64,1280]{1,0:T(8,128)(2,1)S(1)}, bf16[64,1280]{1,0:T(8,128)(2,1)S(1)}, u32[]{:S(2)}, u32[]{:S(2)}) collective-permute-start(bf16[64,1280]{1,0:T(8,128)(2,1)S(1)} %get-tuple-element.53), channel_id=1, source_target_pairs={{0,3},{1,2},{2,1},{3,0},{4,7},{5,6},{6,5},{7,4},{8,11},{9,10},{10,... | collective-permute-start | bytes 491528 | tf_op jit(solution)/shard_map/ppermute | solution.py:23
  45.6 10.7 %collective-permute-start.15 = (bf16[64,1280]{1,0:T(8,128)(2,1)S(1)}, bf16[64,1280]{1,0:T(8,128)(2,1)S(1)}, u32[]{:S(2)}, u32[]{:S(2)}) collective-permute-start(bf16[64,1280]{1,0:T(8,128)(2,1)S(1)} %get-tuple-element.64.refs_6_), channel_id=1, source_target_pairs={{0,2},{1,3},{2,0},{3,1},{4,6},{5,7},{6,4},{7,5},{8,10},{9,11},{10,... | collective-permute-start | bytes 491528 | tf_op jit(solution)/shard_map/ppermute | solution.py:23
  48.3 25.4 %copy-start.2 = (s32[512]{0:T(512)S(1)}, s32[512]{0:T(512)}, u32[]{:S(2)}) copy-start(s32[512]{0:T(512)} %param.18) | copy-start | bytes 6148
  48.3 1.2 %collective-permute-start.14 = (f32[8,128]{1,0:T(8,128)S(1)}, f32[8,128]{1,0:T(8,128)S(1)}, u32[]{:S(2)}, u32[]{:S(2)}) collective-permute-start(f32[8,128]{1,0:T(8,128)S(1)} %get-tuple-element.55), channel_id=1, source_target_pairs={{0,4},{4,0},{8,12},{12,8},{16,20},{20,16},{24,28},{28,24},{1,5},{5... | collective-permute-start | bytes 12296 | tf_op jit(solution)/shard_map/ppermute | solution.py:23
  48.3 9.7 %collective-permute-start.19 = (bf16[64,1280]{1,0:T(8,128)(2,1)S(1)}, bf16[64,1280]{1,0:T(8,128)(2,1)S(1)}, u32[]{:S(2)}, u32[]{:S(2)}) collective-permute-start(bf16[64,1280]{1,0:T(8,128)(2,1)S(1)} %get-tuple-element.64.refs_6_), channel_id=1, source_target_pairs={{0,1},{1,0},{2,3},{3,2},{4,5},{5,4},{6,7},{7,6},{8,9},{9,8},{10,11... | collective-permute-start | bytes 491528 | tf_op jit(solution)/shard_map/ppermute | solution.py:23
  49.5 10.5 %collective-permute-start.17 = (bf16[64,1280]{1,0:T(8,128)(2,1)S(1)}, bf16[64,1280]{1,0:T(8,128)(2,1)S(1)}, u32[]{:S(2)}, u32[]{:S(2)}) collective-permute-start(bf16[64,1280]{1,0:T(8,128)(2,1)S(1)} %get-tuple-element.64.refs_6_), channel_id=1, source_target_pairs={{0,16},{4,20},{8,24},{12,28},{16,0},{20,4},{24,8},{28,12},{1,17},{... | collective-permute-start | bytes 491528 | tf_op jit(solution)/shard_map/ppermute | solution.py:23
  50.0 11.6 %collective-permute-start.16 = (bf16[64,1280]{1,0:T(8,128)(2,1)S(1)}, bf16[64,1280]{1,0:T(8,128)(2,1)S(1)}, u32[]{:S(2)}, u32[]{:S(2)}) collective-permute-start(bf16[64,1280]{1,0:T(8,128)(2,1)S(1)} %get-tuple-element.64.refs_6_), channel_id=1, source_target_pairs={{0,8},{4,12},{8,0},{12,4},{16,24},{20,28},{24,16},{28,20},{1,9},{5... | collective-permute-start | bytes 491528 | tf_op jit(solution)/shard_map/ppermute | solution.py:23
  56.4 5.8 %collective-permute-start.26 = (bf16[64,1280]{1,0:T(8,128)(2,1)S(1)}, bf16[64,1280]{1,0:T(8,128)(2,1)S(1)}, u32[]{:S(2)}, u32[]{:S(2)}) collective-permute-start(bf16[64,1280]{1,0:T(8,128)(2,1)S(1)} %collective-permute-done.15.refs_6_), channel_id=1, source_target_pairs={{0,1},{1,0},{2,3},{3,2},{4,5},{5,4},{6,7},{7,6},{8,9},{9,8},{10,11... | collective-permute-start | bytes 491528 | tf_op jit(solution)/shard_map/ppermute | solution.py:23
  58.0 6.6 %collective-permute-start.20 = (bf16[64,1280]{1,0:T(8,128)(2,1)S(1)}, bf16[64,1280]{1,0:T(8,128)(2,1)S(1)}, u32[]{:S(2)}, u32[]{:S(2)}) collective-permute-start(bf16[64,1280]{1,0:T(8,128)(2,1)S(1)} %collective-permute-done.19.refs_10_), channel_id=1, source_target_pairs={{0,8},{4,12},{8,0},{12,4},{16,24},{20,28},{24,16},{28,20},{1,9},{5... | collective-permute-start | bytes 491528 | tf_op jit(solution)/shard_map/ppermute | solution.py:23
  59.5 7.1 %collective-permute-start.24 = (bf16[64,1280]{1,0:T(8,128)(2,1)S(1)}, bf16[64,1280]{1,0:T(8,128)(2,1)S(1)}, u32[]{:S(2)}, u32[]{:S(2)}) collective-permute-start(bf16[64,1280]{1,0:T(8,128)(2,1)S(1)} %collective-permute-done.15.refs_6_), channel_id=1, source_target_pairs={{0,16},{4,20},{8,24},{12,28},{16,0},{20,4},{24,8},{28,12},{1,17},{... | collective-permute-start | bytes 491528 | tf_op jit(solution)/shard_map/ppermute | solution.py:23
  60.0 10.2 %collective-permute-start.21 = (bf16[64,1280]{1,0:T(8,128)(2,1)S(1)}, bf16[64,1280]{1,0:T(8,128)(2,1)S(1)}, u32[]{:S(2)}, u32[]{:S(2)}) collective-permute-start(bf16[64,1280]{1,0:T(8,128)(2,1)S(1)} %collective-permute-done.19.refs_10_), channel_id=1, source_target_pairs={{0,16},{4,20},{8,24},{12,28},{16,0},{20,4},{24,8},{28,12},{1,17},{... | collective-permute-start | bytes 491528 | tf_op jit(solution)/shard_map/ppermute | solution.py:23
  61.6 9.1 %collective-permute-start.18 = (bf16[64,1280]{1,0:T(8,128)(2,1)S(1)}, bf16[64,1280]{1,0:T(8,128)(2,1)S(1)}, u32[]{:S(2)}, u32[]{:S(2)}) collective-permute-start(bf16[64,1280]{1,0:T(8,128)(2,1)S(1)} %collective-permute-done.17.refs_8_), channel_id=1, source_target_pairs={{0,8},{4,12},{8,0},{12,4},{16,24},{20,28},{24,16},{28,20},{1,9},{5... | collective-permute-start | bytes 491528 | tf_op jit(solution)/shard_map/ppermute | solution.py:23
  62.1 10.1 %collective-permute-start.27 = (bf16[64,1280]{1,0:T(8,128)(2,1)S(1)}, bf16[64,1280]{1,0:T(8,128)(2,1)S(1)}, u32[]{:S(2)}, u32[]{:S(2)}) collective-permute-start(bf16[64,1280]{1,0:T(8,128)(2,1)S(1)} %collective-permute-done.26.refs_10_), channel_id=1, source_target_pairs={{0,8},{4,12},{8,0},{12,4},{16,24},{20,28},{24,16},{28,20},{1,9},{5... | collective-permute-start | bytes 491528 | tf_op jit(solution)/shard_map/ppermute | solution.py:23
  64.6 9.1 %collective-permute-start.22 = (bf16[64,1280]{1,0:T(8,128)(2,1)S(1)}, bf16[64,1280]{1,0:T(8,128)(2,1)S(1)}, u32[]{:S(2)}, u32[]{:S(2)}) collective-permute-start(bf16[64,1280]{1,0:T(8,128)(2,1)S(1)} %collective-permute-done.20.refs_11_), channel_id=1, source_target_pairs={{0,16},{4,20},{8,24},{12,28},{16,0},{20,4},{24,8},{28,12},{1,17},{... | collective-permute-start | bytes 491528 | tf_op jit(solution)/shard_map/ppermute | solution.py:23
  66.7 9.3 %collective-permute-start.23 = (bf16[64,1280]{1,0:T(8,128)(2,1)S(1)}, bf16[64,1280]{1,0:T(8,128)(2,1)S(1)}, u32[]{:S(2)}, u32[]{:S(2)}) collective-permute-start(bf16[64,1280]{1,0:T(8,128)(2,1)S(1)} %collective-permute-done.15.refs_6_), channel_id=1, source_target_pairs={{0,8},{4,12},{8,0},{12,4},{16,24},{20,28},{24,16},{28,20},{1,9},{5... | collective-permute-start | bytes 491528 | tf_op jit(solution)/shard_map/ppermute | solution.py:23
  70.2 7.7 %collective-permute-start.28 = (bf16[64,1280]{1,0:T(8,128)(2,1)S(1)}, bf16[64,1280]{1,0:T(8,128)(2,1)S(1)}, u32[]{:S(2)}, u32[]{:S(2)}) collective-permute-start(bf16[64,1280]{1,0:T(8,128)(2,1)S(1)} %collective-permute-done.26.refs_10_), channel_id=1, source_target_pairs={{0,16},{4,20},{8,24},{12,28},{16,0},{20,4},{24,8},{28,12},{1,17},{... | collective-permute-start | bytes 491528 | tf_op jit(solution)/shard_map/ppermute | solution.py:23
  70.6 7.3 %collective-permute-start.25 = (bf16[64,1280]{1,0:T(8,128)(2,1)S(1)}, bf16[64,1280]{1,0:T(8,128)(2,1)S(1)}, u32[]{:S(2)}, u32[]{:S(2)}) collective-permute-start(bf16[64,1280]{1,0:T(8,128)(2,1)S(1)} %collective-permute-done.24.refs_8_), channel_id=1, source_target_pairs={{0,8},{4,12},{8,0},{12,4},{16,24},{20,28},{24,16},{28,20},{1,9},{5... | collective-permute-start | bytes 491528 | tf_op jit(solution)/shard_map/ppermute | solution.py:23
  72.2 6.9 %collective-permute-start.29 = (bf16[64,1280]{1,0:T(8,128)(2,1)S(1)}, bf16[64,1280]{1,0:T(8,128)(2,1)S(1)}, u32[]{:S(2)}, u32[]{:S(2)}) collective-permute-start(bf16[64,1280]{1,0:T(8,128)(2,1)S(1)} %collective-permute-done.27.refs_11_), channel_id=1, source_target_pairs={{0,16},{4,20},{8,24},{12,28},{16,0},{20,4},{24,8},{28,12},{1,17},{... | collective-permute-start | bytes 491528 | tf_op jit(solution)/shard_map/ppermute | solution.py:23
  75.9 15.6 %copy-start.4 = (f32[64]{0:T(128)S(1)}, f32[64]{0:T(128)}, u32[]{:S(2)}) copy-start(f32[64]{0:T(128)} %param.19) | copy-start | bytes 772

commit v5 on v4

--- a/solution.py
+++ b/solution.py
@@ -34,6 +34,29 @@
     if len(found) != 3:
         return found
     return [*found, swap(found[2 - turn], "ctx", 2 + 2 * turn)]
+
+
+def pack_kernel(all_ref, key_sib_ref, value_sib_ref, low_ref, high_ref):
+    width = key_sib_ref.shape[1]
+    half = (all_ref.shape[1] - 2 * width) // 2
+    for side, (out_ref, sib_ref) in enumerate(((low_ref, key_sib_ref), (high_ref, value_sib_ref))):
+        own = 2 * half + side * width
+        out_ref[:, :half] = all_ref[:, side * half : (side + 1) * half]
+        out_ref[:, half : half + width] = all_ref[:, own : own + width]
+        out_ref[:, half + width :] = sib_ref[...]
+
+
+def pack(together, key_sibling, value_sibling):
+    rows, width = key_sibling.shape
+    shape = jax.ShapeDtypeStruct((rows, together.shape[1] // 2 + width), BF16)
+    return pl.pallas_call(
+        pack_kernel,
+        out_shape=[shape, shape],
+        in_specs=[VMEM] * 3,
+        out_specs=[VMEM, VMEM],
+        compiler_params=pltpu.CompilerParams(vmem_limit_bytes=4 << 20),
+        name="pack",
+    )(together, key_sibling, value_sibling)
 
 
 def attend_kernel(chips, tp_count, own_rows, kv_width, ks, blocks, place_ref, after_ref, lens_ref, weight_ref, *refs):
@@ -184,6 +207,8 @@
 
 def score_kernel(chips, tp_count, own_rows, blocks, first, place_ref, after_ref, ready_ref, tokens_ref, gain_ref, head_ref, *refs):
     pieces, out_ref, normed = refs[:-2], refs[-2], refs[-1]
+    if first:
+        pieces, earlier_ref = pieces[:-1], pieces[-1]
     spans = len(pieces) // chips
     ctx, tp = place_ref[0], place_ref[1]
     ranks = 2 * chips
@@ -220,14 +245,14 @@
     lane = lax.broadcasted_iota(jnp.int32, (rows, 128), 1)
     packed = jnp.where(lane == 0, highest, jnp.where(lane == 1, total, jnp.where(lane == 2, target, 0.0)))
     turned = packed.T[:8]
-    out_ref[...] = jnp.zeros(out_ref.shape, F32)
+    out_ref[...] = earlier_ref[...] if first else jnp.zeros(out_ref.shape, F32)
     for i, owner in enumerate(owners):
         tile = turned[:, i * own_rows : (i + 1) * own_rows]
         for k in range(tp_count):
             out_ref[pl.ds(owner * tp_count + k, 1), :, :own_rows] = tile[None]
 
 
-def score(place, after, ready, tokens, gain, head, spans, first, tp_count, own_rows, blocks):
+def score(place, after, ready, tokens, gain, head, spans, first, earlier, tp_count, own_rows, blocks):
     chips = len(spans[0])
     rows = len(spans) * spans[0][0].shape[0]
     depth, vocab = head.shape
@@ -235,12 +260,12 @@
     return pl.pallas_call(
         lambda *refs: score_kernel(chips, tp_count, own_rows, blocks, first, *refs),
         out_shape=jax.ShapeDtypeStruct((2 * chips * tp_count, 8, 128), F32),
-        in_specs=[SMEM, ANY, ANY] + [VMEM] * (3 + len(spans) * chips),
+        in_specs=[SMEM, ANY, ANY] + [VMEM] * (3 + len(spans) * chips + len(earlier)),
         out_specs=VMEM,
         scratch_shapes=[pltpu.VMEM((rows, depth), BF16)],
         compiler_params=pltpu.CompilerParams(vmem_limit_bytes=need + (12 << 20)),
         name="score",
-    )(place, after, ready, tokens, gain, head, *[piece for span in spans for piece in span])
+    )(place, after, ready, tokens, gain, head, *[piece for span in spans for piece in span], *earlier)
 
 
 def merge_kernel(chips, tp_count, place_ref, policy_ref, stats_ref, logprob_ref, penalty_ref):
@@ -296,9 +321,8 @@
     mid = tp_count // 2
     place = jnp.stack([ctx, tp, slab_start[0]]).astype(jnp.int32)
 
-    half = queries.shape[1] // 2
-    low = jnp.concatenate([queries[:, :half], key_rows, swap(key_rows, "ctx", 1)], axis=1)
-    high = jnp.concatenate([queries[:, half:], value_rows, swap(value_rows, "ctx", 1)], axis=1)
+    together = jnp.concatenate([queries, key_rows, value_rows], axis=1)
+    low, high = pack(together, swap(key_rows, "ctx", 1), swap(value_rows, "ctx", 1))
     low, high, out_weight, stream = lax.optimization_barrier((low, high, out_weight, stream))
     sets = list(zip(corners(sides(low, chips), 0), corners(sides(high, chips), 1)))
     out_sibling, stream_sibling = swap(out_weight, "ctx", 1), swap(stream, "ctx", 1)
@@ -325,11 +349,18 @@
             pieces[k - step], ready = lax.optimization_barrier((pieces[k - step], ready))
         pieces.append(swap(pieces[k - step], "tp", step))
     for k, piece in enumerate([here] + pieces[1:]):
-        spans.append(sides(piece, chips))
-    spans = [corners(span, k % 2) for k, span in enumerate(spans)]
-    stats = score(place, mark, ready, tokens, gain, head, spans[:mid], 0, tp_count, own_rows, blocks) + score(
-        place, mark, ready, tokens, gain, head, spans[mid:], mid, tp_count, own_rows, blocks
-    )
+        if k == 1 and chips == 4:
+            spans.append([piece] + [swap(one, "tp", 1) for one in spans[0][1:]])
+        else:
+            spans.append(sides(piece, chips))
+    for k in range(tp_count):
+        if k == 1 and chips == 4:
+            spans[k].append(swap(spans[0][3], "tp", 1))
+        else:
+            spans[k] = corners(spans[k], k % 2)
+    sizes = (tp_count, own_rows, blocks)
+    stats = score(place, mark, ready, tokens, gain, head, spans[:mid], 0, [], *sizes)
+    stats = score(place, mark, ready, tokens, gain, head, spans[mid:], mid, [stats], *sizes)
     stats = lax.all_to_all(stats, ("ctx", "tp"), 0, 0, tiled=True)
     logprob, penalty = merge(place, policy_logprob[None], stats, chips, tp_count)
     return (logprob[0], penalty[0])

time: 93.1 us -> 91 us (0.977)
  waiting for transfers between devices: 29 us -> 24.7 us
  starting transfers between devices: 28.1 us -> 30.6 us
  blocking collectives: 10.1 us -> 11.6 us
  local copies, waits for them, and re-layouts: 2.77 us -> 1.79 us
    ppermute x30, waiting for transfers between devices: 29 us -> 24.7 us  [swap(): return lax.ppermute(x, axis, [(i, i ^ k) for i in range(size)])]
    ppermute x30, starting transfers between devices: 28.1 us -> 30.6 us  [swap(): return lax.ppermute(x, axis, [(i, i ^ k) for i in range(size)])]
    all_to_all x1, blocking collectives: 10.1 us -> 11.6 us  [local(): stats = lax.all_to_all(stats, ('ctx', 'tp'), 0, 0, tiled=True)]
    slice x1 -> x0, local copies, waits for them, and re-layouts: 0.98 us -> none  [local(): queries[:, half:]]
  transfers between devices with their start and end apart: 30 -> 30, of which waited for: 13 -> 12; matrix products, arithmetic and copies ran while one was open for 2% -> 1% of each run, Pallas kernels for 12% -> 12%
where the time goes in v5:
time: 91 us; the launch traced here: 90.8 us
  starting transfers between devices  30.6 us (34%)
  waiting for transfers between devices  24.7 us (27%)
  Pallas kernels  19.6 us (22%)
  blocking collectives  11.6 us (13%)
  local copies, waits for them, and re-layouts  1.79 us (2%)
  between operations  1.45 us (2%)
  other arithmetic  1.09 us (1%)
    ppermute x30, starting transfers between devices, swap(): return lax.ppermute(x, axis, [(i, i ^ k) for i in range(size)])  30.6 us
    ppermute x30, waiting for transfers between devices, swap(): return lax.ppermute(x, axis, [(i, i ^ k) for i in range(size)])  24.7 us
    all_to_all x1, blocking collectives, local(): stats = lax.all_to_all(stats, ('ctx', 'tp'), 0, 0, tiled=True)  11.6 us
    pallas_call x2, Pallas kernels, attend(): pl.pallas_call(lambda *refs: attend_kernel(chips, tp_count, own_rows, kv_...  8.01 us
    pallas_call x2, Pallas kernels, stage(): pl.pallas_call(stage_kernel, out_shape=[jax.ShapeDtypeStruct((depth, 2 *...  4.92 us
    pallas_call x2, Pallas kernels, score(): pl.pallas_call(lambda *refs: score_kernel(chips, tp_count, own_rows, bloc...  4.52 us
  transfers between devices with their start and end apart: 30, of which 12 were waited for; matrix products, arithmetic and copies ran while one was open for 1% of the time, Pallas kernels for 12%

profile of v5, /device:TPU:0, one launch (start us, length us, event | category | flops | bytes accessed | tf_op | source)
XLA Modules:
  0.0 90.8 jit_solution(878261967473239140)
XLA Ops:
  0.6 0.5 collective-permute-start
  1.2 0.1 collective-permute-start.1
  1.2 1.0 %pad_maximum_fusion.all_ref = bf16[64,2560]{1,0:T(8,128)(2,1)S(1)} fusion(bf16[64,256]{1,0:T(8,128)(2,1)} %param.13, bf16[64,256]{1,0:T(8,128)(2,1)} %param.12, bf16[64,2048]{1,0:T(8,128)(2,1)} %param.11), kind=kLoop, calls=%fused_computation | loop fusion | flops 983040 | bytes 655360 | tf_op jit(solution)/shard_map/concatenate | solution.py:324
  2.3 0.0 collective-permute-done.key_sib_ref
  2.3 0.3 collective-permute-done.1.value_sib_ref
  2.6 0.2 collective-permute-start.2
  2.8 2.9 %collective-permute-start.6 = (bf16[64,1536]{1,0:T(8,128)(2,1)S(1)}, bf16[64,1536]{1,0:T(8,128)(2,1)S(1)}, u32[]{:S(2)}, u32[]{:S(2)}) collective-permute-start(bf16[64,1536]{1,0:T(8,128)(2,1)S(1)} %get-tuple-element.44.refs_4_), channel_id=1, source_target_pairs={{0,16},{4,20},{8,24},{12,28},{16,0},{20,4},{24,8},{28,12},{1,17},{... | collective-permute-start | bytes 589832 | tf_op jit(solution)/shard_map/ppermute | solution.py:23
  5.7 1.5 %collective-permute-start.5 = (bf16[64,1536]{1,0:T(8,128)(2,1)S(1)}, bf16[64,1536]{1,0:T(8,128)(2,1)S(1)}, u32[]{:S(2)}, u32[]{:S(2)}) collective-permute-start(bf16[64,1536]{1,0:T(8,128)(2,1)S(1)} %get-tuple-element.45.refs_5_), channel_id=1, source_target_pairs={{0,8},{4,12},{8,0},{12,4},{16,24},{20,28},{24,16},{28,20},{1,9},{5... | collective-permute-start | bytes 589832 | tf_op jit(solution)/shard_map/ppermute | solution.py:23
  7.2 0.5 collective-permute-start.4
  7.7 0.0 collective-permute-start.7
  7.7 3.6 %collective-permute-done.6.refs_8_ = bf16[64,1536]{1,0:T(8,128)(2,1)S(1)} collective-permute-done((bf16[64,1536]{1,0:T(8,128)(2,1)S(1)}, bf16[64,1536]{1,0:T(8,128)(2,1)S(1)}, u32[]{:S(2)}, u32[]{:S(2)}) %collective-permute-start.6) | collective-permute-done | bytes 196640 | tf_op jit(solution)/shard_map/ppermute | solution.py:23
  11.4 2.0 %collective-permute-start.8 = (bf16[64,1536]{1,0:T(8,128)(2,1)S(1)}, bf16[64,1536]{1,0:T(8,128)(2,1)}, u32[]{:S(2)}, u32[]{:S(2)}) collective-permute-start(bf16[64,1536]{1,0:T(8,128)(2,1)S(1)} %collective-permute-done.6.refs_8_), channel_id=1, source_target_pairs={{0,8},{4,12},{8,0},{12,4},{16,24},{20,28},{24,16},{28,20},{1,9},{5... | collective-permute-start | bytes 589832 | tf_op jit(solution)/shard_map/ppermute | solution.py:23
  13.4 0.1 collective-permute-done.5.refs_7_
  13.5 1.5 %collective-permute-start.9 = (bf16[64,1536]{1,0:T(8,128)(2,1)S(1)}, bf16[64,1536]{1,0:T(8,128)(2,1)}, u32[]{:S(2)}, u32[]{:S(2)}) collective-permute-start(bf16[64,1536]{1,0:T(8,128)(2,1)S(1)} %collective-permute-done.5.refs_7_), channel_id=1, source_target_pairs={{0,16},{4,20},{8,24},{12,28},{16,0},{20,4},{24,8},{28,12},{1,17},{... | collective-permute-start | bytes 589832 | tf_op jit(solution)/shard_map/ppermute | solution.py:23
  14.9 0.0 collective-permute-done.2.sib_ref
  14.9 0.0 collective-permute-start.3
  15.6 0.1 pad_add_fusion.place_ref.refs_0_
  15.7 1.7 %copy-done = bf16[2048,640]{1,0:T(8,128)(2,1)S(1)} copy-done((bf16[2048,640]{1,0:T(8,128)(2,1)S(1)}, bf16[2048,640]{1,0:T(8,128)(2,1)}, u32[]{:S(2)}) %copy-start) | copy-done | bytes 2621464
  17.4 1.0 %stage.2 = (bf16[2048,1280]{1,0:T(8,128)(2,1)S(1)}, f32[8,128]{1,0:T(8,128)S(1)}) custom-call(s32[3]{0:T(128)S(1)} %pad_add_fusion.place_ref.refs_0_, bf16[2048,640]{1,0:T(8,128)(2,1)S(1)} %copy-done, bf16[2048,640]{1,0:T(8,128)(2,1)S(1)} %collective-permute-done.2.sib_ref), custom_call_target="tpu_custom_call" | custom-call | tf_op jit(solution)/shard_map/stage/pallas_call | solution.py:197
  18.5 0.0 collective-permute-done.4.refs_6_
  18.5 0.0 collective-permute-done.7.refs_9_
  18.5 2.4 %collective-permute-done.8.refs_10_ = bf16[64,1536]{1,0:T(8,128)(2,1)} collective-permute-done((bf16[64,1536]{1,0:T(8,128)(2,1)S(1)}, bf16[64,1536]{1,0:T(8,128)(2,1)}, u32[]{:S(2)}, u32[]{:S(2)}) %collective-permute-start.8) | collective-permute-done | bytes 196640 | tf_op jit(solution)/shard_map/ppermute | solution.py:23
  20.9 4.0 %attend.2 = (bf16[64,1280]{1,0:T(8,128)(2,1)S(1)}, bf16[64,1280]{1,0:T(8,128)(2,1)S(1)}) custom-call(s32[3]{0:T(128)S(1)} %pad_add_fusion.place_ref.refs_0_, f32[8,128]{1,0:T(8,128)S(1)} %get-tuple-element.42.refs_1_, s32[1,64]{1,0:T(1,128)S(1)} %bitcast.9, bf16[2048,1280]{1,0:T(8,128)(2,1)S(1)} %get-tuple-element.43.refs_3_, ...), custom_call_target="tpu_custom_call" | custom-call | tf_op jit(solution)/shard_map/attend/pallas_call | solution.py:130
  24.9 0.0 copy-start.5
  24.9 0.0 copy-start.1
  25.0 0.1 collective-permute-start.10
  25.0 2.7 %collective-permute-start.12 = (bf16[64,1280]{1,0:T(8,128)(2,1)S(1)}, bf16[64,1280]{1,0:T(8,128)(2,1)S(1)}, u32[]{:S(2)}, u32[]{:S(2)}) collective-permute-start(bf16[64,1280]{1,0:T(8,128)(2,1)S(1)} %get-tuple-element.48.refs_1_), channel_id=1, source_target_pairs={{0,2},{1,3},{2,0},{3,1},{4,6},{5,7},{6,4},{7,5},{8,10},{9,11},{10,... | collective-permute-start | bytes 491528 | tf_op jit(solution)/shard_map/ppermute | solution.py:23
  27.7 4.0 %attend.3 = (f32[64,1280]{1,0:T(8,128)S(1)}, bf16[64,1280]{1,0:T(8,128)(2,1)S(1)}) custom-call(s32[3]{0:T(128)S(1)} %pad_add_fusion.place_ref.refs_0_, bf16[64,1280]{1,0:T(8,128)(2,1)S(1)} %get-tuple-element.48.refs_1_, s32[1,64]{1,0:T(1,128)S(1)} %bitcast.10, bf16[2048,1280]{1,0:T(8,128)(2,1)S(1)} %get-tuple-element.43.refs_3_, ...), custom_call_target="tpu_custom_call" | custom-call | tf_op jit(solution)/shard_map/attend/pallas_call | solution.py:130
  31.7 1.6 %collective-permute-start.11 = (bf16[64,1280]{1,0:T(8,128)(2,1)S(1)}, bf16[64,1280]{1,0:T(8,128)(2,1)S(1)}, u32[]{:S(2)}, u32[]{:S(2)}) collective-permute-start(bf16[64,1280]{1,0:T(8,128)(2,1)S(1)} %get-tuple-element.56), channel_id=1, source_target_pairs={{0,1},{1,0},{2,3},{3,2},{4,5},{5,4},{6,7},{7,6},{8,9},{9,8},{10,11... | collective-permute-start | bytes 491528 | tf_op jit(solution)/shard_map/ppermute | solution.py:23
  33.3 0.2 collective-permute-start.13
  33.6 9.5 %collective-permute-done.11.refs_5_ = bf16[64,1280]{1,0:T(8,128)(2,1)S(1)} collective-permute-done((bf16[64,1280]{1,0:T(8,128)(2,1)S(1)}, bf16[64,1280]{1,0:T(8,128)(2,1)S(1)}, u32[]{:S(2)}, u32[]{:S(2)}) %collective-permute-start.11) | collective-permute-done | bytes 163872 | tf_op jit(solution)/shard_map/ppermute | solution.py:23
  43.1 1.0 %update.1 = (bf16[64,1280]{1,0:T(8,128)(2,1)S(1)}, f32[8,128]{1,0:T(8,128)S(1)}) custom-call(s32[3]{0:T(128)S(1)} %pad_add_fusion.place_ref.refs_0_, f32[64,1280]{1,0:T(8,128)S(1)} %get-tuple-element.54.refs_1_.refs_4_, bf16[128,640]{1,0:T(8,128)(2,1)S(1)} %copy-done.1, bf16[128,640]{1,0:T(8,128)(2,1)} %collective-permute-done.3.refs_3_, ...), custom_call_target="tpu_custom_call" | custom-call | tf_op jit(solution)/shard_map/update/pallas_call | solution.py:163
  44.1 2.7 %collective-permute-start.15 = (bf16[64,1280]{1,0:T(8,128)(2,1)S(1)}, bf16[64,1280]{1,0:T(8,128)(2,1)S(1)}, u32[]{:S(2)}, u32[]{:S(2)}) collective-permute-start(bf16[64,1280]{1,0:T(8,128)(2,1)S(1)} %get-tuple-element.69.refs_6_), channel_id=1, source_target_pairs={{0,2},{1,3},{2,0},{3,1},{4,6},{5,7},{6,4},{7,5},{8,10},{9,11},{10,... | collective-permute-start | bytes 491528 | tf_op jit(solution)/shard_map/ppermute | solution.py:23
  46.8 0.0 collective-permute-start.14
  46.8 1.2 %collective-permute-done.14.refs_1_ = f32[8,128]{1,0:T(8,128)S(1)} collective-permute-done((f32[8,128]{1,0:T(8,128)S(1)}, f32[8,128]{1,0:T(8,128)S(1)}, u32[]{:S(2)}, u32[]{:S(2)}) %collective-permute-start.14) | collective-permute-done | bytes 4128 | tf_op jit(solution)/shard_map/ppermute | solution.py:23
  48.0 0.5 collective-permute-start.24
  48.5 1.2 %collective-permute-start.26 = (bf16[64,1280]{1,0:T(8,128)(2,1)S(1)}, bf16[64,1280]{1,0:T(8,128)(2,1)S(1)}, u32[]{:S(2)}, u32[]{:S(2)}) collective-permute-start(bf16[64,1280]{1,0:T(8,128)(2,1)S(1)} %get-tuple-element.69.refs_6_), channel_id=1, source_target_pairs={{0,1},{1,0},{2,3},{3,2},{4,5},{5,4},{6,7},{7,6},{8,9},{9,8},{10,11... | collective-permute-start | bytes 491528 | tf_op jit(solution)/shard_map/ppermute | solution.py:23
  49.7 1.5 %collective-permute-start.23 = (bf16[64,1280]{1,0:T(8,128)(2,1)S(1)}, bf16[64,1280]{1,0:T(8,128)(2,1)S(1)}, u32[]{:S(2)}, u32[]{:S(2)}) collective-permute-start(bf16[64,1280]{1,0:T(8,128)(2,1)S(1)} %get-tuple-element.69.refs_6_), channel_id=1, source_target_pairs={{0,8},{4,12},{8,0},{12,4},{16,24},{20,28},{24,16},{28,20},{1,9},{5... | collective-permute-start | bytes 491528 | tf_op jit(solution)/shard_map/ppermute | solution.py:23
  51.2 3.9 %stage.3 = (bf16[5120,768]{1,0:T(8,128)(2,1)S(1)}, f32[8,128]{1,0:T(8,128)S(1)}) custom-call(s32[3]{0:T(128)S(1)} %pad_add_fusion.place_ref.refs_0_, bf16[5120,384]{1,0:T(8,128)(2,1)} %own_ref.1, bf16[5120,384]{1,0:T(8,128)(2,1)} %collective-permute-done.10.sib_ref), custom_call_target="tpu_custom_call" | custom-call | tf_op jit(solution)/shard_map/stage/pallas_call | solution.py:197
  55.1 0.0 collective-permute-done.15.refs_6_
  55.1 0.9 %collective-permute-start.19 = (bf16[64,1280]{1,0:T(8,128)(2,1)S(1)}, bf16[64,1280]{1,0:T(8,128)(2,1)S(1)}, u32[]{:S(2)}, u32[]{:S(2)}) collective-permute-start(bf16[64,1280]{1,0:T(8,128)(2,1)S(1)} %collective-permute-done.15.refs_6_), channel_id=1, source_target_pairs={{0,1},{1,0},{2,3},{3,2},{4,5},{5,4},{6,7},{7,6},{8,9},{9,8},{10,11... | collective-permute-start | bytes 491528 | tf_op jit(solution)/shard_map/ppermute | solution.py:23
  56.0 0.0 collective-permute-done.24.refs_8_
  56.0 0.5 collective-permute-start.25
  56.6 1.5 %collective-permute-start.17 = (bf16[64,1280]{1,0:T(8,128)(2,1)S(1)}, bf16[64,1280]{1,0:T(8,128)(2,1)S(1)}, u32[]{:S(2)}, u32[]{:S(2)}) collective-permute-start(bf16[64,1280]{1,0:T(8,128)(2,1)S(1)} %collective-permute-done.15.refs_6_), channel_id=1, source_target_pairs={{0,16},{4,20},{8,24},{12,28},{16,0},{20,4},{24,8},{28,12},{1,17},{... | collective-permute-start | bytes 491528 | tf_op jit(solution)/shard_map/ppermute | solution.py:23
  58.1 1.2 %collective-permute-start.27 = (bf16[64,1280]{1,0:T(8,128)(2,1)S(1)}, bf16[64,1280]{1,0:T(8,128)(2,1)S(1)}, u32[]{:S(2)}, u32[]{:S(2)}) collective-permute-start(bf16[64,1280]{1,0:T(8,128)(2,1)S(1)} %collective-permute-done.23.refs_7_), channel_id=1, source_target_pairs={{0,1},{1,0},{2,3},{3,2},{4,5},{5,4},{6,7},{7,6},{8,9},{9,8},{10,11... | collective-permute-start | bytes 491528 | tf_op jit(solution)/shard_map/ppermute | solution.py:23
  59.2 0.0 collective-permute-done.26.refs_10_
  59.2 0.9 collective-permute-start.28
  60.1 2.2 %collective-permute-done.19.refs_10_ = bf16[64,1280]{1,0:T(8,128)(2,1)S(1)} collective-permute-done((bf16[64,1280]{1,0:T(8,128)(2,1)S(1)}, bf16[64,1280]{1,0:T(8,128)(2,1)S(1)}, u32[]{:S(2)}, u32[]{:S(2)}) %collective-permute-start.19) | collective-permute-done | bytes 163872 | tf_op jit(solution)/shard_map/ppermute | solution.py:23
  62.3 1.2 %collective-permute-start.20 = (bf16[64,1280]{1,0:T(8,128)(2,1)S(1)}, bf16[64,1280]{1,0:T(8,128)(2,1)S(1)}, u32[]{:S(2)}, u32[]{:S(2)}) collective-permute-start(bf16[64,1280]{1,0:T(8,128)(2,1)S(1)} %collective-permute-done.19.refs_10_), channel_id=1, source_target_pairs={{0,8},{4,12},{8,0},{12,4},{16,24},{20,28},{24,16},{28,20},{1,9},{5... | collective-permute-start | bytes 491528 | tf_op jit(solution)/shard_map/ppermute | solution.py:23
  63.5 0.0 collective-permute-done.17.refs_8_
  63.5 1.1 %collective-permute-start.16 = (bf16[64,1280]{1,0:T(8,128)(2,1)S(1)}, bf16[64,1280]{1,0:T(8,128)(2,1)S(1)}, u32[]{:S(2)}, u32[]{:S(2)}) collective-permute-start(bf16[64,1280]{1,0:T(8,128)(2,1)S(1)} %collective-permute-done.15.refs_6_), channel_id=1, source_target_pairs={{0,8},{4,12},{8,0},{12,4},{16,24},{20,28},{24,16},{28,20},{1,9},{5... | collective-permute-start | bytes 491528 | tf_op jit(solution)/shard_map/ppermute | solution.py:23
  64.6 1.2 %collective-permute-done.27.refs_11_ = bf16[64,1280]{1,0:T(8,128)(2,1)S(1)} collective-permute-done((bf16[64,1280]{1,0:T(8,128)(2,1)S(1)}, bf16[64,1280]{1,0:T(8,128)(2,1)S(1)}, u32[]{:S(2)}, u32[]{:S(2)}) %collective-permute-start.27) | collective-permute-done | bytes 163872 | tf_op jit(solution)/shard_map/ppermute | solution.py:23
  65.8 1.5 %collective-permute-start.21 = (bf16[64,1280]{1,0:T(8,128)(2,1)S(1)}, bf16[64,1280]{1,0:T(8,128)(2,1)S(1)}, u32[]{:S(2)}, u32[]{:S(2)}) collective-permute-start(bf16[64,1280]{1,0:T(8,128)(2,1)S(1)} %collective-permute-done.19.refs_10_), channel_id=1, source_target_pairs={{0,16},{4,20},{8,24},{12,28},{16,0},{20,4},{24,8},{28,12},{1,17},{... | collective-permute-start | bytes 491528 | tf_op jit(solution)/shard_map/ppermute | solution.py:23
  67.3 2.0 %collective-permute-done.28.refs_12_ = bf16[64,1280]{1,0:T(8,128)(2,1)S(1)} collective-permute-done((bf16[64,1280]{1,0:T(8,128)(2,1)S(1)}, bf16[64,1280]{1,0:T(8,128)(2,1)S(1)}, u32[]{:S(2)}, u32[]{:S(2)}) %collective-permute-start.28) | collective-permute-done | bytes 163872 | tf_op jit(solution)/shard_map/ppermute | solution.py:23
  69.3 1.2 %collective-permute-start.18 = (bf16[64,1280]{1,0:T(8,128)(2,1)S(1)}, bf16[64,1280]{1,0:T(8,128)(2,1)S(1)}, u32[]{:S(2)}, u32[]{:S(2)}) collective-permute-start(bf16[64,1280]{1,0:T(8,128)(2,1)S(1)} %collective-permute-done.17.refs_8_), channel_id=1, source_target_pairs={{0,8},{4,12},{8,0},{12,4},{16,24},{20,28},{24,16},{28,20},{1,9},{5... | collective-permute-start | bytes 491528 | tf_op jit(solution)/shard_map/ppermute | solution.py:23
  70.5 0.0 collective-permute-done.20.refs_11_
  70.5 0.9 collective-permute-start.22
  71.4 0.2 collective-permute-done.29.refs_13_
  71.6 2.3 %score.2.refs_14_ = f32[32,8,128]{2,1,0:T(8,128)S(1)} custom-call(s32[3]{0:T(128)S(1)} %pad_add_fusion.place_ref.refs_0_, f32[8,128]{1,0:T(8,128)S(1)} %collective-permute-done.14.refs_1_, f32[8,128]{1,0:T(8,128)S(1)} %get-tuple-element.64.refs_2_, s32[1,512]{1,0:T(1,128)S(1)} %bitcast.7, f32[8,640]{1,0:T(8,128)S(1)} %reshape.13.refs_4_, ...), custom_call_target="tpu_custom_call" | custom-call | tf_op jit(solution)/shard_map/score/pallas_call | solution.py:260
  73.8 0.8 collective-permute-done.18.refs_9_
  74.6 1.2 %collective-permute-done.22.refs_13_ = bf16[64,1280]{1,0:T(8,128)(2,1)S(1)} collective-permute-done((bf16[64,1280]{1,0:T(8,128)(2,1)S(1)}, bf16[64,1280]{1,0:T(8,128)(2,1)S(1)}, u32[]{:S(2)}, u32[]{:S(2)}) %collective-permute-start.22) | collective-permute-done | bytes 163872 | tf_op jit(solution)/shard_map/ppermute | solution.py:23
  75.8 2.3 %score.3 = f32[32,8,128]{2,1,0:T(8,128)S(1)} custom-call(s32[3]{0:T(128)S(1)} %pad_add_fusion.place_ref.refs_0_, f32[8,128]{1,0:T(8,128)S(1)} %collective-permute-done.14.refs_1_, f32[8,128]{1,0:T(8,128)S(1)} %get-tuple-element.64.refs_2_, s32[1,512]{1,0:T(1,128)S(1)} %bitcast.8, f32[8,640]{1,0:T(8,128)S(1)} %reshape.13.refs_4_, ...), custom_call_target="tpu_custom_call" | custom-call | tf_op jit(solution)/shard_map/score/pallas_call | solution.py:260
  78.1 11.6 %all_to_all.5.refs_2_ = f32[32,8,128]{2,1,0:T(8,128)S(1)} all-to-all(f32[32,8,128]{2,1,0:T(8,128)S(1)} %score.3), channel_id=1, replica_groups=mesh['ctx'=8,'tp'=4] {'ctx','tp'}, dimensions={0} | all-to-all | bytes 262144 | tf_op jit(solution)/shard_map/all_to_all | solution.py:364
  89.6 1.1 %merge.1 = (f32[1,64]{1,0:T(1,128)}, f32[1,64]{1,0:T(1,128)}) custom-call(s32[3]{0:T(128)S(1)} %pad_add_fusion.place_ref.refs_0_, f32[1,64]{1,0:T(1,128)S(1)} %bitcast.11, f32[32,8,128]{2,1,0:T(8,128)S(1)} %all_to_all.5.refs_2_), custom_call_target="tpu_custom_call" | custom-call | tf_op jit(solution)/shard_map/merge/pallas_call | solution.py:293
  (21 shorter events, 0.1 us)
Async XLA Ops:
  0.6 20.3 %copy-start.3 = (s32[64]{0:T(128)S(1)}, s32[64]{0:T(128)}, u32[]{:S(2)}) copy-start(s32[64]{0:T(128)} %param.20) | copy-start | bytes 772
  0.6 1.6 %collective-permute-start = (bf16[64,256]{1,0:T(8,128)(2,1)}, bf16[64,256]{1,0:T(8,128)(2,1)S(1)}, u32[]{:S(2)}, u32[]{:S(2)}) collective-permute-start(bf16[64,256]{1,0:T(8,128)(2,1)} %param.12), channel_id=1, source_target_pairs={{0,4},{4,0},{8,12},{12,8},{16,20},{20,16},{24,28},{28,24},{1,5},{5... | collective-permute-start | bytes 98312 | tf_op jit(solution)/shard_map/ppermute | solution.py:23
  1.2 1.4 %collective-permute-start.1 = (bf16[64,256]{1,0:T(8,128)(2,1)}, bf16[64,256]{1,0:T(8,128)(2,1)S(1)}, u32[]{:S(2)}, u32[]{:S(2)}) collective-permute-start(bf16[64,256]{1,0:T(8,128)(2,1)} %param.13), channel_id=1, source_target_pairs={{0,4},{4,0},{8,12},{12,8},{16,20},{20,16},{24,28},{28,24},{1,5},{5... | collective-permute-start | bytes 98312 | tf_op jit(solution)/shard_map/ppermute | solution.py:23
  2.6 12.3 %collective-permute-start.2 = (bf16[2048,640]{1,0:T(8,128)(2,1)}, bf16[2048,640]{1,0:T(8,128)(2,1)S(1)}, u32[]{:S(2)}, u32[]{:S(2)}) collective-permute-start(bf16[2048,640]{1,0:T(8,128)(2,1)} %own_ref), channel_id=1, source_target_pairs={{0,4},{4,0},{8,12},{12,8},{16,20},{20,16},{24,28},{28,24},{1,5},{5... | collective-permute-start | bytes 7864328 | tf_op jit(solution)/shard_map/ppermute | solution.py:23
  2.8 8.5 %collective-permute-start.6 = (bf16[64,1536]{1,0:T(8,128)(2,1)S(1)}, bf16[64,1536]{1,0:T(8,128)(2,1)S(1)}, u32[]{:S(2)}, u32[]{:S(2)}) collective-permute-start(bf16[64,1536]{1,0:T(8,128)(2,1)S(1)} %get-tuple-element.44.refs_4_), channel_id=1, source_target_pairs={{0,16},{4,20},{8,24},{12,28},{16,0},{20,4},{24,8},{28,12},{1,17},{... | collective-permute-start | bytes 589832 | tf_op jit(solution)/shard_map/ppermute | solution.py:23
  5.7 7.8 %collective-permute-start.5 = (bf16[64,1536]{1,0:T(8,128)(2,1)S(1)}, bf16[64,1536]{1,0:T(8,128)(2,1)S(1)}, u32[]{:S(2)}, u32[]{:S(2)}) collective-permute-start(bf16[64,1536]{1,0:T(8,128)(2,1)S(1)} %get-tuple-element.45.refs_5_), channel_id=1, source_target_pairs={{0,8},{4,12},{8,0},{12,4},{16,24},{20,28},{24,16},{28,20},{1,9},{5... | collective-permute-start | bytes 589832 | tf_op jit(solution)/shard_map/ppermute | solution.py:23
  7.2 11.3 %collective-permute-start.4 = (bf16[64,1536]{1,0:T(8,128)(2,1)S(1)}, bf16[64,1536]{1,0:T(8,128)(2,1)}, u32[]{:S(2)}, u32[]{:S(2)}) collective-permute-start(bf16[64,1536]{1,0:T(8,128)(2,1)S(1)} %get-tuple-element.44.refs_4_), channel_id=1, source_target_pairs={{0,8},{4,12},{8,0},{12,4},{16,24},{20,28},{24,16},{28,20},{1,9},{5... | collective-permute-start | bytes 589832 | tf_op jit(solution)/shard_map/ppermute | solution.py:23
  7.7 10.7 %collective-permute-start.7 = (bf16[64,1536]{1,0:T(8,128)(2,1)S(1)}, bf16[64,1536]{1,0:T(8,128)(2,1)}, u32[]{:S(2)}, u32[]{:S(2)}) collective-permute-start(bf16[64,1536]{1,0:T(8,128)(2,1)S(1)} %get-tuple-element.45.refs_5_), channel_id=1, source_target_pairs={{0,16},{4,20},{8,24},{12,28},{16,0},{20,4},{24,8},{28,12},{1,17},{... | collective-permute-start | bytes 589832 | tf_op jit(solution)/shard_map/ppermute | solution.py:23
  11.4 9.5 %collective-permute-start.8 = (bf16[64,1536]{1,0:T(8,128)(2,1)S(1)}, bf16[64,1536]{1,0:T(8,128)(2,1)}, u32[]{:S(2)}, u32[]{:S(2)}) collective-permute-start(bf16[64,1536]{1,0:T(8,128)(2,1)S(1)} %collective-permute-done.6.refs_8_), channel_id=1, source_target_pairs={{0,8},{4,12},{8,0},{12,4},{16,24},{20,28},{24,16},{28,20},{1,9},{5... | collective-permute-start | bytes 589832 | tf_op jit(solution)/shard_map/ppermute | solution.py:23
  13.5 7.4 %collective-permute-start.9 = (bf16[64,1536]{1,0:T(8,128)(2,1)S(1)}, bf16[64,1536]{1,0:T(8,128)(2,1)}, u32[]{:S(2)}, u32[]{:S(2)}) collective-permute-start(bf16[64,1536]{1,0:T(8,128)(2,1)S(1)} %collective-permute-done.5.refs_7_), channel_id=1, source_target_pairs={{0,16},{4,20},{8,24},{12,28},{16,0},{20,4},{24,8},{28,12},{1,17},{... | collective-permute-start | bytes 589832 | tf_op jit(solution)/shard_map/ppermute | solution.py:23
  14.9 3.5 %collective-permute-start.3 = (bf16[128,640]{1,0:T(8,128)(2,1)}, bf16[128,640]{1,0:T(8,128)(2,1)}, u32[]{:S(2)}, u32[]{:S(2)}) collective-permute-start(bf16[128,640]{1,0:T(8,128)(2,1)} %refs_2_), channel_id=1, source_target_pairs={{0,4},{4,0},{8,12},{12,8},{16,20},{20,16},{24,28},{28,24},{1,5},{5... | collective-permute-start | bytes 491528 | tf_op jit(solution)/shard_map/ppermute | solution.py:23
  15.7 1.7 %copy-start = (bf16[2048,640]{1,0:T(8,128)(2,1)S(1)}, bf16[2048,640]{1,0:T(8,128)(2,1)}, u32[]{:S(2)}) copy-start(bf16[2048,640]{1,0:T(8,128)(2,1)} %own_ref) | copy-start | bytes 7864324
  24.9 8.6 %copy-start.5 = (bf16[5120]{0:T(1024)(128)(2,1)S(1)}, bf16[5120]{0:T(1024)(128)(2,1)}, u32[]{:S(2)}) copy-start(bf16[5120]{0:T(1024)(128)(2,1)} %param.16) | copy-start | bytes 30724
  24.9 18.1 %copy-start.1 = (bf16[128,640]{1,0:T(8,128)(2,1)S(1)}, bf16[128,640]{1,0:T(8,128)(2,1)}, u32[]{:S(2)}) copy-start(bf16[128,640]{1,0:T(8,128)(2,1)} %refs_2_) | copy-start | bytes 491524
  25.0 8.6 %collective-permute-start.10 = (bf16[5120,384]{1,0:T(8,128)(2,1)}, bf16[5120,384]{1,0:T(8,128)(2,1)}, u32[]{:S(2)}, u32[]{:S(2)}) collective-permute-start(bf16[5120,384]{1,0:T(8,128)(2,1)} %own_ref.1), channel_id=1, source_target_pairs={{0,4},{4,0},{8,12},{12,8},{16,20},{20,16},{24,28},{28,24},{1,5},{5... | collective-permute-start | bytes 11796488 | tf_op jit(solution)/shard_map/ppermute | solution.py:23
  25.0 18.0 %collective-permute-start.12 = (bf16[64,1280]{1,0:T(8,128)(2,1)S(1)}, bf16[64,1280]{1,0:T(8,128)(2,1)S(1)}, u32[]{:S(2)}, u32[]{:S(2)}) collective-permute-start(bf16[64,1280]{1,0:T(8,128)(2,1)S(1)} %get-tuple-element.48.refs_1_), channel_id=1, source_target_pairs={{0,2},{1,3},{2,0},{3,1},{4,6},{5,7},{6,4},{7,5},{8,10},{9,11},{10,... | collective-permute-start | bytes 491528 | tf_op jit(solution)/shard_map/ppermute | solution.py:23
  31.7 11.4 %collective-permute-start.11 = (bf16[64,1280]{1,0:T(8,128)(2,1)S(1)}, bf16[64,1280]{1,0:T(8,128)(2,1)S(1)}, u32[]{:S(2)}, u32[]{:S(2)}) collective-permute-start(bf16[64,1280]{1,0:T(8,128)(2,1)S(1)} %get-tuple-element.56), channel_id=1, source_target_pairs={{0,1},{1,0},{2,3},{3,2},{4,5},{5,4},{6,7},{7,6},{8,9},{9,8},{10,11... | collective-permute-start | bytes 491528 | tf_op jit(solution)/shard_map/ppermute | solution.py:23
  33.3 9.7 %collective-permute-start.13 = (bf16[64,1280]{1,0:T(8,128)(2,1)S(1)}, bf16[64,1280]{1,0:T(8,128)(2,1)S(1)}, u32[]{:S(2)}, u32[]{:S(2)}) collective-permute-start(bf16[64,1280]{1,0:T(8,128)(2,1)S(1)} %get-tuple-element.57), channel_id=1, source_target_pairs={{0,3},{1,2},{2,1},{3,0},{4,7},{5,6},{6,5},{7,4},{8,11},{9,10},{10,... | collective-permute-start | bytes 491528 | tf_op jit(solution)/shard_map/ppermute | solution.py:23
  44.1 10.9 %collective-permute-start.15 = (bf16[64,1280]{1,0:T(8,128)(2,1)S(1)}, bf16[64,1280]{1,0:T(8,128)(2,1)S(1)}, u32[]{:S(2)}, u32[]{:S(2)}) collective-permute-start(bf16[64,1280]{1,0:T(8,128)(2,1)S(1)} %get-tuple-element.69.refs_6_), channel_id=1, source_target_pairs={{0,2},{1,3},{2,0},{3,1},{4,6},{5,7},{6,4},{7,5},{8,10},{9,11},{10,... | collective-permute-start | bytes 491528 | tf_op jit(solution)/shard_map/ppermute | solution.py:23
  46.8 24.7 %copy-start.2 = (s32[512]{0:T(512)S(1)}, s32[512]{0:T(512)}, u32[]{:S(2)}) copy-start(s32[512]{0:T(512)} %param.18) | copy-start | bytes 6148
  46.8 1.2 %collective-permute-start.14 = (f32[8,128]{1,0:T(8,128)S(1)}, f32[8,128]{1,0:T(8,128)S(1)}, u32[]{:S(2)}, u32[]{:S(2)}) collective-permute-start(f32[8,128]{1,0:T(8,128)S(1)} %get-tuple-element.59), channel_id=1, source_target_pairs={{0,4},{4,0},{8,12},{12,8},{16,20},{20,16},{24,28},{28,24},{1,5},{5... | collective-permute-start | bytes 12296 | tf_op jit(solution)/shard_map/ppermute | solution.py:23
  48.0 8.0 %collective-permute-start.24 = (bf16[64,1280]{1,0:T(8,128)(2,1)S(1)}, bf16[64,1280]{1,0:T(8,128)(2,1)S(1)}, u32[]{:S(2)}, u32[]{:S(2)}) collective-permute-start(bf16[64,1280]{1,0:T(8,128)(2,1)S(1)} %get-tuple-element.69.refs_6_), channel_id=1, source_target_pairs={{0,16},{4,20},{8,24},{12,28},{16,0},{20,4},{24,8},{28,12},{1,17},{... | collective-permute-start | bytes 491528 | tf_op jit(solution)/shard_map/ppermute | solution.py:23
  48.5 10.7 %collective-permute-start.26 = (bf16[64,1280]{1,0:T(8,128)(2,1)S(1)}, bf16[64,1280]{1,0:T(8,128)(2,1)S(1)}, u32[]{:S(2)}, u32[]{:S(2)}) collective-permute-start(bf16[64,1280]{1,0:T(8,128)(2,1)S(1)} %get-tuple-element.69.refs_6_), channel_id=1, source_target_pairs={{0,1},{1,0},{2,3},{3,2},{4,5},{5,4},{6,7},{7,6},{8,9},{9,8},{10,11... | collective-permute-start | bytes 491528 | tf_op jit(solution)/shard_map/ppermute | solution.py:23
  49.7 8.4 %collective-permute-start.23 = (bf16[64,1280]{1,0:T(8,128)(2,1)S(1)}, bf16[64,1280]{1,0:T(8,128)(2,1)S(1)}, u32[]{:S(2)}, u32[]{:S(2)}) collective-permute-start(bf16[64,1280]{1,0:T(8,128)(2,1)S(1)} %get-tuple-element.69.refs_6_), channel_id=1, source_target_pairs={{0,8},{4,12},{8,0},{12,4},{16,24},{20,28},{24,16},{28,20},{1,9},{5... | collective-permute-start | bytes 491528 | tf_op jit(solution)/shard_map/ppermute | solution.py:23
  55.1 7.2 %collective-permute-start.19 = (bf16[64,1280]{1,0:T(8,128)(2,1)S(1)}, bf16[64,1280]{1,0:T(8,128)(2,1)S(1)}, u32[]{:S(2)}, u32[]{:S(2)}) collective-permute-start(bf16[64,1280]{1,0:T(8,128)(2,1)S(1)} %collective-permute-done.15.refs_6_), channel_id=1, source_target_pairs={{0,1},{1,0},{2,3},{3,2},{4,5},{5,4},{6,7},{7,6},{8,9},{9,8},{10,11... | collective-permute-start | bytes 491528 | tf_op jit(solution)/shard_map/ppermute | solution.py:23
  56.0 7.5 %collective-permute-start.25 = (bf16[64,1280]{1,0:T(8,128)(2,1)S(1)}, bf16[64,1280]{1,0:T(8,128)(2,1)S(1)}, u32[]{:S(2)}, u32[]{:S(2)}) collective-permute-start(bf16[64,1280]{1,0:T(8,128)(2,1)S(1)} %collective-permute-done.24.refs_8_), channel_id=1, source_target_pairs={{0,8},{4,12},{8,0},{12,4},{16,24},{20,28},{24,16},{28,20},{1,9},{5... | collective-permute-start | bytes 491528 | tf_op jit(solution)/shard_map/ppermute | solution.py:23
  56.6 6.9 %collective-permute-start.17 = (bf16[64,1280]{1,0:T(8,128)(2,1)S(1)}, bf16[64,1280]{1,0:T(8,128)(2,1)S(1)}, u32[]{:S(2)}, u32[]{:S(2)}) collective-permute-start(bf16[64,1280]{1,0:T(8,128)(2,1)S(1)} %collective-permute-done.15.refs_6_), channel_id=1, source_target_pairs={{0,16},{4,20},{8,24},{12,28},{16,0},{20,4},{24,8},{28,12},{1,17},{... | collective-permute-start | bytes 491528 | tf_op jit(solution)/shard_map/ppermute | solution.py:23
  58.1 7.7 %collective-permute-start.27 = (bf16[64,1280]{1,0:T(8,128)(2,1)S(1)}, bf16[64,1280]{1,0:T(8,128)(2,1)S(1)}, u32[]{:S(2)}, u32[]{:S(2)}) collective-permute-start(bf16[64,1280]{1,0:T(8,128)(2,1)S(1)} %collective-permute-done.23.refs_7_), channel_id=1, source_target_pairs={{0,1},{1,0},{2,3},{3,2},{4,5},{5,4},{6,7},{7,6},{8,9},{9,8},{10,11... | collective-permute-start | bytes 491528 | tf_op jit(solution)/shard_map/ppermute | solution.py:23
  59.2 10.1 %collective-permute-start.28 = (bf16[64,1280]{1,0:T(8,128)(2,1)S(1)}, bf16[64,1280]{1,0:T(8,128)(2,1)S(1)}, u32[]{:S(2)}, u32[]{:S(2)}) collective-permute-start(bf16[64,1280]{1,0:T(8,128)(2,1)S(1)} %collective-permute-done.24.refs_8_), channel_id=1, source_target_pairs={{0,1},{1,0},{2,3},{3,2},{4,5},{5,4},{6,7},{7,6},{8,9},{9,8},{10,11... | collective-permute-start | bytes 491528 | tf_op jit(solution)/shard_map/ppermute | solution.py:23
  62.3 8.2 %collective-permute-start.20 = (bf16[64,1280]{1,0:T(8,128)(2,1)S(1)}, bf16[64,1280]{1,0:T(8,128)(2,1)S(1)}, u32[]{:S(2)}, u32[]{:S(2)}) collective-permute-start(bf16[64,1280]{1,0:T(8,128)(2,1)S(1)} %collective-permute-done.19.refs_10_), channel_id=1, source_target_pairs={{0,8},{4,12},{8,0},{12,4},{16,24},{20,28},{24,16},{28,20},{1,9},{5... | collective-permute-start | bytes 491528 | tf_op jit(solution)/shard_map/ppermute | solution.py:23
  63.5 8.1 %collective-permute-start.29 = (bf16[64,1280]{1,0:T(8,128)(2,1)S(1)}, bf16[64,1280]{1,0:T(8,128)(2,1)S(1)}, u32[]{:S(2)}, u32[]{:S(2)}) collective-permute-start(bf16[64,1280]{1,0:T(8,128)(2,1)S(1)} %collective-permute-done.25.refs_9_), channel_id=1, source_target_pairs={{0,1},{1,0},{2,3},{3,2},{4,5},{5,4},{6,7},{7,6},{8,9},{9,8},{10,11... | collective-permute-start | bytes 491528 | tf_op jit(solution)/shard_map/ppermute | solution.py:23
  63.5 10.3 %collective-permute-start.16 = (bf16[64,1280]{1,0:T(8,128)(2,1)S(1)}, bf16[64,1280]{1,0:T(8,128)(2,1)S(1)}, u32[]{:S(2)}, u32[]{:S(2)}) collective-permute-start(bf16[64,1280]{1,0:T(8,128)(2,1)S(1)} %collective-permute-done.15.refs_6_), channel_id=1, source_target_pairs={{0,8},{4,12},{8,0},{12,4},{16,24},{20,28},{24,16},{28,20},{1,9},{5... | collective-permute-start | bytes 491528 | tf_op jit(solution)/shard_map/ppermute | solution.py:23
  65.8 8.8 %collective-permute-start.21 = (bf16[64,1280]{1,0:T(8,128)(2,1)S(1)}, bf16[64,1280]{1,0:T(8,128)(2,1)S(1)}, u32[]{:S(2)}, u32[]{:S(2)}) collective-permute-start(bf16[64,1280]{1,0:T(8,128)(2,1)S(1)} %collective-permute-done.19.refs_10_), channel_id=1, source_target_pairs={{0,16},{4,20},{8,24},{12,28},{16,0},{20,4},{24,8},{28,12},{1,17},{... | collective-permute-start | bytes 491528 | tf_op jit(solution)/shard_map/ppermute | solution.py:23
  69.3 5.3 %collective-permute-start.18 = (bf16[64,1280]{1,0:T(8,128)(2,1)S(1)}, bf16[64,1280]{1,0:T(8,128)(2,1)S(1)}, u32[]{:S(2)}, u32[]{:S(2)}) collective-permute-start(bf16[64,1280]{1,0:T(8,128)(2,1)S(1)} %collective-permute-done.17.refs_8_), channel_id=1, source_target_pairs={{0,8},{4,12},{8,0},{12,4},{16,24},{20,28},{24,16},{28,20},{1,9},{5... | collective-permute-start | bytes 491528 | tf_op jit(solution)/shard_map/ppermute | solution.py:23
  70.5 5.3 %collective-permute-start.22 = (bf16[64,1280]{1,0:T(8,128)(2,1)S(1)}, bf16[64,1280]{1,0:T(8,128)(2,1)S(1)}, u32[]{:S(2)}, u32[]{:S(2)}) collective-permute-start(bf16[64,1280]{1,0:T(8,128)(2,1)S(1)} %collective-permute-done.20.refs_11_), channel_id=1, source_target_pairs={{0,16},{4,20},{8,24},{12,28},{16,0},{20,4},{24,8},{28,12},{1,17},{... | collective-permute-start | bytes 491528 | tf_op jit(solution)/shard_map/ppermute | solution.py:23
  73.8 15.8 %copy-start.4 = (f32[64]{0:T(128)S(1)}, f32[64]{0:T(128)}, u32[]{:S(2)}) copy-start(f32[64]{0:T(128)} %param.19) | copy-start | bytes 772

commit v6 on v5

--- a/solution.py
+++ b/solution.py
@@ -244,7 +244,7 @@
     target = jnp.sum(jnp.where(column + offset == tokens, logits, 0.0), axis=1, keepdims=True)
     lane = lax.broadcasted_iota(jnp.int32, (rows, 128), 1)
     packed = jnp.where(lane == 0, highest, jnp.where(lane == 1, total, jnp.where(lane == 2, target, 0.0)))
-    turned = packed.T[:8]
+    turned = packed.T[:4]
     out_ref[...] = earlier_ref[...] if first else jnp.zeros(out_ref.shape, F32)
     for i, owner in enumerate(owners):
         tile = turned[:, i * own_rows : (i + 1) * own_rows]
@@ -259,7 +259,7 @@
     need = 2 * depth * vocab + rows * depth * 6 + rows * vocab * 4 * 8
     return pl.pallas_call(
         lambda *refs: score_kernel(chips, tp_count, own_rows, blocks, first, *refs),
-        out_shape=jax.ShapeDtypeStruct((2 * chips * tp_count, 8, 128), F32),
+        out_shape=jax.ShapeDtypeStruct((2 * chips * tp_count, 4, 128), F32),
         in_specs=[SMEM, ANY, ANY] + [VMEM] * (3 + len(spans) * chips + len(earlier)),
         out_specs=VMEM,
         scratch_shapes=[pltpu.VMEM((rows, depth), BF16)],

time: 91 us -> 90.1 us (level)
  no operation moved by 1% of the time
where the time goes in v6:
time: 90.1 us; the launch traced here: 89.9 us
  starting transfers between devices  30.6 us (34%)
  waiting for transfers between devices  24.7 us (27%)
  Pallas kernels  19.6 us (22%)
  blocking collectives  10.7 us (12%)
  local copies, waits for them, and re-layouts  1.79 us (2%)
  between operations  1.45 us (2%)
  other arithmetic  1.09 us (1%)
    ppermute x30, starting transfers between devices, swap(): return lax.ppermute(x, axis, [(i, i ^ k) for i in range(size)])  30.6 us
    ppermute x30, waiting for transfers between devices, swap(): return lax.ppermute(x, axis, [(i, i ^ k) for i in range(size)])  24.7 us
    all_to_all x1, blocking collectives, local(): stats = lax.all_to_all(stats, ('ctx', 'tp'), 0, 0, tiled=True)  10.7 us
    pallas_call x2, Pallas kernels, attend(): pl.pallas_call(lambda *refs: attend_kernel(chips, tp_count, own_rows, kv_...  8.01 us
    pallas_call x2, Pallas kernels, stage(): pl.pallas_call(stage_kernel, out_shape=[jax.ShapeDtypeStruct((depth, 2 *...  4.92 us
    pallas_call x2, Pallas kernels, score(): pl.pallas_call(lambda *refs: score_kernel(chips, tp_count, own_rows, bloc...  4.51 us
  transfers between devices with their start and end apart: 30, of which 12 were waited for; matrix products, arithmetic and copies ran while one was open for 1% of the time, Pallas kernels for 12%

profile of v6, /device:TPU:0, one launch (start us, length us, event | category | flops | bytes accessed | tf_op | source)
XLA Modules:
  0.0 89.9 jit_solution(14695544429445755663)
XLA Ops:
  0.6 0.5 collective-permute-start
  1.2 0.1 collective-permute-start.1
  1.2 1.0 %pad_maximum_fusion.all_ref = bf16[64,2560]{1,0:T(8,128)(2,1)S(1)} fusion(bf16[64,256]{1,0:T(8,128)(2,1)} %param.13, bf16[64,256]{1,0:T(8,128)(2,1)} %param.12, bf16[64,2048]{1,0:T(8,128)(2,1)} %param.11), kind=kLoop, calls=%fused_computation | loop fusion | flops 983040 | bytes 655360 | tf_op jit(solution)/shard_map/concatenate | solution.py:324
  2.3 0.0 collective-permute-done.key_sib_ref
  2.3 0.3 collective-permute-done.1.value_sib_ref
  2.6 0.2 collective-permute-start.2
  2.8 2.9 %collective-permute-start.6 = (bf16[64,1536]{1,0:T(8,128)(2,1)S(1)}, bf16[64,1536]{1,0:T(8,128)(2,1)S(1)}, u32[]{:S(2)}, u32[]{:S(2)}) collective-permute-start(bf16[64,1536]{1,0:T(8,128)(2,1)S(1)} %get-tuple-element.44.refs_4_), channel_id=1, source_target_pairs={{0,16},{4,20},{8,24},{12,28},{16,0},{20,4},{24,8},{28,12},{1,17},{... | collective-permute-start | bytes 589832 | tf_op jit(solution)/shard_map/ppermute | solution.py:23
  5.7 1.5 %collective-permute-start.5 = (bf16[64,1536]{1,0:T(8,128)(2,1)S(1)}, bf16[64,1536]{1,0:T(8,128)(2,1)S(1)}, u32[]{:S(2)}, u32[]{:S(2)}) collective-permute-start(bf16[64,1536]{1,0:T(8,128)(2,1)S(1)} %get-tuple-element.45.refs_5_), channel_id=1, source_target_pairs={{0,8},{4,12},{8,0},{12,4},{16,24},{20,28},{24,16},{28,20},{1,9},{5... | collective-permute-start | bytes 589832 | tf_op jit(solution)/shard_map/ppermute | solution.py:23
  7.2 0.5 collective-permute-start.4
  7.7 0.0 collective-permute-start.7
  7.7 3.6 %collective-permute-done.6.refs_8_ = bf16[64,1536]{1,0:T(8,128)(2,1)S(1)} collective-permute-done((bf16[64,1536]{1,0:T(8,128)(2,1)S(1)}, bf16[64,1536]{1,0:T(8,128)(2,1)S(1)}, u32[]{:S(2)}, u32[]{:S(2)}) %collective-permute-start.6) | collective-permute-done | bytes 196640 | tf_op jit(solution)/shard_map/ppermute | solution.py:23
  11.4 2.0 %collective-permute-start.8 = (bf16[64,1536]{1,0:T(8,128)(2,1)S(1)}, bf16[64,1536]{1,0:T(8,128)(2,1)}, u32[]{:S(2)}, u32[]{:S(2)}) collective-permute-start(bf16[64,1536]{1,0:T(8,128)(2,1)S(1)} %collective-permute-done.6.refs_8_), channel_id=1, source_target_pairs={{0,8},{4,12},{8,0},{12,4},{16,24},{20,28},{24,16},{28,20},{1,9},{5... | collective-permute-start | bytes 589832 | tf_op jit(solution)/shard_map/ppermute | solution.py:23
  13.4 0.1 collective-permute-done.5.refs_7_
  13.5 1.5 %collective-permute-start.9 = (bf16[64,1536]{1,0:T(8,128)(2,1)S(1)}, bf16[64,1536]{1,0:T(8,128)(2,1)}, u32[]{:S(2)}, u32[]{:S(2)}) collective-permute-start(bf16[64,1536]{1,0:T(8,128)(2,1)S(1)} %collective-permute-done.5.refs_7_), channel_id=1, source_target_pairs={{0,16},{4,20},{8,24},{12,28},{16,0},{20,4},{24,8},{28,12},{1,17},{... | collective-permute-start | bytes 589832 | tf_op jit(solution)/shard_map/ppermute | solution.py:23
  14.9 0.0 collective-permute-done.2.sib_ref
  14.9 0.0 collective-permute-start.3
  15.6 0.1 pad_add_fusion.place_ref.refs_0_
  15.7 1.7 %copy-done = bf16[2048,640]{1,0:T(8,128)(2,1)S(1)} copy-done((bf16[2048,640]{1,0:T(8,128)(2,1)S(1)}, bf16[2048,640]{1,0:T(8,128)(2,1)}, u32[]{:S(2)}) %copy-start) | copy-done | bytes 2621464
  17.4 1.0 %stage.2 = (bf16[2048,1280]{1,0:T(8,128)(2,1)S(1)}, f32[8,128]{1,0:T(8,128)S(1)}) custom-call(s32[3]{0:T(128)S(1)} %pad_add_fusion.place_ref.refs_0_, bf16[2048,640]{1,0:T(8,128)(2,1)S(1)} %copy-done, bf16[2048,640]{1,0:T(8,128)(2,1)S(1)} %collective-permute-done.2.sib_ref), custom_call_target="tpu_custom_call" | custom-call | tf_op jit(solution)/shard_map/stage/pallas_call | solution.py:197
  18.5 0.0 collective-permute-done.4.refs_6_
  18.5 0.0 collective-permute-done.7.refs_9_
  18.5 2.4 %collective-permute-done.8.refs_10_ = bf16[64,1536]{1,0:T(8,128)(2,1)} collective-permute-done((bf16[64,1536]{1,0:T(8,128)(2,1)S(1)}, bf16[64,1536]{1,0:T(8,128)(2,1)}, u32[]{:S(2)}, u32[]{:S(2)}) %collective-permute-start.8) | collective-permute-done | bytes 196640 | tf_op jit(solution)/shard_map/ppermute | solution.py:23
  20.9 4.0 %attend.2 = (bf16[64,1280]{1,0:T(8,128)(2,1)S(1)}, bf16[64,1280]{1,0:T(8,128)(2,1)S(1)}) custom-call(s32[3]{0:T(128)S(1)} %pad_add_fusion.place_ref.refs_0_, f32[8,128]{1,0:T(8,128)S(1)} %get-tuple-element.42.refs_1_, s32[1,64]{1,0:T(1,128)S(1)} %bitcast.9, bf16[2048,1280]{1,0:T(8,128)(2,1)S(1)} %get-tuple-element.43.refs_3_, ...), custom_call_target="tpu_custom_call" | custom-call | tf_op jit(solution)/shard_map/attend/pallas_call | solution.py:130
  24.9 0.0 copy-start.5
  24.9 0.0 copy-start.1
  25.0 0.1 collective-permute-start.10
  25.0 2.7 %collective-permute-start.12 = (bf16[64,1280]{1,0:T(8,128)(2,1)S(1)}, bf16[64,1280]{1,0:T(8,128)(2,1)S(1)}, u32[]{:S(2)}, u32[]{:S(2)}) collective-permute-start(bf16[64,1280]{1,0:T(8,128)(2,1)S(1)} %get-tuple-element.48.refs_1_), channel_id=1, source_target_pairs={{0,2},{1,3},{2,0},{3,1},{4,6},{5,7},{6,4},{7,5},{8,10},{9,11},{10,... | collective-permute-start | bytes 491528 | tf_op jit(solution)/shard_map/ppermute | solution.py:23
  27.7 4.0 %attend.3 = (f32[64,1280]{1,0:T(8,128)S(1)}, bf16[64,1280]{1,0:T(8,128)(2,1)S(1)}) custom-call(s32[3]{0:T(128)S(1)} %pad_add_fusion.place_ref.refs_0_, bf16[64,1280]{1,0:T(8,128)(2,1)S(1)} %get-tuple-element.48.refs_1_, s32[1,64]{1,0:T(1,128)S(1)} %bitcast.10, bf16[2048,1280]{1,0:T(8,128)(2,1)S(1)} %get-tuple-element.43.refs_3_, ...), custom_call_target="tpu_custom_call" | custom-call | tf_op jit(solution)/shard_map/attend/pallas_call | solution.py:130
  31.7 1.6 %collective-permute-start.11 = (bf16[64,1280]{1,0:T(8,128)(2,1)S(1)}, bf16[64,1280]{1,0:T(8,128)(2,1)S(1)}, u32[]{:S(2)}, u32[]{:S(2)}) collective-permute-start(bf16[64,1280]{1,0:T(8,128)(2,1)S(1)} %get-tuple-element.56), channel_id=1, source_target_pairs={{0,1},{1,0},{2,3},{3,2},{4,5},{5,4},{6,7},{7,6},{8,9},{9,8},{10,11... | collective-permute-start | bytes 491528 | tf_op jit(solution)/shard_map/ppermute | solution.py:23
  33.3 0.2 collective-permute-start.13
  33.6 9.5 %collective-permute-done.11.refs_5_ = bf16[64,1280]{1,0:T(8,128)(2,1)S(1)} collective-permute-done((bf16[64,1280]{1,0:T(8,128)(2,1)S(1)}, bf16[64,1280]{1,0:T(8,128)(2,1)S(1)}, u32[]{:S(2)}, u32[]{:S(2)}) %collective-permute-start.11) | collective-permute-done | bytes 163872 | tf_op jit(solution)/shard_map/ppermute | solution.py:23
  43.1 1.0 %update.1 = (bf16[64,1280]{1,0:T(8,128)(2,1)S(1)}, f32[8,128]{1,0:T(8,128)S(1)}) custom-call(s32[3]{0:T(128)S(1)} %pad_add_fusion.place_ref.refs_0_, f32[64,1280]{1,0:T(8,128)S(1)} %get-tuple-element.54.refs_1_.refs_4_, bf16[128,640]{1,0:T(8,128)(2,1)S(1)} %copy-done.1, bf16[128,640]{1,0:T(8,128)(2,1)} %collective-permute-done.3.refs_3_, ...), custom_call_target="tpu_custom_call" | custom-call | tf_op jit(solution)/shard_map/update/pallas_call | solution.py:163
  44.1 2.7 %collective-permute-start.15 = (bf16[64,1280]{1,0:T(8,128)(2,1)S(1)}, bf16[64,1280]{1,0:T(8,128)(2,1)S(1)}, u32[]{:S(2)}, u32[]{:S(2)}) collective-permute-start(bf16[64,1280]{1,0:T(8,128)(2,1)S(1)} %get-tuple-element.69.refs_6_), channel_id=1, source_target_pairs={{0,2},{1,3},{2,0},{3,1},{4,6},{5,7},{6,4},{7,5},{8,10},{9,11},{10,... | collective-permute-start | bytes 491528 | tf_op jit(solution)/shard_map/ppermute | solution.py:23
  46.8 0.0 collective-permute-start.14
  46.8 1.2 %collective-permute-done.14.refs_1_ = f32[8,128]{1,0:T(8,128)S(1)} collective-permute-done((f32[8,128]{1,0:T(8,128)S(1)}, f32[8,128]{1,0:T(8,128)S(1)}, u32[]{:S(2)}, u32[]{:S(2)}) %collective-permute-start.14) | collective-permute-done | bytes 4128 | tf_op jit(solution)/shard_map/ppermute | solution.py:23
  48.0 0.5 collective-permute-start.24
  48.5 1.2 %collective-permute-start.26 = (bf16[64,1280]{1,0:T(8,128)(2,1)S(1)}, bf16[64,1280]{1,0:T(8,128)(2,1)S(1)}, u32[]{:S(2)}, u32[]{:S(2)}) collective-permute-start(bf16[64,1280]{1,0:T(8,128)(2,1)S(1)} %get-tuple-element.69.refs_6_), channel_id=1, source_target_pairs={{0,1},{1,0},{2,3},{3,2},{4,5},{5,4},{6,7},{7,6},{8,9},{9,8},{10,11... | collective-permute-start | bytes 491528 | tf_op jit(solution)/shard_map/ppermute | solution.py:23
  49.7 1.5 %collective-permute-start.23 = (bf16[64,1280]{1,0:T(8,128)(2,1)S(1)}, bf16[64,1280]{1,0:T(8,128)(2,1)S(1)}, u32[]{:S(2)}, u32[]{:S(2)}) collective-permute-start(bf16[64,1280]{1,0:T(8,128)(2,1)S(1)} %get-tuple-element.69.refs_6_), channel_id=1, source_target_pairs={{0,8},{4,12},{8,0},{12,4},{16,24},{20,28},{24,16},{28,20},{1,9},{5... | collective-permute-start | bytes 491528 | tf_op jit(solution)/shard_map/ppermute | solution.py:23
  51.2 3.9 %stage.3 = (bf16[5120,768]{1,0:T(8,128)(2,1)S(1)}, f32[8,128]{1,0:T(8,128)S(1)}) custom-call(s32[3]{0:T(128)S(1)} %pad_add_fusion.place_ref.refs_0_, bf16[5120,384]{1,0:T(8,128)(2,1)} %own_ref.1, bf16[5120,384]{1,0:T(8,128)(2,1)} %collective-permute-done.10.sib_ref), custom_call_target="tpu_custom_call" | custom-call | tf_op jit(solution)/shard_map/stage/pallas_call | solution.py:197
  55.1 0.0 collective-permute-done.15.refs_6_
  55.1 0.9 %collective-permute-start.19 = (bf16[64,1280]{1,0:T(8,128)(2,1)S(1)}, bf16[64,1280]{1,0:T(8,128)(2,1)S(1)}, u32[]{:S(2)}, u32[]{:S(2)}) collective-permute-start(bf16[64,1280]{1,0:T(8,128)(2,1)S(1)} %collective-permute-done.15.refs_6_), channel_id=1, source_target_pairs={{0,1},{1,0},{2,3},{3,2},{4,5},{5,4},{6,7},{7,6},{8,9},{9,8},{10,11... | collective-permute-start | bytes 491528 | tf_op jit(solution)/shard_map/ppermute | solution.py:23
  56.0 0.0 collective-permute-done.24.refs_8_
  56.0 0.5 collective-permute-start.25
  56.6 1.5 %collective-permute-start.17 = (bf16[64,1280]{1,0:T(8,128)(2,1)S(1)}, bf16[64,1280]{1,0:T(8,128)(2,1)S(1)}, u32[]{:S(2)}, u32[]{:S(2)}) collective-permute-start(bf16[64,1280]{1,0:T(8,128)(2,1)S(1)} %collective-permute-done.15.refs_6_), channel_id=1, source_target_pairs={{0,16},{4,20},{8,24},{12,28},{16,0},{20,4},{24,8},{28,12},{1,17},{... | collective-permute-start | bytes 491528 | tf_op jit(solution)/shard_map/ppermute | solution.py:23
  58.1 1.2 %collective-permute-start.27 = (bf16[64,1280]{1,0:T(8,128)(2,1)S(1)}, bf16[64,1280]{1,0:T(8,128)(2,1)S(1)}, u32[]{:S(2)}, u32[]{:S(2)}) collective-permute-start(bf16[64,1280]{1,0:T(8,128)(2,1)S(1)} %collective-permute-done.23.refs_7_), channel_id=1, source_target_pairs={{0,1},{1,0},{2,3},{3,2},{4,5},{5,4},{6,7},{7,6},{8,9},{9,8},{10,11... | collective-permute-start | bytes 491528 | tf_op jit(solution)/shard_map/ppermute | solution.py:23
  59.2 0.0 collective-permute-done.26.refs_10_
  59.2 0.9 collective-permute-start.28
  60.1 2.2 %collective-permute-done.19.refs_10_ = bf16[64,1280]{1,0:T(8,128)(2,1)S(1)} collective-permute-done((bf16[64,1280]{1,0:T(8,128)(2,1)S(1)}, bf16[64,1280]{1,0:T(8,128)(2,1)S(1)}, u32[]{:S(2)}, u32[]{:S(2)}) %collective-permute-start.19) | collective-permute-done | bytes 163872 | tf_op jit(solution)/shard_map/ppermute | solution.py:23
  62.3 1.2 %collective-permute-start.20 = (bf16[64,1280]{1,0:T(8,128)(2,1)S(1)}, bf16[64,1280]{1,0:T(8,128)(2,1)S(1)}, u32[]{:S(2)}, u32[]{:S(2)}) collective-permute-start(bf16[64,1280]{1,0:T(8,128)(2,1)S(1)} %collective-permute-done.19.refs_10_), channel_id=1, source_target_pairs={{0,8},{4,12},{8,0},{12,4},{16,24},{20,28},{24,16},{28,20},{1,9},{5... | collective-permute-start | bytes 491528 | tf_op jit(solution)/shard_map/ppermute | solution.py:23
  63.5 0.0 collective-permute-done.17.refs_8_
  63.5 1.1 %collective-permute-start.16 = (bf16[64,1280]{1,0:T(8,128)(2,1)S(1)}, bf16[64,1280]{1,0:T(8,128)(2,1)S(1)}, u32[]{:S(2)}, u32[]{:S(2)}) collective-permute-start(bf16[64,1280]{1,0:T(8,128)(2,1)S(1)} %collective-permute-done.15.refs_6_), channel_id=1, source_target_pairs={{0,8},{4,12},{8,0},{12,4},{16,24},{20,28},{24,16},{28,20},{1,9},{5... | collective-permute-start | bytes 491528 | tf_op jit(solution)/shard_map/ppermute | solution.py:23
  64.6 1.2 %collective-permute-done.27.refs_11_ = bf16[64,1280]{1,0:T(8,128)(2,1)S(1)} collective-permute-done((bf16[64,1280]{1,0:T(8,128)(2,1)S(1)}, bf16[64,1280]{1,0:T(8,128)(2,1)S(1)}, u32[]{:S(2)}, u32[]{:S(2)}) %collective-permute-start.27) | collective-permute-done | bytes 163872 | tf_op jit(solution)/shard_map/ppermute | solution.py:23
  65.8 1.5 %collective-permute-start.21 = (bf16[64,1280]{1,0:T(8,128)(2,1)S(1)}, bf16[64,1280]{1,0:T(8,128)(2,1)S(1)}, u32[]{:S(2)}, u32[]{:S(2)}) collective-permute-start(bf16[64,1280]{1,0:T(8,128)(2,1)S(1)} %collective-permute-done.19.refs_10_), channel_id=1, source_target_pairs={{0,16},{4,20},{8,24},{12,28},{16,0},{20,4},{24,8},{28,12},{1,17},{... | collective-permute-start | bytes 491528 | tf_op jit(solution)/shard_map/ppermute | solution.py:23
  67.3 2.0 %collective-permute-done.28.refs_12_ = bf16[64,1280]{1,0:T(8,128)(2,1)S(1)} collective-permute-done((bf16[64,1280]{1,0:T(8,128)(2,1)S(1)}, bf16[64,1280]{1,0:T(8,128)(2,1)S(1)}, u32[]{:S(2)}, u32[]{:S(2)}) %collective-permute-start.28) | collective-permute-done | bytes 163872 | tf_op jit(solution)/shard_map/ppermute | solution.py:23
  69.3 1.2 %collective-permute-start.18 = (bf16[64,1280]{1,0:T(8,128)(2,1)S(1)}, bf16[64,1280]{1,0:T(8,128)(2,1)S(1)}, u32[]{:S(2)}, u32[]{:S(2)}) collective-permute-start(bf16[64,1280]{1,0:T(8,128)(2,1)S(1)} %collective-permute-done.17.refs_8_), channel_id=1, source_target_pairs={{0,8},{4,12},{8,0},{12,4},{16,24},{20,28},{24,16},{28,20},{1,9},{5... | collective-permute-start | bytes 491528 | tf_op jit(solution)/shard_map/ppermute | solution.py:23
  70.5 0.0 collective-permute-done.20.refs_11_
  70.5 0.9 collective-permute-start.22
  71.4 0.2 collective-permute-done.29.refs_13_
  71.6 2.3 %score.2.refs_14_ = f32[32,4,128]{2,1,0:T(4,128)S(1)} custom-call(s32[3]{0:T(128)S(1)} %pad_add_fusion.place_ref.refs_0_, f32[8,128]{1,0:T(8,128)S(1)} %collective-permute-done.14.refs_1_, f32[8,128]{1,0:T(8,128)S(1)} %get-tuple-element.64.refs_2_, s32[1,512]{1,0:T(1,128)S(1)} %bitcast.7, f32[8,640]{1,0:T(8,128)S(1)} %reshape.13.refs_4_, ...), custom_call_target="tpu_custom_call" | custom-call | tf_op jit(solution)/shard_map/score/pallas_call | solution.py:260
  73.8 0.8 collective-permute-done.18.refs_9_
  74.6 1.2 %collective-permute-done.22.refs_13_ = bf16[64,1280]{1,0:T(8,128)(2,1)S(1)} collective-permute-done((bf16[64,1280]{1,0:T(8,128)(2,1)S(1)}, bf16[64,1280]{1,0:T(8,128)(2,1)S(1)}, u32[]{:S(2)}, u32[]{:S(2)}) %collective-permute-start.22) | collective-permute-done | bytes 163872 | tf_op jit(solution)/shard_map/ppermute | solution.py:23
  75.8 2.3 %score.3 = f32[32,4,128]{2,1,0:T(4,128)S(1)} custom-call(s32[3]{0:T(128)S(1)} %pad_add_fusion.place_ref.refs_0_, f32[8,128]{1,0:T(8,128)S(1)} %collective-permute-done.14.refs_1_, f32[8,128]{1,0:T(8,128)S(1)} %get-tuple-element.64.refs_2_, s32[1,512]{1,0:T(1,128)S(1)} %bitcast.8, f32[8,640]{1,0:T(8,128)S(1)} %reshape.13.refs_4_, ...), custom_call_target="tpu_custom_call" | custom-call | tf_op jit(solution)/shard_map/score/pallas_call | solution.py:260
  78.1 10.7 %all_to_all.5.refs_2_ = f32[32,4,128]{2,1,0:T(4,128)S(1)} all-to-all(f32[32,4,128]{2,1,0:T(4,128)S(1)} %score.3), channel_id=1, replica_groups=mesh['ctx'=8,'tp'=4] {'ctx','tp'}, dimensions={0} | all-to-all | bytes 131072 | tf_op jit(solution)/shard_map/all_to_all | solution.py:364
  88.7 1.1 %merge.1 = (f32[1,64]{1,0:T(1,128)}, f32[1,64]{1,0:T(1,128)}) custom-call(s32[3]{0:T(128)S(1)} %pad_add_fusion.place_ref.refs_0_, f32[1,64]{1,0:T(1,128)S(1)} %bitcast.11, f32[32,4,128]{2,1,0:T(4,128)S(1)} %all_to_all.5.refs_2_), custom_call_target="tpu_custom_call" | custom-call | tf_op jit(solution)/shard_map/merge/pallas_call | solution.py:293
  (21 shorter events, 0.1 us)
Async XLA Ops:
  0.6 20.3 %copy-start.3 = (s32[64]{0:T(128)S(1)}, s32[64]{0:T(128)}, u32[]{:S(2)}) copy-start(s32[64]{0:T(128)} %param.20) | copy-start | bytes 772
  0.6 1.6 %collective-permute-start = (bf16[64,256]{1,0:T(8,128)(2,1)}, bf16[64,256]{1,0:T(8,128)(2,1)S(1)}, u32[]{:S(2)}, u32[]{:S(2)}) collective-permute-start(bf16[64,256]{1,0:T(8,128)(2,1)} %param.12), channel_id=1, source_target_pairs={{0,4},{4,0},{8,12},{12,8},{16,20},{20,16},{24,28},{28,24},{1,5},{5... | collective-permute-start | bytes 98312 | tf_op jit(solution)/shard_map/ppermute | solution.py:23
  1.2 1.4 %collective-permute-start.1 = (bf16[64,256]{1,0:T(8,128)(2,1)}, bf16[64,256]{1,0:T(8,128)(2,1)S(1)}, u32[]{:S(2)}, u32[]{:S(2)}) collective-permute-start(bf16[64,256]{1,0:T(8,128)(2,1)} %param.13), channel_id=1, source_target_pairs={{0,4},{4,0},{8,12},{12,8},{16,20},{20,16},{24,28},{28,24},{1,5},{5... | collective-permute-start | bytes 98312 | tf_op jit(solution)/shard_map/ppermute | solution.py:23
  2.6 12.3 %collective-permute-start.2 = (bf16[2048,640]{1,0:T(8,128)(2,1)}, bf16[2048,640]{1,0:T(8,128)(2,1)S(1)}, u32[]{:S(2)}, u32[]{:S(2)}) collective-permute-start(bf16[2048,640]{1,0:T(8,128)(2,1)} %own_ref), channel_id=1, source_target_pairs={{0,4},{4,0},{8,12},{12,8},{16,20},{20,16},{24,28},{28,24},{1,5},{5... | collective-permute-start | bytes 7864328 | tf_op jit(solution)/shard_map/ppermute | solution.py:23
  2.8 8.5 %collective-permute-start.6 = (bf16[64,1536]{1,0:T(8,128)(2,1)S(1)}, bf16[64,1536]{1,0:T(8,128)(2,1)S(1)}, u32[]{:S(2)}, u32[]{:S(2)}) collective-permute-start(bf16[64,1536]{1,0:T(8,128)(2,1)S(1)} %get-tuple-element.44.refs_4_), channel_id=1, source_target_pairs={{0,16},{4,20},{8,24},{12,28},{16,0},{20,4},{24,8},{28,12},{1,17},{... | collective-permute-start | bytes 589832 | tf_op jit(solution)/shard_map/ppermute | solution.py:23
  5.7 7.8 %collective-permute-start.5 = (bf16[64,1536]{1,0:T(8,128)(2,1)S(1)}, bf16[64,1536]{1,0:T(8,128)(2,1)S(1)}, u32[]{:S(2)}, u32[]{:S(2)}) collective-permute-start(bf16[64,1536]{1,0:T(8,128)(2,1)S(1)} %get-tuple-element.45.refs_5_), channel_id=1, source_target_pairs={{0,8},{4,12},{8,0},{12,4},{16,24},{20,28},{24,16},{28,20},{1,9},{5... | collective-permute-start | bytes 589832 | tf_op jit(solution)/shard_map/ppermute | solution.py:23
  7.2 11.3 %collective-permute-start.4 = (bf16[64,1536]{1,0:T(8,128)(2,1)S(1)}, bf16[64,1536]{1,0:T(8,128)(2,1)}, u32[]{:S(2)}, u32[]{:S(2)}) collective-permute-start(bf16[64,1536]{1,0:T(8,128)(2,1)S(1)} %get-tuple-element.44.refs_4_), channel_id=1, source_target_pairs={{0,8},{4,12},{8,0},{12,4},{16,24},{20,28},{24,16},{28,20},{1,9},{5... | collective-permute-start | bytes 589832 | tf_op jit(solution)/shard_map/ppermute | solution.py:23
  7.7 10.7 %collective-permute-start.7 = (bf16[64,1536]{1,0:T(8,128)(2,1)S(1)}, bf16[64,1536]{1,0:T(8,128)(2,1)}, u32[]{:S(2)}, u32[]{:S(2)}) collective-permute-start(bf16[64,1536]{1,0:T(8,128)(2,1)S(1)} %get-tuple-element.45.refs_5_), channel_id=1, source_target_pairs={{0,16},{4,20},{8,24},{12,28},{16,0},{20,4},{24,8},{28,12},{1,17},{... | collective-permute-start | bytes 589832 | tf_op jit(solution)/shard_map/ppermute | solution.py:23
  11.4 9.5 %collective-permute-start.8 = (bf16[64,1536]{1,0:T(8,128)(2,1)S(1)}, bf16[64,1536]{1,0:T(8,128)(2,1)}, u32[]{:S(2)}, u32[]{:S(2)}) collective-permute-start(bf16[64,1536]{1,0:T(8,128)(2,1)S(1)} %collective-permute-done.6.refs_8_), channel_id=1, source_target_pairs={{0,8},{4,12},{8,0},{12,4},{16,24},{20,28},{24,16},{28,20},{1,9},{5... | collective-permute-start | bytes 589832 | tf_op jit(solution)/shard_map/ppermute | solution.py:23
  13.5 7.4 %collective-permute-start.9 = (bf16[64,1536]{1,0:T(8,128)(2,1)S(1)}, bf16[64,1536]{1,0:T(8,128)(2,1)}, u32[]{:S(2)}, u32[]{:S(2)}) collective-permute-start(bf16[64,1536]{1,0:T(8,128)(2,1)S(1)} %collective-permute-done.5.refs_7_), channel_id=1, source_target_pairs={{0,16},{4,20},{8,24},{12,28},{16,0},{20,4},{24,8},{28,12},{1,17},{... | collective-permute-start | bytes 589832 | tf_op jit(solution)/shard_map/ppermute | solution.py:23
  14.9 3.5 %collective-permute-start.3 = (bf16[128,640]{1,0:T(8,128)(2,1)}, bf16[128,640]{1,0:T(8,128)(2,1)}, u32[]{:S(2)}, u32[]{:S(2)}) collective-permute-start(bf16[128,640]{1,0:T(8,128)(2,1)} %refs_2_), channel_id=1, source_target_pairs={{0,4},{4,0},{8,12},{12,8},{16,20},{20,16},{24,28},{28,24},{1,5},{5... | collective-permute-start | bytes 491528 | tf_op jit(solution)/shard_map/ppermute | solution.py:23
  15.7 1.7 %copy-start = (bf16[2048,640]{1,0:T(8,128)(2,1)S(1)}, bf16[2048,640]{1,0:T(8,128)(2,1)}, u32[]{:S(2)}) copy-start(bf16[2048,640]{1,0:T(8,128)(2,1)} %own_ref) | copy-start | bytes 7864324
  24.9 8.6 %copy-start.5 = (bf16[5120]{0:T(1024)(128)(2,1)S(1)}, bf16[5120]{0:T(1024)(128)(2,1)}, u32[]{:S(2)}) copy-start(bf16[5120]{0:T(1024)(128)(2,1)} %param.16) | copy-start | bytes 30724
  24.9 18.1 %copy-start.1 = (bf16[128,640]{1,0:T(8,128)(2,1)S(1)}, bf16[128,640]{1,0:T(8,128)(2,1)}, u32[]{:S(2)}) copy-start(bf16[128,640]{1,0:T(8,128)(2,1)} %refs_2_) | copy-start | bytes 491524
  25.0 8.6 %collective-permute-start.10 = (bf16[5120,384]{1,0:T(8,128)(2,1)}, bf16[5120,384]{1,0:T(8,128)(2,1)}, u32[]{:S(2)}, u32[]{:S(2)}) collective-permute-start(bf16[5120,384]{1,0:T(8,128)(2,1)} %own_ref.1), channel_id=1, source_target_pairs={{0,4},{4,0},{8,12},{12,8},{16,20},{20,16},{24,28},{28,24},{1,5},{5... | collective-permute-start | bytes 11796488 | tf_op jit(solution)/shard_map/ppermute | solution.py:23
  25.0 18.0 %collective-permute-start.12 = (bf16[64,1280]{1,0:T(8,128)(2,1)S(1)}, bf16[64,1280]{1,0:T(8,128)(2,1)S(1)}, u32[]{:S(2)}, u32[]{:S(2)}) collective-permute-start(bf16[64,1280]{1,0:T(8,128)(2,1)S(1)} %get-tuple-element.48.refs_1_), channel_id=1, source_target_pairs={{0,2},{1,3},{2,0},{3,1},{4,6},{5,7},{6,4},{7,5},{8,10},{9,11},{10,... | collective-permute-start | bytes 491528 | tf_op jit(solution)/shard_map/ppermute | solution.py:23
  31.7 11.4 %collective-permute-start.11 = (bf16[64,1280]{1,0:T(8,128)(2,1)S(1)}, bf16[64,1280]{1,0:T(8,128)(2,1)S(1)}, u32[]{:S(2)}, u32[]{:S(2)}) collective-permute-start(bf16[64,1280]{1,0:T(8,128)(2,1)S(1)} %get-tuple-element.56), channel_id=1, source_target_pairs={{0,1},{1,0},{2,3},{3,2},{4,5},{5,4},{6,7},{7,6},{8,9},{9,8},{10,11... | collective-permute-start | bytes 491528 | tf_op jit(solution)/shard_map/ppermute | solution.py:23
  33.3 9.7 %collective-permute-start.13 = (bf16[64,1280]{1,0:T(8,128)(2,1)S(1)}, bf16[64,1280]{1,0:T(8,128)(2,1)S(1)}, u32[]{:S(2)}, u32[]{:S(2)}) collective-permute-start(bf16[64,1280]{1,0:T(8,128)(2,1)S(1)} %get-tuple-element.57), channel_id=1, source_target_pairs={{0,3},{1,2},{2,1},{3,0},{4,7},{5,6},{6,5},{7,4},{8,11},{9,10},{10,... | collective-permute-start | bytes 491528 | tf_op jit(solution)/shard_map/ppermute | solution.py:23
  44.1 10.9 %collective-permute-start.15 = (bf16[64,1280]{1,0:T(8,128)(2,1)S(1)}, bf16[64,1280]{1,0:T(8,128)(2,1)S(1)}, u32[]{:S(2)}, u32[]{:S(2)}) collective-permute-start(bf16[64,1280]{1,0:T(8,128)(2,1)S(1)} %get-tuple-element.69.refs_6_), channel_id=1, source_target_pairs={{0,2},{1,3},{2,0},{3,1},{4,6},{5,7},{6,4},{7,5},{8,10},{9,11},{10,... | collective-permute-start | bytes 491528 | tf_op jit(solution)/shard_map/ppermute | solution.py:23
  46.8 24.7 %copy-start.2 = (s32[512]{0:T(512)S(1)}, s32[512]{0:T(512)}, u32[]{:S(2)}) copy-start(s32[512]{0:T(512)} %param.18) | copy-start | bytes 6148
  46.8 1.2 %collective-permute-start.14 = (f32[8,128]{1,0:T(8,128)S(1)}, f32[8,128]{1,0:T(8,128)S(1)}, u32[]{:S(2)}, u32[]{:S(2)}) collective-permute-start(f32[8,128]{1,0:T(8,128)S(1)} %get-tuple-element.59), channel_id=1, source_target_pairs={{0,4},{4,0},{8,12},{12,8},{16,20},{20,16},{24,28},{28,24},{1,5},{5... | collective-permute-start | bytes 12296 | tf_op jit(solution)/shard_map/ppermute | solution.py:23
  48.0 8.0 %collective-permute-start.24 = (bf16[64,1280]{1,0:T(8,128)(2,1)S(1)}, bf16[64,1280]{1,0:T(8,128)(2,1)S(1)}, u32[]{:S(2)}, u32[]{:S(2)}) collective-permute-start(bf16[64,1280]{1,0:T(8,128)(2,1)S(1)} %get-tuple-element.69.refs_6_), channel_id=1, source_target_pairs={{0,16},{4,20},{8,24},{12,28},{16,0},{20,4},{24,8},{28,12},{1,17},{... | collective-permute-start | bytes 491528 | tf_op jit(solution)/shard_map/ppermute | solution.py:23
  48.5 10.7 %collective-permute-start.26 = (bf16[64,1280]{1,0:T(8,128)(2,1)S(1)}, bf16[64,1280]{1,0:T(8,128)(2,1)S(1)}, u32[]{:S(2)}, u32[]{:S(2)}) collective-permute-start(bf16[64,1280]{1,0:T(8,128)(2,1)S(1)} %get-tuple-element.69.refs_6_), channel_id=1, source_target_pairs={{0,1},{1,0},{2,3},{3,2},{4,5},{5,4},{6,7},{7,6},{8,9},{9,8},{10,11... | collective-permute-start | bytes 491528 | tf_op jit(solution)/shard_map/ppermute | solution.py:23
  49.7 8.4 %collective-permute-start.23 = (bf16[64,1280]{1,0:T(8,128)(2,1)S(1)}, bf16[64,1280]{1,0:T(8,128)(2,1)S(1)}, u32[]{:S(2)}, u32[]{:S(2)}) collective-permute-start(bf16[64,1280]{1,0:T(8,128)(2,1)S(1)} %get-tuple-element.69.refs_6_), channel_id=1, source_target_pairs={{0,8},{4,12},{8,0},{12,4},{16,24},{20,28},{24,16},{28,20},{1,9},{5... | collective-permute-start | bytes 491528 | tf_op jit(solution)/shard_map/ppermute | solution.py:23
  55.1 7.2 %collective-permute-start.19 = (bf16[64,1280]{1,0:T(8,128)(2,1)S(1)}, bf16[64,1280]{1,0:T(8,128)(2,1)S(1)}, u32[]{:S(2)}, u32[]{:S(2)}) collective-permute-start(bf16[64,1280]{1,0:T(8,128)(2,1)S(1)} %collective-permute-done.15.refs_6_), channel_id=1, source_target_pairs={{0,1},{1,0},{2,3},{3,2},{4,5},{5,4},{6,7},{7,6},{8,9},{9,8},{10,11... | collective-permute-start | bytes 491528 | tf_op jit(solution)/shard_map/ppermute | solution.py:23
  56.0 7.5 %collective-permute-start.25 = (bf16[64,1280]{1,0:T(8,128)(2,1)S(1)}, bf16[64,1280]{1,0:T(8,128)(2,1)S(1)}, u32[]{:S(2)}, u32[]{:S(2)}) collective-permute-start(bf16[64,1280]{1,0:T(8,128)(2,1)S(1)} %collective-permute-done.24.refs_8_), channel_id=1, source_target_pairs={{0,8},{4,12},{8,0},{12,4},{16,24},{20,28},{24,16},{28,20},{1,9},{5... | collective-permute-start | bytes 491528 | tf_op jit(solution)/shard_map/ppermute | solution.py:23
  56.6 6.9 %collective-permute-start.17 = (bf16[64,1280]{1,0:T(8,128)(2,1)S(1)}, bf16[64,1280]{1,0:T(8,128)(2,1)S(1)}, u32[]{:S(2)}, u32[]{:S(2)}) collective-permute-start(bf16[64,1280]{1,0:T(8,128)(2,1)S(1)} %collective-permute-done.15.refs_6_), channel_id=1, source_target_pairs={{0,16},{4,20},{8,24},{12,28},{16,0},{20,4},{24,8},{28,12},{1,17},{... | collective-permute-start | bytes 491528 | tf_op jit(solution)/shard_map/ppermute | solution.py:23
  58.1 7.7 %collective-permute-start.27 = (bf16[64,1280]{1,0:T(8,128)(2,1)S(1)}, bf16[64,1280]{1,0:T(8,128)(2,1)S(1)}, u32[]{:S(2)}, u32[]{:S(2)}) collective-permute-start(bf16[64,1280]{1,0:T(8,128)(2,1)S(1)} %collective-permute-done.23.refs_7_), channel_id=1, source_target_pairs={{0,1},{1,0},{2,3},{3,2},{4,5},{5,4},{6,7},{7,6},{8,9},{9,8},{10,11... | collective-permute-start | bytes 491528 | tf_op jit(solution)/shard_map/ppermute | solution.py:23
  59.2 10.1 %collective-permute-start.28 = (bf16[64,1280]{1,0:T(8,128)(2,1)S(1)}, bf16[64,1280]{1,0:T(8,128)(2,1)S(1)}, u32[]{:S(2)}, u32[]{:S(2)}) collective-permute-start(bf16[64,1280]{1,0:T(8,128)(2,1)S(1)} %collective-permute-done.24.refs_8_), channel_id=1, source_target_pairs={{0,1},{1,0},{2,3},{3,2},{4,5},{5,4},{6,7},{7,6},{8,9},{9,8},{10,11... | collective-permute-start | bytes 491528 | tf_op jit(solution)/shard_map/ppermute | solution.py:23
  62.3 8.2 %collective-permute-start.20 = (bf16[64,1280]{1,0:T(8,128)(2,1)S(1)}, bf16[64,1280]{1,0:T(8,128)(2,1)S(1)}, u32[]{:S(2)}, u32[]{:S(2)}) collective-permute-start(bf16[64,1280]{1,0:T(8,128)(2,1)S(1)} %collective-permute-done.19.refs_10_), channel_id=1, source_target_pairs={{0,8},{4,12},{8,0},{12,4},{16,24},{20,28},{24,16},{28,20},{1,9},{5... | collective-permute-start | bytes 491528 | tf_op jit(solution)/shard_map/ppermute | solution.py:23
  63.5 8.1 %collective-permute-start.29 = (bf16[64,1280]{1,0:T(8,128)(2,1)S(1)}, bf16[64,1280]{1,0:T(8,128)(2,1)S(1)}, u32[]{:S(2)}, u32[]{:S(2)}) collective-permute-start(bf16[64,1280]{1,0:T(8,128)(2,1)S(1)} %collective-permute-done.25.refs_9_), channel_id=1, source_target_pairs={{0,1},{1,0},{2,3},{3,2},{4,5},{5,4},{6,7},{7,6},{8,9},{9,8},{10,11... | collective-permute-start | bytes 491528 | tf_op jit(solution)/shard_map/ppermute | solution.py:23
  63.5 10.3 %collective-permute-start.16 = (bf16[64,1280]{1,0:T(8,128)(2,1)S(1)}, bf16[64,1280]{1,0:T(8,128)(2,1)S(1)}, u32[]{:S(2)}, u32[]{:S(2)}) collective-permute-start(bf16[64,1280]{1,0:T(8,128)(2,1)S(1)} %collective-permute-done.15.refs_6_), channel_id=1, source_target_pairs={{0,8},{4,12},{8,0},{12,4},{16,24},{20,28},{24,16},{28,20},{1,9},{5... | collective-permute-start | bytes 491528 | tf_op jit(solution)/shard_map/ppermute | solution.py:23
  65.8 8.8 %collective-permute-start.21 = (bf16[64,1280]{1,0:T(8,128)(2,1)S(1)}, bf16[64,1280]{1,0:T(8,128)(2,1)S(1)}, u32[]{:S(2)}, u32[]{:S(2)}) collective-permute-start(bf16[64,1280]{1,0:T(8,128)(2,1)S(1)} %collective-permute-done.19.refs_10_), channel_id=1, source_target_pairs={{0,16},{4,20},{8,24},{12,28},{16,0},{20,4},{24,8},{28,12},{1,17},{... | collective-permute-start | bytes 491528 | tf_op jit(solution)/shard_map/ppermute | solution.py:23
  69.3 5.3 %collective-permute-start.18 = (bf16[64,1280]{1,0:T(8,128)(2,1)S(1)}, bf16[64,1280]{1,0:T(8,128)(2,1)S(1)}, u32[]{:S(2)}, u32[]{:S(2)}) collective-permute-start(bf16[64,1280]{1,0:T(8,128)(2,1)S(1)} %collective-permute-done.17.refs_8_), channel_id=1, source_target_pairs={{0,8},{4,12},{8,0},{12,4},{16,24},{20,28},{24,16},{28,20},{1,9},{5... | collective-permute-start | bytes 491528 | tf_op jit(solution)/shard_map/ppermute | solution.py:23
  70.5 5.3 %collective-permute-start.22 = (bf16[64,1280]{1,0:T(8,128)(2,1)S(1)}, bf16[64,1280]{1,0:T(8,128)(2,1)S(1)}, u32[]{:S(2)}, u32[]{:S(2)}) collective-permute-start(bf16[64,1280]{1,0:T(8,128)(2,1)S(1)} %collective-permute-done.20.refs_11_), channel_id=1, source_target_pairs={{0,16},{4,20},{8,24},{12,28},{16,0},{20,4},{24,8},{28,12},{1,17},{... | collective-permute-start | bytes 491528 | tf_op jit(solution)/shard_map/ppermute | solution.py:23
  73.8 14.9 %copy-start.4 = (f32[64]{0:T(128)S(1)}, f32[64]{0:T(128)}, u32[]{:S(2)}) copy-start(f32[64]{0:T(128)} %param.19) | copy-start | bytes 772

commit v7 on v6

--- a/solution.py
+++ b/solution.py
@@ -339,7 +339,7 @@
     gain, tokens, sums[0] = lax.optimization_barrier((final_gain, token_ids, sums[0]))
     gain, tokens = gain.astype(F32).reshape(ctx_count, -1), tokens[None]
     sums[0], gain, tokens, head_sibling = lax.optimization_barrier((sums[0], gain, tokens, head_sibling))
-    updated, mark = update(place, sums[0], stream, stream_sibling, [sums[0]] + received, blocks, own_rows)
+    updated, mark = update(place, gain, stream, stream_sibling, [sums[0]] + received, blocks, own_rows)
     here, mark, head_sibling = lax.optimization_barrier((updated, swap(mark, "ctx", 1), head_sibling))
     head, ready = stage(place, head_weight, head_sibling, ctx_count)
     pieces, spans = [updated], []

time: 90.1 us -> 90 us (level)
  starting transfers between devices: 30.6 us -> 28.6 us
  waiting for transfers between devices: 24.7 us -> 26.7 us
    ppermute x30, waiting for transfers between devices: 24.7 us -> 26.7 us  [swap(): return lax.ppermute(x, axis, [(i, i ^ k) for i in range(size)])]
    ppermute x30, starting transfers between devices: 30.6 us -> 28.6 us  [swap(): return lax.ppermute(x, axis, [(i, i ^ k) for i in range(size)])]
where the time goes in v7:
time: 90 us; the launch traced here: 89.8 us
  starting transfers between devices  28.6 us (32%)
  waiting for transfers between devices  26.7 us (30%)
  Pallas kernels  19.6 us (22%)
  blocking collectives  10.5 us (12%)
  local copies, waits for them, and re-layouts  1.79 us (2%)
  between operations  1.44 us (2%)
  other arithmetic  1.09 us (1%)
    ppermute x30, starting transfers between devices, swap(): return lax.ppermute(x, axis, [(i, i ^ k) for i in range(size)])  28.6 us
    ppermute x30, waiting for transfers between devices, swap(): return lax.ppermute(x, axis, [(i, i ^ k) for i in range(size)])  26.7 us
    all_to_all x1, blocking collectives, local(): stats = lax.all_to_all(stats, ('ctx', 'tp'), 0, 0, tiled=True)  10.5 us
    pallas_call x2, Pallas kernels, attend(): pl.pallas_call(lambda *refs: attend_kernel(chips, tp_count, own_rows, kv_...  8.01 us
    pallas_call x2, Pallas kernels, stage(): pl.pallas_call(stage_kernel, out_shape=[jax.ShapeDtypeStruct((depth, 2 *...  4.92 us
    pallas_call x2, Pallas kernels, score(): pl.pallas_call(lambda *refs: score_kernel(chips, tp_count, own_rows, bloc...  4.51 us
  transfers between devices with their start and end apart: 30, of which 12 were waited for; matrix products, arithmetic and copies ran while one was open for 1% of the time, Pallas kernels for 12%

profile of v7, /device:TPU:0, one launch (start us, length us, event | category | flops | bytes accessed | tf_op | source)
XLA Modules:
  0.0 89.8 jit_solution(13318316118817438232)
XLA Ops:
  0.6 0.5 collective-permute-start
  1.2 0.1 collective-permute-start.1
  1.2 1.0 %pad_maximum_fusion.all_ref = bf16[64,2560]{1,0:T(8,128)(2,1)S(1)} fusion(bf16[64,256]{1,0:T(8,128)(2,1)} %param.13, bf16[64,256]{1,0:T(8,128)(2,1)} %param.12, bf16[64,2048]{1,0:T(8,128)(2,1)} %param.11), kind=kLoop, calls=%fused_computation | loop fusion | flops 983040 | bytes 655360 | tf_op jit(solution)/shard_map/concatenate | solution.py:324
  2.3 0.0 collective-permute-done.key_sib_ref
  2.3 0.3 collective-permute-done.1.value_sib_ref
  2.6 0.2 collective-permute-start.2
  2.8 2.9 %collective-permute-start.6 = (bf16[64,1536]{1,0:T(8,128)(2,1)S(1)}, bf16[64,1536]{1,0:T(8,128)(2,1)S(1)}, u32[]{:S(2)}, u32[]{:S(2)}) collective-permute-start(bf16[64,1536]{1,0:T(8,128)(2,1)S(1)} %get-tuple-element.44.refs_4_), channel_id=1, source_target_pairs={{0,16},{4,20},{8,24},{12,28},{16,0},{20,4},{24,8},{28,12},{1,17},{... | collective-permute-start | bytes 589832 | tf_op jit(solution)/shard_map/ppermute | solution.py:23
  5.7 1.5 %collective-permute-start.5 = (bf16[64,1536]{1,0:T(8,128)(2,1)S(1)}, bf16[64,1536]{1,0:T(8,128)(2,1)S(1)}, u32[]{:S(2)}, u32[]{:S(2)}) collective-permute-start(bf16[64,1536]{1,0:T(8,128)(2,1)S(1)} %get-tuple-element.45.refs_5_), channel_id=1, source_target_pairs={{0,8},{4,12},{8,0},{12,4},{16,24},{20,28},{24,16},{28,20},{1,9},{5... | collective-permute-start | bytes 589832 | tf_op jit(solution)/shard_map/ppermute | solution.py:23
  7.2 0.5 collective-permute-start.4
  7.7 0.0 collective-permute-start.7
  7.7 3.6 %collective-permute-done.6.refs_8_ = bf16[64,1536]{1,0:T(8,128)(2,1)S(1)} collective-permute-done((bf16[64,1536]{1,0:T(8,128)(2,1)S(1)}, bf16[64,1536]{1,0:T(8,128)(2,1)S(1)}, u32[]{:S(2)}, u32[]{:S(2)}) %collective-permute-start.6) | collective-permute-done | bytes 196640 | tf_op jit(solution)/shard_map/ppermute | solution.py:23
  11.4 2.0 %collective-permute-start.8 = (bf16[64,1536]{1,0:T(8,128)(2,1)S(1)}, bf16[64,1536]{1,0:T(8,128)(2,1)}, u32[]{:S(2)}, u32[]{:S(2)}) collective-permute-start(bf16[64,1536]{1,0:T(8,128)(2,1)S(1)} %collective-permute-done.6.refs_8_), channel_id=1, source_target_pairs={{0,8},{4,12},{8,0},{12,4},{16,24},{20,28},{24,16},{28,20},{1,9},{5... | collective-permute-start | bytes 589832 | tf_op jit(solution)/shard_map/ppermute | solution.py:23
  13.4 0.1 collective-permute-done.5.refs_7_
  13.5 1.5 %collective-permute-start.9 = (bf16[64,1536]{1,0:T(8,128)(2,1)S(1)}, bf16[64,1536]{1,0:T(8,128)(2,1)}, u32[]{:S(2)}, u32[]{:S(2)}) collective-permute-start(bf16[64,1536]{1,0:T(8,128)(2,1)S(1)} %collective-permute-done.5.refs_7_), channel_id=1, source_target_pairs={{0,16},{4,20},{8,24},{12,28},{16,0},{20,4},{24,8},{28,12},{1,17},{... | collective-permute-start | bytes 589832 | tf_op jit(solution)/shard_map/ppermute | solution.py:23
  14.9 0.0 collective-permute-done.2.sib_ref
  14.9 0.0 collective-permute-start.3
  15.6 0.1 pad_add_fusion.place_ref.refs_0_
  15.7 1.7 %copy-done = bf16[2048,640]{1,0:T(8,128)(2,1)S(1)} copy-done((bf16[2048,640]{1,0:T(8,128)(2,1)S(1)}, bf16[2048,640]{1,0:T(8,128)(2,1)}, u32[]{:S(2)}) %copy-start) | copy-done | bytes 2621464
  17.4 1.0 %stage.2 = (bf16[2048,1280]{1,0:T(8,128)(2,1)S(1)}, f32[8,128]{1,0:T(8,128)S(1)}) custom-call(s32[3]{0:T(128)S(1)} %pad_add_fusion.place_ref.refs_0_, bf16[2048,640]{1,0:T(8,128)(2,1)S(1)} %copy-done, bf16[2048,640]{1,0:T(8,128)(2,1)S(1)} %collective-permute-done.2.sib_ref), custom_call_target="tpu_custom_call" | custom-call | tf_op jit(solution)/shard_map/stage/pallas_call | solution.py:197
  18.5 0.0 collective-permute-done.4.refs_6_
  18.5 0.0 collective-permute-done.7.refs_9_
  18.5 2.4 %collective-permute-done.8.refs_10_ = bf16[64,1536]{1,0:T(8,128)(2,1)} collective-permute-done((bf16[64,1536]{1,0:T(8,128)(2,1)S(1)}, bf16[64,1536]{1,0:T(8,128)(2,1)}, u32[]{:S(2)}, u32[]{:S(2)}) %collective-permute-start.8) | collective-permute-done | bytes 196640 | tf_op jit(solution)/shard_map/ppermute | solution.py:23
  20.9 4.0 %attend.2 = (bf16[64,1280]{1,0:T(8,128)(2,1)S(1)}, bf16[64,1280]{1,0:T(8,128)(2,1)S(1)}) custom-call(s32[3]{0:T(128)S(1)} %pad_add_fusion.place_ref.refs_0_, f32[8,128]{1,0:T(8,128)S(1)} %get-tuple-element.42.refs_1_, s32[1,64]{1,0:T(1,128)S(1)} %bitcast.9, bf16[2048,1280]{1,0:T(8,128)(2,1)S(1)} %get-tuple-element.43.refs_3_, ...), custom_call_target="tpu_custom_call" | custom-call | tf_op jit(solution)/shard_map/attend/pallas_call | solution.py:130
  24.9 0.0 copy-start.5
  24.9 0.0 copy-start.1
  25.0 0.1 collective-permute-start.10
  25.0 2.7 %collective-permute-start.12 = (bf16[64,1280]{1,0:T(8,128)(2,1)S(1)}, bf16[64,1280]{1,0:T(8,128)(2,1)S(1)}, u32[]{:S(2)}, u32[]{:S(2)}) collective-permute-start(bf16[64,1280]{1,0:T(8,128)(2,1)S(1)} %get-tuple-element.48.refs_1_), channel_id=1, source_target_pairs={{0,2},{1,3},{2,0},{3,1},{4,6},{5,7},{6,4},{7,5},{8,10},{9,11},{10,... | collective-permute-start | bytes 491528 | tf_op jit(solution)/shard_map/ppermute | solution.py:23
  27.7 4.0 %attend.3 = (f32[64,1280]{1,0:T(8,128)S(1)}, bf16[64,1280]{1,0:T(8,128)(2,1)S(1)}) custom-call(s32[3]{0:T(128)S(1)} %pad_add_fusion.place_ref.refs_0_, bf16[64,1280]{1,0:T(8,128)(2,1)S(1)} %get-tuple-element.48.refs_1_, s32[1,64]{1,0:T(1,128)S(1)} %bitcast.10, bf16[2048,1280]{1,0:T(8,128)(2,1)S(1)} %get-tuple-element.43.refs_3_, ...), custom_call_target="tpu_custom_call" | custom-call | tf_op jit(solution)/shard_map/attend/pallas_call | solution.py:130
  31.7 1.6 %collective-permute-start.11 = (bf16[64,1280]{1,0:T(8,128)(2,1)S(1)}, bf16[64,1280]{1,0:T(8,128)(2,1)S(1)}, u32[]{:S(2)}, u32[]{:S(2)}) collective-permute-start(bf16[64,1280]{1,0:T(8,128)(2,1)S(1)} %get-tuple-element.57), channel_id=1, source_target_pairs={{0,1},{1,0},{2,3},{3,2},{4,5},{5,4},{6,7},{7,6},{8,9},{9,8},{10,11... | collective-permute-start | bytes 491528 | tf_op jit(solution)/shard_map/ppermute | solution.py:23
  33.3 0.2 collective-permute-start.13
  33.6 9.5 %collective-permute-done.11.refs_5_ = bf16[64,1280]{1,0:T(8,128)(2,1)S(1)} collective-permute-done((bf16[64,1280]{1,0:T(8,128)(2,1)S(1)}, bf16[64,1280]{1,0:T(8,128)(2,1)S(1)}, u32[]{:S(2)}, u32[]{:S(2)}) %collective-permute-start.11) | collective-permute-done | bytes 163872 | tf_op jit(solution)/shard_map/ppermute | solution.py:23
  43.1 1.0 %update.1 = (bf16[64,1280]{1,0:T(8,128)(2,1)S(1)}, f32[8,128]{1,0:T(8,128)S(1)}) custom-call(s32[3]{0:T(128)S(1)} %pad_add_fusion.place_ref.refs_0_, f32[8,640]{1,0:T(8,128)S(1)} %reshape.13.refs_1_.refs_4_, bf16[128,640]{1,0:T(8,128)(2,1)S(1)} %copy-done.1, bf16[128,640]{1,0:T(8,128)(2,1)} %collective-permute-done.3.refs_3_, ...), custom_call_target="tpu_custom_call" | custom-call | tf_op jit(solution)/shard_map/update/pallas_call | solution.py:163
  44.1 2.7 %collective-permute-start.15 = (bf16[64,1280]{1,0:T(8,128)(2,1)S(1)}, bf16[64,1280]{1,0:T(8,128)(2,1)S(1)}, u32[]{:S(2)}, u32[]{:S(2)}) collective-permute-start(bf16[64,1280]{1,0:T(8,128)(2,1)S(1)} %get-tuple-element.69.refs_6_), channel_id=1, source_target_pairs={{0,2},{1,3},{2,0},{3,1},{4,6},{5,7},{6,4},{7,5},{8,10},{9,11},{10,... | collective-permute-start | bytes 491528 | tf_op jit(solution)/shard_map/ppermute | solution.py:23
  46.8 1.2 %collective-permute-start.26 = (bf16[64,1280]{1,0:T(8,128)(2,1)S(1)}, bf16[64,1280]{1,0:T(8,128)(2,1)S(1)}, u32[]{:S(2)}, u32[]{:S(2)}) collective-permute-start(bf16[64,1280]{1,0:T(8,128)(2,1)S(1)} %get-tuple-element.69.refs_6_), channel_id=1, source_target_pairs={{0,1},{1,0},{2,3},{3,2},{4,5},{5,4},{6,7},{7,6},{8,9},{9,8},{10,11... | collective-permute-start | bytes 491528 | tf_op jit(solution)/shard_map/ppermute | solution.py:23
  48.0 0.0 collective-permute-done.14.refs_1_
  48.0 0.5 collective-permute-start.24
  48.5 1.5 %collective-permute-start.23 = (bf16[64,1280]{1,0:T(8,128)(2,1)S(1)}, bf16[64,1280]{1,0:T(8,128)(2,1)S(1)}, u32[]{:S(2)}, u32[]{:S(2)}) collective-permute-start(bf16[64,1280]{1,0:T(8,128)(2,1)S(1)} %get-tuple-element.69.refs_6_), channel_id=1, source_target_pairs={{0,8},{4,12},{8,0},{12,4},{16,24},{20,28},{24,16},{28,20},{1,9},{5... | collective-permute-start | bytes 491528 | tf_op jit(solution)/shard_map/ppermute | solution.py:23
  50.0 3.9 %stage.3 = (bf16[5120,768]{1,0:T(8,128)(2,1)S(1)}, f32[8,128]{1,0:T(8,128)S(1)}) custom-call(s32[3]{0:T(128)S(1)} %pad_add_fusion.place_ref.refs_0_, bf16[5120,384]{1,0:T(8,128)(2,1)} %own_ref.1, bf16[5120,384]{1,0:T(8,128)(2,1)} %collective-permute-done.10.sib_ref), custom_call_target="tpu_custom_call" | custom-call | tf_op jit(solution)/shard_map/stage/pallas_call | solution.py:197
  53.9 1.0 %collective-permute-done.15.refs_6_ = bf16[64,1280]{1,0:T(8,128)(2,1)S(1)} collective-permute-done((bf16[64,1280]{1,0:T(8,128)(2,1)S(1)}, bf16[64,1280]{1,0:T(8,128)(2,1)S(1)}, u32[]{:S(2)}, u32[]{:S(2)}) %collective-permute-start.15) | collective-permute-done | bytes 163872 | tf_op jit(solution)/shard_map/ppermute | solution.py:23
  54.9 0.3 collective-permute-start.19
  55.1 0.0 collective-permute-done.24.refs_8_
  55.2 1.2 %collective-permute-start.25 = (bf16[64,1280]{1,0:T(8,128)(2,1)S(1)}, bf16[64,1280]{1,0:T(8,128)(2,1)S(1)}, u32[]{:S(2)}, u32[]{:S(2)}) collective-permute-start(bf16[64,1280]{1,0:T(8,128)(2,1)S(1)} %collective-permute-done.24.refs_8_), channel_id=1, source_target_pairs={{0,8},{4,12},{8,0},{12,4},{16,24},{20,28},{24,16},{28,20},{1,9},{5... | collective-permute-start | bytes 491528 | tf_op jit(solution)/shard_map/ppermute | solution.py:23
  56.4 0.8 collective-permute-start.17
  57.2 1.7 %collective-permute-start.27 = (bf16[64,1280]{1,0:T(8,128)(2,1)S(1)}, bf16[64,1280]{1,0:T(8,128)(2,1)S(1)}, u32[]{:S(2)}, u32[]{:S(2)}) collective-permute-start(bf16[64,1280]{1,0:T(8,128)(2,1)S(1)} %collective-permute-done.23.refs_7_), channel_id=1, source_target_pairs={{0,1},{1,0},{2,3},{3,2},{4,5},{5,4},{6,7},{7,6},{8,9},{9,8},{10,11... | collective-permute-start | bytes 491528 | tf_op jit(solution)/shard_map/ppermute | solution.py:23
  58.9 0.0 collective-permute-done.26.refs_10_
  58.9 0.3 collective-permute-start.28
  59.2 2.7 %collective-permute-done.19.refs_10_ = bf16[64,1280]{1,0:T(8,128)(2,1)S(1)} collective-permute-done((bf16[64,1280]{1,0:T(8,128)(2,1)S(1)}, bf16[64,1280]{1,0:T(8,128)(2,1)S(1)}, u32[]{:S(2)}, u32[]{:S(2)}) %collective-permute-start.19) | collective-permute-done | bytes 163872 | tf_op jit(solution)/shard_map/ppermute | solution.py:23
  62.0 1.5 %collective-permute-start.20 = (bf16[64,1280]{1,0:T(8,128)(2,1)S(1)}, bf16[64,1280]{1,0:T(8,128)(2,1)S(1)}, u32[]{:S(2)}, u32[]{:S(2)}) collective-permute-start(bf16[64,1280]{1,0:T(8,128)(2,1)S(1)} %collective-permute-done.19.refs_10_), channel_id=1, source_target_pairs={{0,8},{4,12},{8,0},{12,4},{16,24},{20,28},{24,16},{28,20},{1,9},{5... | collective-permute-start | bytes 491528 | tf_op jit(solution)/shard_map/ppermute | solution.py:23
  63.5 0.0 collective-permute-done.25.refs_9_
  63.5 0.0 collective-permute-start.29
  63.5 0.0 collective-permute-done.17.refs_8_
  63.5 0.6 collective-permute-start.16
  64.1 1.4 %collective-permute-done.27.refs_11_ = bf16[64,1280]{1,0:T(8,128)(2,1)S(1)} collective-permute-done((bf16[64,1280]{1,0:T(8,128)(2,1)S(1)}, bf16[64,1280]{1,0:T(8,128)(2,1)S(1)}, u32[]{:S(2)}, u32[]{:S(2)}) %collective-permute-start.27) | collective-permute-done | bytes 163872 | tf_op jit(solution)/shard_map/ppermute | solution.py:23
  65.5 0.5 collective-permute-start.21
  66.0 3.0 %collective-permute-done.28.refs_12_ = bf16[64,1280]{1,0:T(8,128)(2,1)S(1)} collective-permute-done((bf16[64,1280]{1,0:T(8,128)(2,1)S(1)}, bf16[64,1280]{1,0:T(8,128)(2,1)S(1)}, u32[]{:S(2)}, u32[]{:S(2)}) %collective-permute-start.28) | collective-permute-done | bytes 163872 | tf_op jit(solution)/shard_map/ppermute | solution.py:23
  69.0 1.5 %collective-permute-start.18 = (bf16[64,1280]{1,0:T(8,128)(2,1)S(1)}, bf16[64,1280]{1,0:T(8,128)(2,1)S(1)}, u32[]{:S(2)}, u32[]{:S(2)}) collective-permute-start(bf16[64,1280]{1,0:T(8,128)(2,1)S(1)} %collective-permute-done.17.refs_8_), channel_id=1, source_target_pairs={{0,8},{4,12},{8,0},{12,4},{16,24},{20,28},{24,16},{28,20},{1,9},{5... | collective-permute-start | bytes 491528 | tf_op jit(solution)/shard_map/ppermute | solution.py:23
  70.5 0.5 collective-permute-start.22
  71.0 0.2 collective-permute-done.29.refs_13_
  71.2 2.3 %score.2.refs_14_ = f32[32,4,128]{2,1,0:T(4,128)S(1)} custom-call(s32[3]{0:T(128)S(1)} %pad_add_fusion.place_ref.refs_0_, f32[8,128]{1,0:T(8,128)S(1)} %collective-permute-done.14.refs_1_, f32[8,128]{1,0:T(8,128)S(1)} %get-tuple-element.65.refs_2_, s32[1,512]{1,0:T(1,128)S(1)} %bitcast.7, f32[8,640]{1,0:T(8,128)S(1)} %reshape.13.refs_1_.refs_4_, ...), custom_call_target="tpu_custom_call" | custom-call | tf_op jit(solution)/shard_map/score/pallas_call | solution.py:260
  73.4 0.9 collective-permute-done.18.refs_9_
  74.3 1.5 %collective-permute-done.22.refs_13_ = bf16[64,1280]{1,0:T(8,128)(2,1)S(1)} collective-permute-done((bf16[64,1280]{1,0:T(8,128)(2,1)S(1)}, bf16[64,1280]{1,0:T(8,128)(2,1)S(1)}, u32[]{:S(2)}, u32[]{:S(2)}) %collective-permute-start.22) | collective-permute-done | bytes 163872 | tf_op jit(solution)/shard_map/ppermute | solution.py:23
  75.8 2.3 %score.3 = f32[32,4,128]{2,1,0:T(4,128)S(1)} custom-call(s32[3]{0:T(128)S(1)} %pad_add_fusion.place_ref.refs_0_, f32[8,128]{1,0:T(8,128)S(1)} %collective-permute-done.14.refs_1_, f32[8,128]{1,0:T(8,128)S(1)} %get-tuple-element.65.refs_2_, s32[1,512]{1,0:T(1,128)S(1)} %bitcast.8, f32[8,640]{1,0:T(8,128)S(1)} %reshape.13.refs_1_.refs_4_, ...), custom_call_target="tpu_custom_call" | custom-call | tf_op jit(solution)/shard_map/score/pallas_call | solution.py:260
  78.1 10.5 %all_to_all.5.refs_2_ = f32[32,4,128]{2,1,0:T(4,128)S(1)} all-to-all(f32[32,4,128]{2,1,0:T(4,128)S(1)} %score.3), channel_id=1, replica_groups=mesh['ctx'=8,'tp'=4] {'ctx','tp'}, dimensions={0} | all-to-all | bytes 131072 | tf_op jit(solution)/shard_map/all_to_all | solution.py:364
  88.6 1.1 %merge.1 = (f32[1,64]{1,0:T(1,128)}, f32[1,64]{1,0:T(1,128)}) custom-call(s32[3]{0:T(128)S(1)} %pad_add_fusion.place_ref.refs_0_, f32[1,64]{1,0:T(1,128)S(1)} %bitcast.11, f32[32,4,128]{2,1,0:T(4,128)S(1)} %all_to_all.5.refs_2_), custom_call_target="tpu_custom_call" | custom-call | tf_op jit(solution)/shard_map/merge/pallas_call | solution.py:293
  (21 shorter events, 0.1 us)
Async XLA Ops:
  0.6 20.3 %copy-start.3 = (s32[64]{0:T(128)S(1)}, s32[64]{0:T(128)}, u32[]{:S(2)}) copy-start(s32[64]{0:T(128)} %param.20) | copy-start | bytes 772
  0.6 1.6 %collective-permute-start = (bf16[64,256]{1,0:T(8,128)(2,1)}, bf16[64,256]{1,0:T(8,128)(2,1)S(1)}, u32[]{:S(2)}, u32[]{:S(2)}) collective-permute-start(bf16[64,256]{1,0:T(8,128)(2,1)} %param.12), channel_id=1, source_target_pairs={{0,4},{4,0},{8,12},{12,8},{16,20},{20,16},{24,28},{28,24},{1,5},{5... | collective-permute-start | bytes 98312 | tf_op jit(solution)/shard_map/ppermute | solution.py:23
  1.2 1.4 %collective-permute-start.1 = (bf16[64,256]{1,0:T(8,128)(2,1)}, bf16[64,256]{1,0:T(8,128)(2,1)S(1)}, u32[]{:S(2)}, u32[]{:S(2)}) collective-permute-start(bf16[64,256]{1,0:T(8,128)(2,1)} %param.13), channel_id=1, source_target_pairs={{0,4},{4,0},{8,12},{12,8},{16,20},{20,16},{24,28},{28,24},{1,5},{5... | collective-permute-start | bytes 98312 | tf_op jit(solution)/shard_map/ppermute | solution.py:23
  2.6 12.3 %collective-permute-start.2 = (bf16[2048,640]{1,0:T(8,128)(2,1)}, bf16[2048,640]{1,0:T(8,128)(2,1)S(1)}, u32[]{:S(2)}, u32[]{:S(2)}) collective-permute-start(bf16[2048,640]{1,0:T(8,128)(2,1)} %own_ref), channel_id=1, source_target_pairs={{0,4},{4,0},{8,12},{12,8},{16,20},{20,16},{24,28},{28,24},{1,5},{5... | collective-permute-start | bytes 7864328 | tf_op jit(solution)/shard_map/ppermute | solution.py:23
  2.8 8.5 %collective-permute-start.6 = (bf16[64,1536]{1,0:T(8,128)(2,1)S(1)}, bf16[64,1536]{1,0:T(8,128)(2,1)S(1)}, u32[]{:S(2)}, u32[]{:S(2)}) collective-permute-start(bf16[64,1536]{1,0:T(8,128)(2,1)S(1)} %get-tuple-element.44.refs_4_), channel_id=1, source_target_pairs={{0,16},{4,20},{8,24},{12,28},{16,0},{20,4},{24,8},{28,12},{1,17},{... | collective-permute-start | bytes 589832 | tf_op jit(solution)/shard_map/ppermute | solution.py:23
  5.7 7.8 %collective-permute-start.5 = (bf16[64,1536]{1,0:T(8,128)(2,1)S(1)}, bf16[64,1536]{1,0:T(8,128)(2,1)S(1)}, u32[]{:S(2)}, u32[]{:S(2)}) collective-permute-start(bf16[64,1536]{1,0:T(8,128)(2,1)S(1)} %get-tuple-element.45.refs_5_), channel_id=1, source_target_pairs={{0,8},{4,12},{8,0},{12,4},{16,24},{20,28},{24,16},{28,20},{1,9},{5... | collective-permute-start | bytes 589832 | tf_op jit(solution)/shard_map/ppermute | solution.py:23
  7.2 11.3 %collective-permute-start.4 = (bf16[64,1536]{1,0:T(8,128)(2,1)S(1)}, bf16[64,1536]{1,0:T(8,128)(2,1)}, u32[]{:S(2)}, u32[]{:S(2)}) collective-permute-start(bf16[64,1536]{1,0:T(8,128)(2,1)S(1)} %get-tuple-element.44.refs_4_), channel_id=1, source_target_pairs={{0,8},{4,12},{8,0},{12,4},{16,24},{20,28},{24,16},{28,20},{1,9},{5... | collective-permute-start | bytes 589832 | tf_op jit(solution)/shard_map/ppermute | solution.py:23
  7.7 10.7 %collective-permute-start.7 = (bf16[64,1536]{1,0:T(8,128)(2,1)S(1)}, bf16[64,1536]{1,0:T(8,128)(2,1)}, u32[]{:S(2)}, u32[]{:S(2)}) collective-permute-start(bf16[64,1536]{1,0:T(8,128)(2,1)S(1)} %get-tuple-element.45.refs_5_), channel_id=1, source_target_pairs={{0,16},{4,20},{8,24},{12,28},{16,0},{20,4},{24,8},{28,12},{1,17},{... | collective-permute-start | bytes 589832 | tf_op jit(solution)/shard_map/ppermute | solution.py:23
  11.4 9.5 %collective-permute-start.8 = (bf16[64,1536]{1,0:T(8,128)(2,1)S(1)}, bf16[64,1536]{1,0:T(8,128)(2,1)}, u32[]{:S(2)}, u32[]{:S(2)}) collective-permute-start(bf16[64,1536]{1,0:T(8,128)(2,1)S(1)} %collective-permute-done.6.refs_8_), channel_id=1, source_target_pairs={{0,8},{4,12},{8,0},{12,4},{16,24},{20,28},{24,16},{28,20},{1,9},{5... | collective-permute-start | bytes 589832 | tf_op jit(solution)/shard_map/ppermute | solution.py:23
  13.5 7.4 %collective-permute-start.9 = (bf16[64,1536]{1,0:T(8,128)(2,1)S(1)}, bf16[64,1536]{1,0:T(8,128)(2,1)}, u32[]{:S(2)}, u32[]{:S(2)}) collective-permute-start(bf16[64,1536]{1,0:T(8,128)(2,1)S(1)} %collective-permute-done.5.refs_7_), channel_id=1, source_target_pairs={{0,16},{4,20},{8,24},{12,28},{16,0},{20,4},{24,8},{28,12},{1,17},{... | collective-permute-start | bytes 589832 | tf_op jit(solution)/shard_map/ppermute | solution.py:23
  14.9 3.5 %collective-permute-start.3 = (bf16[128,640]{1,0:T(8,128)(2,1)}, bf16[128,640]{1,0:T(8,128)(2,1)}, u32[]{:S(2)}, u32[]{:S(2)}) collective-permute-start(bf16[128,640]{1,0:T(8,128)(2,1)} %refs_2_), channel_id=1, source_target_pairs={{0,4},{4,0},{8,12},{12,8},{16,20},{20,16},{24,28},{28,24},{1,5},{5... | collective-permute-start | bytes 491528 | tf_op jit(solution)/shard_map/ppermute | solution.py:23
  15.7 1.7 %copy-start = (bf16[2048,640]{1,0:T(8,128)(2,1)S(1)}, bf16[2048,640]{1,0:T(8,128)(2,1)}, u32[]{:S(2)}) copy-start(bf16[2048,640]{1,0:T(8,128)(2,1)} %own_ref) | copy-start | bytes 7864324
  24.9 8.6 %copy-start.5 = (bf16[5120]{0:T(1024)(128)(2,1)S(1)}, bf16[5120]{0:T(1024)(128)(2,1)}, u32[]{:S(2)}) copy-start(bf16[5120]{0:T(1024)(128)(2,1)} %param.16) | copy-start | bytes 30724
  24.9 18.1 %copy-start.1 = (bf16[128,640]{1,0:T(8,128)(2,1)S(1)}, bf16[128,640]{1,0:T(8,128)(2,1)}, u32[]{:S(2)}) copy-start(bf16[128,640]{1,0:T(8,128)(2,1)} %refs_2_) | copy-start | bytes 491524
  25.0 8.6 %collective-permute-start.10 = (bf16[5120,384]{1,0:T(8,128)(2,1)}, bf16[5120,384]{1,0:T(8,128)(2,1)}, u32[]{:S(2)}, u32[]{:S(2)}) collective-permute-start(bf16[5120,384]{1,0:T(8,128)(2,1)} %own_ref.1), channel_id=1, source_target_pairs={{0,4},{4,0},{8,12},{12,8},{16,20},{20,16},{24,28},{28,24},{1,5},{5... | collective-permute-start | bytes 11796488 | tf_op jit(solution)/shard_map/ppermute | solution.py:23
  25.0 18.0 %collective-permute-start.12 = (bf16[64,1280]{1,0:T(8,128)(2,1)S(1)}, bf16[64,1280]{1,0:T(8,128)(2,1)S(1)}, u32[]{:S(2)}, u32[]{:S(2)}) collective-permute-start(bf16[64,1280]{1,0:T(8,128)(2,1)S(1)} %get-tuple-element.48.refs_1_), channel_id=1, source_target_pairs={{0,2},{1,3},{2,0},{3,1},{4,6},{5,7},{6,4},{7,5},{8,10},{9,11},{10,... | collective-permute-start | bytes 491528 | tf_op jit(solution)/shard_map/ppermute | solution.py:23
  31.7 11.4 %collective-permute-start.11 = (bf16[64,1280]{1,0:T(8,128)(2,1)S(1)}, bf16[64,1280]{1,0:T(8,128)(2,1)S(1)}, u32[]{:S(2)}, u32[]{:S(2)}) collective-permute-start(bf16[64,1280]{1,0:T(8,128)(2,1)S(1)} %get-tuple-element.57), channel_id=1, source_target_pairs={{0,1},{1,0},{2,3},{3,2},{4,5},{5,4},{6,7},{7,6},{8,9},{9,8},{10,11... | collective-permute-start | bytes 491528 | tf_op jit(solution)/shard_map/ppermute | solution.py:23
  33.3 9.7 %collective-permute-start.13 = (bf16[64,1280]{1,0:T(8,128)(2,1)S(1)}, bf16[64,1280]{1,0:T(8,128)(2,1)S(1)}, u32[]{:S(2)}, u32[]{:S(2)}) collective-permute-start(bf16[64,1280]{1,0:T(8,128)(2,1)S(1)} %get-tuple-element.58), channel_id=1, source_target_pairs={{0,3},{1,2},{2,1},{3,0},{4,7},{5,6},{6,5},{7,4},{8,11},{9,10},{10,... | collective-permute-start | bytes 491528 | tf_op jit(solution)/shard_map/ppermute | solution.py:23
  44.1 10.7 %collective-permute-start.15 = (bf16[64,1280]{1,0:T(8,128)(2,1)S(1)}, bf16[64,1280]{1,0:T(8,128)(2,1)S(1)}, u32[]{:S(2)}, u32[]{:S(2)}) collective-permute-start(bf16[64,1280]{1,0:T(8,128)(2,1)S(1)} %get-tuple-element.69.refs_6_), channel_id=1, source_target_pairs={{0,2},{1,3},{2,0},{3,1},{4,6},{5,7},{6,4},{7,5},{8,10},{9,11},{10,... | collective-permute-start | bytes 491528 | tf_op jit(solution)/shard_map/ppermute | solution.py:23
  46.8 24.3 %copy-start.2 = (s32[512]{0:T(512)S(1)}, s32[512]{0:T(512)}, u32[]{:S(2)}) copy-start(s32[512]{0:T(512)} %param.18) | copy-start | bytes 6148
  46.8 1.2 %collective-permute-start.14 = (f32[8,128]{1,0:T(8,128)S(1)}, f32[8,128]{1,0:T(8,128)S(1)}, u32[]{:S(2)}, u32[]{:S(2)}) collective-permute-start(f32[8,128]{1,0:T(8,128)S(1)} %get-tuple-element.60), channel_id=1, source_target_pairs={{0,4},{4,0},{8,12},{12,8},{16,20},{20,16},{24,28},{28,24},{1,5},{5... | collective-permute-start | bytes 12296 | tf_op jit(solution)/shard_map/ppermute | solution.py:23
  46.8 12.1 %collective-permute-start.26 = (bf16[64,1280]{1,0:T(8,128)(2,1)S(1)}, bf16[64,1280]{1,0:T(8,128)(2,1)S(1)}, u32[]{:S(2)}, u32[]{:S(2)}) collective-permute-start(bf16[64,1280]{1,0:T(8,128)(2,1)S(1)} %get-tuple-element.69.refs_6_), channel_id=1, source_target_pairs={{0,1},{1,0},{2,3},{3,2},{4,5},{5,4},{6,7},{7,6},{8,9},{9,8},{10,11... | collective-permute-start | bytes 491528 | tf_op jit(solution)/shard_map/ppermute | solution.py:23
  48.0 7.2 %collective-permute-start.24 = (bf16[64,1280]{1,0:T(8,128)(2,1)S(1)}, bf16[64,1280]{1,0:T(8,128)(2,1)S(1)}, u32[]{:S(2)}, u32[]{:S(2)}) collective-permute-start(bf16[64,1280]{1,0:T(8,128)(2,1)S(1)} %get-tuple-element.69.refs_6_), channel_id=1, source_target_pairs={{0,16},{4,20},{8,24},{12,28},{16,0},{20,4},{24,8},{28,12},{1,17},{... | collective-permute-start | bytes 491528 | tf_op jit(solution)/shard_map/ppermute | solution.py:23
  48.5 8.7 %collective-permute-start.23 = (bf16[64,1280]{1,0:T(8,128)(2,1)S(1)}, bf16[64,1280]{1,0:T(8,128)(2,1)S(1)}, u32[]{:S(2)}, u32[]{:S(2)}) collective-permute-start(bf16[64,1280]{1,0:T(8,128)(2,1)S(1)} %get-tuple-element.69.refs_6_), channel_id=1, source_target_pairs={{0,8},{4,12},{8,0},{12,4},{16,24},{20,28},{24,16},{28,20},{1,9},{5... | collective-permute-start | bytes 491528 | tf_op jit(solution)/shard_map/ppermute | solution.py:23
  54.9 7.1 %collective-permute-start.19 = (bf16[64,1280]{1,0:T(8,128)(2,1)S(1)}, bf16[64,1280]{1,0:T(8,128)(2,1)S(1)}, u32[]{:S(2)}, u32[]{:S(2)}) collective-permute-start(bf16[64,1280]{1,0:T(8,128)(2,1)S(1)} %collective-permute-done.15.refs_6_), channel_id=1, source_target_pairs={{0,1},{1,0},{2,3},{3,2},{4,5},{5,4},{6,7},{7,6},{8,9},{9,8},{10,11... | collective-permute-start | bytes 491528 | tf_op jit(solution)/shard_map/ppermute | solution.py:23
  55.2 8.3 %collective-permute-start.25 = (bf16[64,1280]{1,0:T(8,128)(2,1)S(1)}, bf16[64,1280]{1,0:T(8,128)(2,1)S(1)}, u32[]{:S(2)}, u32[]{:S(2)}) collective-permute-start(bf16[64,1280]{1,0:T(8,128)(2,1)S(1)} %collective-permute-done.24.refs_8_), channel_id=1, source_target_pairs={{0,8},{4,12},{8,0},{12,4},{16,24},{20,28},{24,16},{28,20},{1,9},{5... | collective-permute-start | bytes 491528 | tf_op jit(solution)/shard_map/ppermute | solution.py:23
  56.4 7.1 %collective-permute-start.17 = (bf16[64,1280]{1,0:T(8,128)(2,1)S(1)}, bf16[64,1280]{1,0:T(8,128)(2,1)S(1)}, u32[]{:S(2)}, u32[]{:S(2)}) collective-permute-start(bf16[64,1280]{1,0:T(8,128)(2,1)S(1)} %collective-permute-done.15.refs_6_), channel_id=1, source_target_pairs={{0,16},{4,20},{8,24},{12,28},{16,0},{20,4},{24,8},{28,12},{1,17},{... | collective-permute-start | bytes 491528 | tf_op jit(solution)/shard_map/ppermute | solution.py:23
  57.2 8.3 %collective-permute-start.27 = (bf16[64,1280]{1,0:T(8,128)(2,1)S(1)}, bf16[64,1280]{1,0:T(8,128)(2,1)S(1)}, u32[]{:S(2)}, u32[]{:S(2)}) collective-permute-start(bf16[64,1280]{1,0:T(8,128)(2,1)S(1)} %collective-permute-done.23.refs_7_), channel_id=1, source_target_pairs={{0,1},{1,0},{2,3},{3,2},{4,5},{5,4},{6,7},{7,6},{8,9},{9,8},{10,11... | collective-permute-start | bytes 491528 | tf_op jit(solution)/shard_map/ppermute | solution.py:23
  58.9 10.1 %collective-permute-start.28 = (bf16[64,1280]{1,0:T(8,128)(2,1)S(1)}, bf16[64,1280]{1,0:T(8,128)(2,1)S(1)}, u32[]{:S(2)}, u32[]{:S(2)}) collective-permute-start(bf16[64,1280]{1,0:T(8,128)(2,1)S(1)} %collective-permute-done.24.refs_8_), channel_id=1, source_target_pairs={{0,1},{1,0},{2,3},{3,2},{4,5},{5,4},{6,7},{7,6},{8,9},{9,8},{10,11... | collective-permute-start | bytes 491528 | tf_op jit(solution)/shard_map/ppermute | solution.py:23
  62.0 8.5 %collective-permute-start.20 = (bf16[64,1280]{1,0:T(8,128)(2,1)S(1)}, bf16[64,1280]{1,0:T(8,128)(2,1)S(1)}, u32[]{:S(2)}, u32[]{:S(2)}) collective-permute-start(bf16[64,1280]{1,0:T(8,128)(2,1)S(1)} %collective-permute-done.19.refs_10_), channel_id=1, source_target_pairs={{0,8},{4,12},{8,0},{12,4},{16,24},{20,28},{24,16},{28,20},{1,9},{5... | collective-permute-start | bytes 491528 | tf_op jit(solution)/shard_map/ppermute | solution.py:23
  63.5 7.7 %collective-permute-start.29 = (bf16[64,1280]{1,0:T(8,128)(2,1)S(1)}, bf16[64,1280]{1,0:T(8,128)(2,1)S(1)}, u32[]{:S(2)}, u32[]{:S(2)}) collective-permute-start(bf16[64,1280]{1,0:T(8,128)(2,1)S(1)} %collective-permute-done.25.refs_9_), channel_id=1, source_target_pairs={{0,1},{1,0},{2,3},{3,2},{4,5},{5,4},{6,7},{7,6},{8,9},{9,8},{10,11... | collective-permute-start | bytes 491528 | tf_op jit(solution)/shard_map/ppermute | solution.py:23
  63.5 9.9 %collective-permute-start.16 = (bf16[64,1280]{1,0:T(8,128)(2,1)S(1)}, bf16[64,1280]{1,0:T(8,128)(2,1)S(1)}, u32[]{:S(2)}, u32[]{:S(2)}) collective-permute-start(bf16[64,1280]{1,0:T(8,128)(2,1)S(1)} %collective-permute-done.15.refs_6_), channel_id=1, source_target_pairs={{0,8},{4,12},{8,0},{12,4},{16,24},{20,28},{24,16},{28,20},{1,9},{5... | collective-permute-start | bytes 491528 | tf_op jit(solution)/shard_map/ppermute | solution.py:23
  65.5 8.8 %collective-permute-start.21 = (bf16[64,1280]{1,0:T(8,128)(2,1)S(1)}, bf16[64,1280]{1,0:T(8,128)(2,1)S(1)}, u32[]{:S(2)}, u32[]{:S(2)}) collective-permute-start(bf16[64,1280]{1,0:T(8,128)(2,1)S(1)} %collective-permute-done.19.refs_10_), channel_id=1, source_target_pairs={{0,16},{4,20},{8,24},{12,28},{16,0},{20,4},{24,8},{28,12},{1,17},{... | collective-permute-start | bytes 491528 | tf_op jit(solution)/shard_map/ppermute | solution.py:23
  69.0 5.3 %collective-permute-start.18 = (bf16[64,1280]{1,0:T(8,128)(2,1)S(1)}, bf16[64,1280]{1,0:T(8,128)(2,1)S(1)}, u32[]{:S(2)}, u32[]{:S(2)}) collective-permute-start(bf16[64,1280]{1,0:T(8,128)(2,1)S(1)} %collective-permute-done.17.refs_8_), channel_id=1, source_target_pairs={{0,8},{4,12},{8,0},{12,4},{16,24},{20,28},{24,16},{28,20},{1,9},{5... | collective-permute-start | bytes 491528 | tf_op jit(solution)/shard_map/ppermute | solution.py:23
  70.5 5.3 %collective-permute-start.22 = (bf16[64,1280]{1,0:T(8,128)(2,1)S(1)}, bf16[64,1280]{1,0:T(8,128)(2,1)S(1)}, u32[]{:S(2)}, u32[]{:S(2)}) collective-permute-start(bf16[64,1280]{1,0:T(8,128)(2,1)S(1)} %collective-permute-done.20.refs_11_), channel_id=1, source_target_pairs={{0,16},{4,20},{8,24},{12,28},{16,0},{20,4},{24,8},{28,12},{1,17},{... | collective-permute-start | bytes 491528 | tf_op jit(solution)/shard_map/ppermute | solution.py:23
  73.4 15.2 %copy-start.4 = (f32[64]{0:T(128)S(1)}, f32[64]{0:T(128)}, u32[]{:S(2)}) copy-start(f32[64]{0:T(128)} %param.19) | copy-start | bytes 772
